TPU v7x, 32 devices: a whole 2x2x4 slice. The times are simulated.
32 devices in a mesh: fibre: 8 (over y, x, core), tm: 4 (over z).
Axes of the slice: x: 2, y: 2, z: 4, core: 2. Of those that a mesh axis runs over, the one named last changes fastest.
Arguments:
- traces: float32 [1024, 32, 512], P('fibre', 'tm'), may hold values from -6 to 6
Outputs:
- correlations: float32 [1024, 32, 256], P(('fibre', 'tm'))
All inputs are finite; a program needn't handle non-finite values.
Results may differ from a plain program's by a relative error of at most 0.0003.
Values sent between devices are 32-bit elements; how exact they have to be, the bound alone decides.
No kernel may reach another device: no remote copies, remote signals or barrier semaphores. Data moves between devices by JAX's collectives and lax.ppermute only.
A program may use at most 128 MiB of HBM per device.

v0:
```python
import math

import jax
import jax.numpy as jnp
from jax import lax
from jax.sharding import PartitionSpec as P

NEAR = 32
LAGS = 256
HALF = 8


def shifted(value, axis, steps):
    count = lax.axis_size(axis)
    leading, last = (max(0, -steps), min(count, count - steps))
    return lax.ppermute(value, axis, [(source, source + steps) for source in range(leading, last)])


def make_tables(win, bins, lags, segs):
    sample_idx = jnp.arange(win, dtype=jnp.int32)[:, None]
    bin_idx = jnp.arange(1, bins + 1, dtype=jnp.int32)[None, :]
    phases = (sample_idx * bin_idx % win).astype(jnp.float32) * (2.0 * math.pi / win)
    hann_taper = 0.5 - 0.5 * jnp.cos(sample_idx.astype(jnp.float32) * (2.0 * math.pi / win))
    forward = jnp.concatenate([hann_taper * jnp.cos(phases), -hann_taper * jnp.sin(phases)], axis=1)
    rows_idx = jnp.arange(bins, dtype=jnp.int32)
    band_matrix = (jnp.abs(rows_idx[:, None] - rows_idx[None, :]) <= HALF).astype(jnp.float32) / (
        2 * HALF + 1
    )
    lag_shift = jnp.arange(lags, dtype=jnp.int32)[None, :] - lags // 2
    back_phase = (bin_idx.reshape(bins, 1) * lag_shift % win).astype(jnp.float32) * (
        2.0 * math.pi / win
    )
    inverse = jnp.concatenate([jnp.cos(back_phase), -jnp.sin(back_phase)], axis=0) / segs
    return (forward, band_matrix, inverse)


def whiten(samples, forward, band_matrix):
    channels, segments, win = samples.shape
    bins = forward.shape[1] // 2
    seg_rows = samples.reshape(channels * segments, win)
    spectrum = jnp.dot(seg_rows, forward, precision=lax.Precision.HIGHEST)
    real_part = spectrum[:, :bins]
    imag_part = spectrum[:, bins:]
    energy = real_part * real_part + imag_part * imag_part
    smoothed = jnp.dot(energy, band_matrix, precision=lax.Precision.HIGHEST)
    overall = jnp.mean(energy, axis=1, keepdims=True)
    divisor = jnp.sqrt(smoothed + 0.1 * overall + 1e-06)
    whitened = jnp.concatenate([real_part / divisor, imag_part / divisor], axis=1)
    return whitened.reshape(channels, segments, 2 * bins)


def band_of(products):
    count = products.shape[0]
    width = products.shape[2]
    flat_rows = products.reshape(count * 2 * count, width)[1:]
    flat_rows = jnp.pad(flat_rows, ((0, count + 1), (0, 0)))
    return flat_rows.reshape(count, 2 * count + 1, width)[:, :count]


def shards(traces):
    channels, segments, win = traces.shape
    bins = win // 2
    segs = segments * lax.axis_size("tm")
    forward, band_matrix, inverse = make_tables(win, bins, LAGS, segs)
    spectra = whiten(traces, forward, band_matrix)
    ahead_part = shifted(spectra[:NEAR], "fibre", -1)
    extended = jnp.concatenate([spectra, ahead_part], axis=0)
    pieces = []
    for block_id in range(channels // NEAR):
        first = extended[block_id * NEAR : (block_id + 1) * NEAR]
        second = extended[block_id * NEAR : (block_id + 2) * NEAR]
        first_re = first[..., :bins]
        first_im = first[..., bins:]
        second_re = second[..., :bins]
        second_im = second[..., bins:]
        both_re = jnp.einsum("ask,bsk->abk", first_re, second_re, precision=lax.Precision.HIGHEST)
        both_im = jnp.einsum("ask,bsk->abk", first_im, second_im, precision=lax.Precision.HIGHEST)
        im_re = jnp.einsum("ask,bsk->abk", first_im, second_re, precision=lax.Precision.HIGHEST)
        re_im = jnp.einsum("ask,bsk->abk", first_re, second_im, precision=lax.Precision.HIGHEST)
        pieces.append(jnp.concatenate([band_of(both_re + both_im), band_of(im_re - re_im)], axis=2))
    pairs = jnp.concatenate(pieces, axis=0)
    share = channels // lax.axis_size("tm")
    stacked = lax.psum_scatter(pairs, "tm", scatter_dimension=0, tiled=True)
    correlations = jnp.dot(
        stacked.reshape(share * NEAR, 2 * bins), inverse, precision=lax.Precision.HIGHEST
    ).reshape(share, NEAR, LAGS)
    return correlations


def solution(mesh):
    in_specs = (P("fibre", "tm", None),)
    out_specs = P(("fibre", "tm"), None, None)
    return jax.shard_map(shards, mesh=mesh, in_specs=in_specs, out_specs=out_specs, check_vma=False)
```

profile of v0, /device:TPU:0, one launch (start us, length us, event | category | flops | bytes accessed | tf_op | source)
XLA Modules:
  0.0 445.3 jit_solution(13411951215203812136)
XLA Ops:
  8.7 6.9 %fusion.2 = f32[1024,512]{0,1:T(8,128)S(1)} fusion(f32[128,8,512]{2,1,0:T(8,128)S(1)} %copy-done, f32[512,256]{1,0:T(8,128)S(1)} %get-tuple-element.33, f32[512,256]{1,0:T(8,128)S(1)} %get-tuple-element.32), kind=kOutput, calls=%fused_computation.26 | convolution fusion | flops 3221487616 | bytes 5242880 | tf_op jit(solution)/shard_map/dot_general | solution.py:41
  32.0 8.0 %fusion.57 = f32[256,64,32]{1,2,0:T(8,128)S(1)} fusion(f32[64,8,256]{0,1,2:T(8,128)} %copy.98, f32[32,8,256]{0,1,2:T(8,128)S(1)} %copy.101), kind=kOutput, calls=%fused_computation.101 | convolution fusion | flops 50331648 | bytes 2883584 | tf_op jit(solution)/shard_map/ask,bsk->abk/dot_general | solution.py:78
  40.0 7.1 %fusion.56 = f32[256,64,32]{1,2,0:T(8,128)S(1)} fusion(f32[64,8,256]{0,1,2:T(8,128)S(1)} %copy-done.9, f32[32,8,256]{0,1,2:T(8,128)S(1)} %copy.99), kind=kOutput, calls=%fused_computation.100 | convolution fusion | flops 50331648 | bytes 2883584 | tf_op jit(solution)/shard_map/ask,bsk->abk/dot_general | solution.py:76
  47.2 8.4 %subtract_bitcast_fusion.1 = f32[32,64,256]{1,0,2:T(8,128)} fusion(f32[256,64,32]{1,2,0:T(8,128)S(1)} %fusion.57, f32[64,8,256]{0,1,2:T(8,128)S(1)} %copy.100, f32[32,8,256]{0,1,2:T(8,128)S(1)} %copy.99), kind=kOutput, calls=%fused_computation.18 | convolution fusion | flops 50855936 | bytes 4980736 | tf_op jit(solution)/shard_map/ask,bsk->abk/dot_general | solution.py:79
  55.6 8.4 %add_bitcast_fusion.1 = f32[32,64,256]{1,0,2:T(8,128)} fusion(f32[256,64,32]{1,2,0:T(8,128)S(1)} %fusion.56, f32[64,8,256]{0,1,2:T(8,128)S(1)} %copy.100, f32[32,8,256]{0,1,2:T(8,128)S(1)} %copy.101), kind=kOutput, calls=%fused_computation.19 | convolution fusion | flops 50855936 | bytes 4980736 | tf_op jit(solution)/shard_map/ask,bsk->abk/dot_general | solution.py:77
  69.1 8.0 %fusion.55 = f32[256,64,32]{1,2,0:T(8,128)S(1)} fusion(f32[64,8,256]{0,1,2:T(8,128)} %copy.94, f32[32,8,256]{0,1,2:T(8,128)S(1)} %copy.97), kind=kOutput, calls=%fused_computation.99 | convolution fusion | flops 50331648 | bytes 2883584 | tf_op jit(solution)/shard_map/ask,bsk->abk/dot_general | solution.py:78
  77.2 7.0 %fusion.54 = f32[256,64,32]{1,2,0:T(8,128)S(1)} fusion(f32[64,8,256]{0,1,2:T(8,128)S(1)} %copy-done.8, f32[32,8,256]{0,1,2:T(8,128)S(1)} %copy.95), kind=kOutput, calls=%fused_computation.98 | convolution fusion | flops 50331648 | bytes 2883584 | tf_op jit(solution)/shard_map/ask,bsk->abk/dot_general | solution.py:76
  84.1 8.3 %subtract_bitcast_fusion.2 = f32[32,64,256]{1,0,2:T(8,128)} fusion(f32[256,64,32]{1,2,0:T(8,128)S(1)} %fusion.55, f32[64,8,256]{0,1,2:T(8,128)S(1)} %copy.96, f32[32,8,256]{0,1,2:T(8,128)S(1)} %copy.95), kind=kOutput, calls=%fused_computation.20 | convolution fusion | flops 50855936 | bytes 4980736 | tf_op jit(solution)/shard_map/ask,bsk->abk/dot_general | solution.py:79
  92.5 8.8 %add_bitcast_fusion.2 = f32[32,64,256]{1,0,2:T(8,128)} fusion(f32[256,64,32]{1,2,0:T(8,128)S(1)} %fusion.54, f32[64,8,256]{0,1,2:T(8,128)S(1)} %copy.96, f32[32,8,256]{0,1,2:T(8,128)S(1)} %copy.97), kind=kOutput, calls=%fused_computation.21 | convolution fusion | flops 50855936 | bytes 4980736 | tf_op jit(solution)/shard_map/ask,bsk->abk/dot_general | solution.py:77
  105.4 8.0 %fusion.53 = f32[256,64,32]{1,2,0:T(8,128)S(1)} fusion(f32[64,8,256]{0,1,2:T(8,128)} %copy.90, f32[32,8,256]{0,1,2:T(8,128)S(1)} %copy.93), kind=kOutput, calls=%fused_computation.97 | convolution fusion | flops 50331648 | bytes 2883584 | tf_op jit(solution)/shard_map/ask,bsk->abk/dot_general | solution.py:78
  113.5 8.3 %fusion.52 = f32[256,64,32]{1,2,0:T(8,128)} fusion(f32[64,8,256]{0,1,2:T(8,128)S(1)} %copy-done.10, f32[32,8,256]{0,1,2:T(8,128)S(1)} %copy.91), kind=kOutput, calls=%fused_computation.96 | convolution fusion | flops 50331648 | bytes 2883584 | tf_op jit(solution)/shard_map/ask,bsk->abk/dot_general | solution.py:76
  121.8 8.5 %subtract_bitcast_fusion.3 = f32[32,64,256]{1,0,2:T(8,128)} fusion(f32[256,64,32]{1,2,0:T(8,128)S(1)} %fusion.53, f32[64,8,256]{0,1,2:T(8,128)S(1)} %copy.92, f32[32,8,256]{0,1,2:T(8,128)S(1)} %copy.91), kind=kOutput, calls=%fused_computation.22 | convolution fusion | flops 50855936 | bytes 4980736 | tf_op jit(solution)/shard_map/ask,bsk->abk/dot_general | solution.py:79
  149.6 4.6 %copy.80 = f32[32,64,256]{2,1,0:T(8,128)} copy(f32[32,64,256]{1,0,2:T(8,128)} %add_bitcast_fusion.1) | data formatting | bytes 4194304 | tf_op jit(solution)/shard_map/add | solution.py:80
  160.2 4.6 %copy.73 = f32[32,64,256]{2,1,0:T(8,128)} copy(f32[32,64,256]{1,0,2:T(8,128)} %subtract_bitcast_fusion.2) | data formatting | bytes 4194304 | tf_op jit(solution)/shard_map/sub | solution.py:80
  181.5 5.0 %copy.65 = f32[32,64,256]{2,1,0:T(8,128)} copy(f32[32,64,256]{1,0,2:T(8,128)} %subtract_bitcast_fusion.3) | data formatting | bytes 4194304 | tf_op jit(solution)/shard_map/sub | solution.py:80
  193.8 9.9 %add_bitcast_fusion.3 = f32[32,64,256]{1,0,2:T(8,128)} fusion(f32[256,64,32]{1,2,0:T(8,128)} %fusion.52, f32[64,8,256]{0,1,2:T(8,128)S(1)} %copy.92, f32[32,8,256]{0,1,2:T(8,128)S(1)} %copy-done.3), kind=kOutput, calls=%fused_computation.23 | convolution fusion | flops 50855936 | bytes 4980736 | tf_op jit(solution)/shard_map/ask,bsk->abk/dot_general | solution.py:77
  203.7 4.6 %copy.64 = f32[32,64,256]{2,1,0:T(8,128)} copy(f32[32,64,256]{1,0,2:T(8,128)} %add_bitcast_fusion.3) | data formatting | bytes 4194304 | tf_op jit(solution)/shard_map/add | solution.py:80
  223.2 6.7 %fusion.59 = f32[256,64,32]{1,2,0:T(8,128)S(1)} fusion(f32[64,8,256]{0,1,2:T(8,128)S(1)} %get-tuple-element.6, f32[32,8,256]{0,1,2:T(8,128)S(1)} %copy.102), kind=kOutput, calls=%fused_computation.103 | convolution fusion | flops 50331648 | bytes 2883584 | tf_op jit(solution)/shard_map/ask,bsk->abk/dot_general | solution.py:79
  229.9 8.3 %fusion.58 = f32[256,64,32]{1,2,0:T(8,128)} fusion(f32[64,8,256]{0,1,2:T(8,128)S(1)} %get-tuple-element.6, f32[32,8,256]{0,1,2:T(8,128)S(1)} %copy.103), kind=kOutput, calls=%fused_computation.102 | convolution fusion | flops 50331648 | bytes 2883584 | tf_op jit(solution)/shard_map/ask,bsk->abk/dot_general | solution.py:77
  238.2 8.6 %subtract_bitcast_fusion = f32[32,64,256]{1,0,2:T(8,128)} fusion(f32[256,64,32]{1,2,0:T(8,128)S(1)} %fusion.59, f32[64,8,256]{0,1,2:T(8,128)S(1)} %get-tuple-element.5, f32[32,8,256]{0,1,2:T(8,128)S(1)} %copy.103), kind=kOutput, calls=%fused_computation.16 | convolution fusion | flops 50855936 | bytes 4980736 | tf_op jit(solution)/shard_map/ask,bsk->abk/dot_general | solution.py:78
  246.8 4.6 %copy.89 = f32[32,64,256]{2,1,0:T(8,128)} copy(f32[32,64,256]{1,0,2:T(8,128)} %subtract_bitcast_fusion) | data formatting | bytes 4194304 | tf_op jit(solution)/shard_map/sub | solution.py:80
  259.8 9.9 %add_bitcast_fusion = f32[32,64,256]{1,0,2:T(8,128)} fusion(f32[256,64,32]{1,2,0:T(8,128)} %fusion.58, f32[64,8,256]{0,1,2:T(8,128)S(1)} %get-tuple-element.5, f32[32,8,256]{0,1,2:T(8,128)S(1)} %copy.102), kind=kOutput, calls=%fused_computation.17 | convolution fusion | flops 50855936 | bytes 4980736 | tf_op jit(solution)/shard_map/ask,bsk->abk/dot_general | solution.py:76
  279.7 5.3 %maximum_maximum_fusion = f32[128,32,512]{2,1,0:T(8,128)} fusion(f32[32,32,256]{2,1,0:T(8,128)} %slice.241, f32[32,32,256]{2,1,0:T(8,128)S(1)} %slice.239, f32[32,32,256]{2,1,0:T(8,128)S(1)} %slice-done, f32[32,32,256]{2,1,0:T(8,128)S(1)} %slice-done.1, f32[32,32,256]{2,1,0:T(8,128)S(1)} %slice-done.2, f32[32,32,256]{2,1,0:T(8,128)S(1)} %slice-done.3, ...), kind=kLoop, calls=%fused_computation | loop fusion | flops 14680064 | bytes 16777216 | tf_op jit(solution)/shard_map/concatenate | solution.py:81
  286.1 147.8 %reduce-scatter.2.cloned.1.call-done = f32[32,32,512]{2,1,0:T(8,128)} async-done(((f32[128,32,512]{2,1,0:T(8,128)}), f32[32,32,512]{2,1,0:T(8,128)}) %reduce-scatter.2.cloned.1.call-update) | async-done | bytes 2097168 | tf_op jit(solution)/shard_map/reduce_scatter | solution.py:83
  (121 shorter events, 115.2 us)
Async XLA Ops:
  6.5 2.1 copy-start
  6.5 427.3 %reduce-scatter.2.cloned.1.call-start = ((), (), s32[]{:S(2)}) async-start(), calls=%async_computation.1 | async-start | bytes 10485760 | tf_op jit(solution)/shard_map/reduce_scatter | solution.py:83
  17.4 3.8 copy-start.4
  17.5 3.8 copy-start.6
  19.8 197.0 %collective-permute-start = (f32[32,8,512]{2,1,0:T(8,128)}, f32[32,8,512]{2,1,0:T(8,128)}, u32[]{:S(2)}, u32[]{:S(2)}) collective-permute-start(f32[32,8,512]{2,1,0:T(8,128)} %bitcast.3), channel_id=1, source_target_pairs={{4,0},{8,4},{12,8},{16,12},{20,16},{24,20},{28,24},{5,1},{9,5},{13... | collective-permute-start | bytes 1572872 | tf_op jit(solution)/shard_map/ppermute | solution.py:16
  27.3 1.5 copy-start.14
  32.0 8.1 %copy-start.9 = (f32[64,8,256]{0,1,2:T(8,128)S(1)}, f32[64,8,256]{0,1,2:T(8,128)}, u32[]{:S(2)}) copy-start(f32[64,8,256]{0,1,2:T(8,128)} %copy.98) | copy-start | bytes 1572868
  55.6 8.5 %copy-start.12 = (f32[512,512]{0,1:T(8,128)S(1)}, f32[512,512]{0,1:T(8,128)}, u32[]{:S(2)}) copy-start(f32[512,512]{0,1:T(8,128)} %get-tuple-element.10) | copy-start | bytes 3145732
  64.4 1.5 copy-start.13
  69.1 8.1 %copy-start.8 = (f32[64,8,256]{0,1,2:T(8,128)S(1)}, f32[64,8,256]{0,1,2:T(8,128)}, u32[]{:S(2)}) copy-start(f32[64,8,256]{0,1,2:T(8,128)} %copy.94) | copy-start | bytes 1572868
  92.5 8.8 %copy-start.11 = (f32[512,512]{0,1:T(8,128)S(1)}, f32[512,512]{0,1:T(8,128)}, u32[]{:S(2)}) copy-start(f32[512,512]{0,1:T(8,128)} %get-tuple-element.9) | copy-start | bytes 3145732
  101.6 1.5 copy-start.16
  103.5 9.9 %copy-start.2 = (f32[32,8,256]{0,1,2:T(8,128)}, f32[32,8,256]{0,1,2:T(8,128)S(1)}, u32[]{:S(2)}) copy-start(f32[32,8,256]{0,1,2:T(8,128)S(1)} %copy.93) | copy-start | bytes 786436
  105.4 8.1 %copy-start.10 = (f32[64,8,256]{0,1,2:T(8,128)S(1)}, f32[64,8,256]{0,1,2:T(8,128)}, u32[]{:S(2)}) copy-start(f32[64,8,256]{0,1,2:T(8,128)} %copy.90) | copy-start | bytes 1572868
  121.8 8.5 %copy-start.5 = (f32[1024,256]{0,1:T(8,128)S(1)}, f32[1024,256]{0,1:T(8,128)}, u32[]{:S(2)}) copy-start(f32[1024,256]{0,1:T(8,128)} %copy-done.4) | copy-start | bytes 3145732
  121.8 8.5 %copy-start.7 = (f32[1024,256]{0,1:T(8,128)S(1)}, f32[1024,256]{0,1:T(8,128)}, u32[]{:S(2)}) copy-start(f32[1024,256]{0,1:T(8,128)} %copy-done.6) | copy-start | bytes 3145732
  134.9 3.1 copy-start.15
  192.6 1.2 copy-start.3
  274.8 4.4 slice-start
  274.8 4.4 slice-start.1
  274.8 4.4 slice-start.2
  277.8 1.5 slice-start.3
  277.8 1.9 slice-start.4
  285.0 153.2 %copy-start.1 = (f32[128,8,512]{2,1,0:T(8,128)S(1)}, f32[128,8,512]{2,1,0:T(8,128)}, u32[]{:S(2)}) copy-start(f32[128,8,512]{2,1,0:T(8,128)} %param.1) | copy-start | bytes 6291460
Sparse Core Ops, SparseCore 0:
  285.1 148.7 reduce-scatter.1
where the time goes:
time: 454 us; the launch traced here: 445 us
  waiting for transfers between devices  148 us (33%)
  matrix products  145 us (32%)
  local copies, waits for them, and re-layouts  120 us (26%)
  other arithmetic  16.7 us (4%)
  between operations  14.1 us (3%)
    reduce_scatter x1, waiting for transfers between devices, shards(): stacked = lax.psum_scatter(pairs, 'tm', scatter_dimension=0, tiled=True)  148 us
    dot_general x4, matrix products, shards(): jnp.einsum('ask,bsk->abk', first_im, second_im, precision=lax.Precision.H...  35.5 us
    dot_general x4, matrix products, shards(): jnp.einsum('ask,bsk->abk', first_im, second_re, precision=lax.Precision.H...  32.7 us
    dot_general x4, matrix products, shards(): jnp.einsum('ask,bsk->abk', first_re, second_re, precision=lax.Precision.H...  32.3 us
    dot_general x4, matrix products, shards(): jnp.einsum('ask,bsk->abk', first_re, second_im, precision=lax.Precision.H...  32 us
    reshape x8, local copies, waits for them, and re-layouts, band_of(): return flat_rows.reshape(count, 2 * count + 1, width)[:, :count]  22.4 us
    sub x4, local copies, waits for them, and re-layouts, shards(): im_re - re_im  18.9 us
    add x4, local copies, waits for them, and re-layouts, shards(): both_re + both_im  17.5 us
  transfers between devices with their start and end apart: 2, of which 1 were waited for; matrix products, arithmetic and copies ran while one was open for 44% of the time, Pallas kernels for 0%

commit v1 on v0

v1 whole, which is shorter than its diff:
```python
import functools

import jax
import jax.numpy as jnp
import ml_dtypes
import numpy as np
from jax import lax
from jax.experimental import pallas as pl
from jax.experimental.pallas import tpu as pltpu
from jax.sharding import PartitionSpec as P

NEAR = 32
LAGS = 256
HALF = 8
LANES = 128
VMEM_LIMIT = 48 << 20


def split_table(table):
    high = table.astype(ml_dtypes.bfloat16)
    low = (table - high.astype(np.float64)).astype(ml_dtypes.bfloat16)
    return np.stack([high, low])


def make_tables(win, lags, segs):
    bins = win // 2
    samples = np.arange(win)
    hann = 0.5 - 0.5 * np.cos(2.0 * np.pi * samples / win)
    even, odd = np.arange(2, bins + 1, 2), np.arange(1, bins, 2)
    order = np.concatenate([even, odd])

    def forward(picked):
        phases = 2.0 * np.pi * ((samples[: win // 2, None] * picked[None, :]) % win) / win
        return split_table(np.concatenate([np.cos(phases), -np.sin(phases)], axis=1))

    near = np.abs(order[:, None] - order[None, :]) <= HALF
    band = near / (2.0 * HALF + 1.0) + 0.1 / bins
    lag = np.arange(lags) - lags // 2
    phases = 2.0 * np.pi * ((order[:, None] * lag[None, :]) % win) / win
    inverse = np.concatenate([np.cos(phases), -np.sin(phases)], axis=0) / segs
    return {
        "hann": hann.astype(np.float32)[None, :],
        "even": forward(even),
        "odd": forward(odd),
        "band": split_table(band),
        "inverse": split_table(inverse),
    }


def dot_split(value, table):
    high = value.astype(jnp.bfloat16)
    low = (value - high.astype(jnp.float32)).astype(jnp.bfloat16)
    dot = functools.partial(jnp.dot, preferred_element_type=jnp.float32)
    return dot(high, table[0]) + (dot(high, table[1]) + dot(low, table[0]))


def whiten_kernel(x_ref, hann, even, odd, band, w_ref, stage):
    channels, segs, win = x_ref.shape
    parts = win // LANES
    for part in range(parts):
        lanes = slice(LANES * part, LANES * part + LANES)
        stage[part] = x_ref[:, :, lanes].reshape(channels * segs, LANES)
    pieces = []
    for s in range(segs):
        pieces.append([
            stage[part, pl.ds(s, channels, stride=segs), :] * hann[:, LANES * part : LANES * part + LANES]
            for part in range(parts)
        ])
    quarter = [jnp.concatenate([piece[part] for piece in pieces], axis=0) for part in range(parts)]
    both = jnp.concatenate([quarter[0] + quarter[2], quarter[1] + quarter[3]], axis=1)
    between = jnp.concatenate([quarter[0] - quarter[2], quarter[1] - quarter[3]], axis=1)
    spectra = (dot_split(both, even), dot_split(between, odd))
    energy = jnp.concatenate(
        [sp[:, :LANES] * sp[:, :LANES] + sp[:, LANES:] * sp[:, LANES:] for sp in spectra], axis=1
    )
    scale = lax.rsqrt(dot_split(energy, band) + 1e-06)
    for half, sp in enumerate(spectra):
        own = scale[:, LANES * half : LANES * half + LANES]
        real, imag = sp[:, :LANES] * own, sp[:, LANES:] * own
        for s in range(segs):
            rows = slice(channels * s, channels * s + channels)
            w_ref[half, 0, s] = real[rows]
            w_ref[half, 1, s] = imag[rows]


def whiten(x, tables):
    blocks, near, segs, win = x.shape
    whole = lambda a: pl.BlockSpec(a.shape, lambda i: (0,) * a.ndim)
    names = ("hann", "even", "odd", "band")
    consts = [jnp.asarray(tables[name]) for name in names]
    return pl.pallas_call(
        whiten_kernel,
        grid=(blocks,),
        in_specs=[pl.BlockSpec((None, near, segs, win), lambda i: (i, 0, 0, 0))] + [whole(c) for c in consts],
        out_specs=pl.BlockSpec((None, 2, 2, segs, near, LANES), lambda i: (i, 0, 0, 0, 0, 0)),
        out_shape=jax.ShapeDtypeStruct((blocks, 2, 2, segs, near, LANES), jnp.float32),
        scratch_shapes=[pltpu.VMEM((win // LANES, near * segs, LANES), jnp.float32)],
        compiler_params=pltpu.CompilerParams(vmem_limit_bytes=VMEM_LIMIT),
        cost_estimate=pl.CostEstimate(flops=blocks * 500_000_000, bytes_accessed=blocks << 20, transcendentals=0),
        name="whiten",
    )(x, *consts)


def cross_kernel(count, first, pick_ref, *refs):
    cands = refs[: 2 * count]
    rest = refs[2 * count :]
    prior, (acc, pair) = (None, rest) if first else (rest[0], rest[1:])
    _, segs, near, _ = cands[0].shape
    for side in range(2):
        for part in range(2):
            for s in range(segs):
                value = cands[side * count][part, s]
                for other in range(1, count):
                    value = jnp.where(pick_ref[0] == other, cands[side * count + other][part, s], value)
                pair[part, s, pl.ds(side * near, near), :] = value
    for group in range(near // 8):
        rows = pl.ds(8 * group, 8)
        real = [pair[0, s, rows, :] for s in range(segs)]
        imag = [pair[1, s, rows, :] for s in range(segs)]
        added = [real[s] + imag[s] for s in range(segs)]
        for offset in range(1, near + 1):
            ahead = pl.ds(8 * group + offset, 8)
            rr = ii = mixed = None
            for s in range(segs):
                other_re, other_im = pair[0, s, ahead, :], pair[1, s, ahead, :]
                terms = (real[s] * other_re, imag[s] * other_im, added[s] * (other_re - other_im))
                if rr is None:
                    rr, ii, mixed = terms
                else:
                    rr, ii, mixed = rr + terms[0], ii + terms[1], mixed + terms[2]
            cross_re, cross_im = rr + ii, mixed - rr + ii
            if not first:
                cross_re = cross_re + prior[0, offset - 1, rows, :]
                cross_im = cross_im + prior[1, offset - 1, rows, :]
            acc[0, offset - 1, rows, :] = cross_re
            acc[1, offset - 1, rows, :] = cross_im


def cross(pick, firsts, seconds, prior=None):
    count = len(firsts)
    halves, parts, segs, near, lanes = firsts[0].shape
    half_spec = pl.BlockSpec((None, parts, segs, near, lanes), lambda i, p: (i, 0, 0, 0, 0))
    acc_spec = pl.BlockSpec((None, 2, near, near, lanes), lambda i, p: (i, 0, 0, 0, 0))
    first = prior is None
    return pl.pallas_call(
        functools.partial(cross_kernel, count, first),
        grid_spec=pltpu.PrefetchScalarGridSpec(
            num_scalar_prefetch=1,
            grid=(halves,),
            in_specs=[half_spec] * (2 * count) + ([] if first else [acc_spec]),
            out_specs=acc_spec,
            scratch_shapes=[pltpu.VMEM((parts, segs, 2 * near, lanes), jnp.float32)],
        ),
        out_shape=jax.ShapeDtypeStruct((halves, 2, near, near, lanes), jnp.float32),
        compiler_params=pltpu.CompilerParams(vmem_limit_bytes=VMEM_LIMIT),
        cost_estimate=pl.CostEstimate(flops=4_000_000_000, bytes_accessed=4 << 20, transcendentals=0),
        name="cross",
    )(pick, *firsts, *seconds, *([] if first else [prior]))


def invert_kernel(acc, table, out_ref, stage):
    near = acc.shape[3]
    chunks = 4
    step = near // chunks
    for chunk in range(chunks):
        offsets = slice(chunk * step, chunk * step + step)
        lhs = jnp.concatenate(
            [acc[half, part, offsets].reshape(step * near, LANES) for part in range(2) for half in range(2)], axis=1
        )
        lagged = dot_split(lhs, table)
        for part in range(lagged.shape[1] // LANES):
            for j in range(step):
                stage[part, pl.ds(chunk * step + j, near, stride=near), :] = lagged[
                    near * j : near * j + near, LANES * part : LANES * part + LANES
                ]
    for part in range(stage.shape[0]):
        out_ref[:, :, LANES * part : LANES * part + LANES] = stage[part].reshape(near, near, LANES)


def invert(acc, tables):
    near = acc.shape[3]
    vmem = pl.BlockSpec(memory_space=pltpu.VMEM)
    return pl.pallas_call(
        invert_kernel,
        in_specs=[vmem, vmem],
        out_specs=vmem,
        out_shape=jax.ShapeDtypeStruct((near, near, LAGS), jnp.float32),
        scratch_shapes=[pltpu.VMEM((LAGS // LANES, near * near, LANES), jnp.float32)],
        compiler_params=pltpu.CompilerParams(vmem_limit_bytes=VMEM_LIMIT),
        cost_estimate=pl.CostEstimate(flops=2_000_000_000, bytes_accessed=3 << 20, transcendentals=0),
        name="invert",
    )(acc, jnp.asarray(tables["inverse"]))


def shifted(value, steps):
    count = lax.axis_size("fibre")
    return lax.ppermute(value, "fibre", [(source, source + steps) for source in range(max(0, -steps), count)])


def line_of_four(traces):
    channels, segs, win = traces.shape
    tables = make_tables(win, LAGS, segs * 4)
    z = lax.axis_index("tm")
    blocks = traces.reshape(4, NEAR, segs, win)
    halo = shifted(blocks[0], -1)
    own = whiten(blocks, tables)
    ahead = whiten(halo[None], tables)[0]
    own5 = jnp.concatenate([own, ahead[None]], axis=0)

    def block(at):
        return lax.dynamic_index_in_dim(own5, at, 0, keepdims=False)

    def choose(*picks):
        return block(jnp.asarray(picks, jnp.int32)[z])

    def outer(value):
        return lax.ppermute(value, "tm", [(0, 1), (3, 2)])

    def middle(value):
        return lax.ppermute(value, "tm", [(1, 2), (2, 1)])

    def inner(value):
        return lax.ppermute(value, "tm", [(1, 0), (2, 3)])

    far = choose(3, 3, 0, 0)
    farther = choose(4, 4, 1, 1)
    e1 = outer(far)
    m1 = middle(far)
    i1 = inner(choose(0, 0, 3, 3))
    e2 = outer(farther)
    m2 = middle(farther)
    i2 = inner(choose(1, 1, 4, 4))
    second = own[2]
    m3 = middle(second)
    e3 = outer(second)
    m4 = middle(e1)
    i3 = inner(m1)
    e4 = outer(choose(1, 1, 3, 3))
    m5 = middle(e2)
    i4 = inner(m2)
    m6 = middle(e3)
    i5 = inner(m4)
    i6 = inner(m5)
    role = jnp.asarray([0, 1, 2, 0], jnp.int32)[z][None]
    zero = jnp.zeros((1,), jnp.int32)
    acc = cross(zero, [block(z)], [block(z + 1)])
    acc = cross(role, [i1, e4, e3], [i2, e3, e4], acc)
    acc = cross(role, [i3, m2, m3], [i4, m3, m1], acc)
    acc = cross(role, [i5, m5, m6], [i6, m6, m4], acc)
    return invert(acc, tables)


def band_of(products):
    count, _, width = products.shape[0], products.shape[1], products.shape[2]
    flat_rows = products.reshape(count * 2 * count, width)[1:]
    flat_rows = jnp.pad(flat_rows, ((0, count + 1), (0, 0)))
    return flat_rows.reshape(count, 2 * count + 1, width)[:, :count]


def any_line(traces):
    channels, segs, win = traces.shape
    bins = win // 2
    axis = lax.axis_size("tm")
    tables = make_tables(win, LAGS, segs * axis)
    blocks = traces.reshape(channels // NEAR, NEAR, segs, win)
    halo = shifted(blocks[0], -1)
    spectra = whiten(jnp.concatenate([blocks, halo[None]], axis=0), tables)
    zero = jnp.zeros((1,), jnp.int32)
    inverse = tables["inverse"].astype(np.float32)
    inverse = jnp.asarray(inverse[0] + inverse[1])
    pieces = []
    for index in range(channels // NEAR):
        acc = cross(zero, [spectra[index]], [spectra[index + 1]])
        pairs = acc.transpose(3, 2, 1, 0, 4).reshape(NEAR * NEAR, 2 * bins)
        pieces.append(jnp.dot(pairs, inverse, precision=lax.Precision.HIGHEST))
    lagged = jnp.concatenate(pieces, axis=0).reshape(channels, NEAR, LAGS)
    return lax.psum_scatter(lagged, "tm", scatter_dimension=0, tiled=True)


def shards(traces):
    if lax.axis_size("tm") == 4 and traces.shape[0] == 4 * NEAR:
        return line_of_four(traces)
    return any_line(traces)


def solution(mesh):
    in_specs = (P("fibre", "tm", None),)
    out_specs = P(("fibre", "tm"), None, None)
    return jax.shard_map(shards, mesh=mesh, in_specs=in_specs, out_specs=out_specs, check_vma=False)
```

time: 454 us -> 145 us (0.32); the launches traced: 445 us -> 145 us
  matrix products: 145 us -> 0 us
  local copies, waits for them, and re-layouts: 120 us -> 19.7 us
  waiting for transfers between devices: 148 us -> 58.5 us
  starting transfers between devices: 1.49 us -> 31.7 us
  Pallas kernels: 0 us -> 23 us
  other arithmetic: 16.7 us -> 1.91 us
    reduce_scatter x1 -> x0, waiting for transfers between devices: 148 us -> none  [shards(): stacked = lax.psum_scatter(pairs, 'tm', scatter_dimension=0, tiled=True)]
    dot_general x19 -> x0, matrix products: 145 us -> none  [the longest x4 35.5 us: shards(): jnp.einsum('ask,bsk->abk', first_im, second_im, precision=lax.Precision.H...]
    ppermute x1 -> x17, waiting for transfers between devices: 0.01 us -> 58.5 us  [the longest x6 39.5 us: inner(): return lax.ppermute(value, 'tm', [(1, 0), (2, 3)])]
    ppermute x1 -> x17, starting transfers between devices: 1.49 us -> 31.7 us  [the longest x4 14.7 us: outer(): return lax.ppermute(value, 'tm', [(0, 1), (3, 2)])]
    reshape x9 -> x0, local copies, waits for them, and re-layouts: 25.5 us -> none  [the longest x8 22.4 us: band_of(): return flat_rows.reshape(count, 2 * count + 1, width)[:, :count]]
    slice x35 -> x1, local copies, waits for them, and re-layouts: 26.6 us -> 1.08 us  [line_of_four(): halo = shifted(blocks[0], -1)]
    pallas_call x0 -> x7, Pallas kernels: none -> 23 us  [the longest x4 16.3 us: cross(): pl.pallas_call(functools.partial(cross_kernel, count, first), grid_spec=p...]
    sub x4 -> x0, local copies, waits for them, and re-layouts: 18.9 us -> none  [shards(): im_re - re_im]
  transfers between devices with their start and end apart: 2 -> 17, of which waited for: 1 -> 8; matrix products, arithmetic and copies ran while one was open for 44% -> 5% of each run, Pallas kernels for 0% -> 10%
where the time goes in v1:
time: 145 us
  waiting for transfers between devices  58.5 us (40%)
  starting transfers between devices  31.7 us (22%)
  Pallas kernels  23 us (16%)
  local copies, waits for them, and re-layouts  19.7 us (14%)
  between operations  9.68 us (7%)
  other arithmetic  1.91 us (1%)
    ppermute x6, waiting for transfers between devices, inner(): return lax.ppermute(value, 'tm', [(1, 0), (2, 3)])  39.5 us
    ppermute x4, waiting for transfers between devices, outer(): return lax.ppermute(value, 'tm', [(0, 1), (3, 2)])  19 us
    pallas_call x4, Pallas kernels, cross(): pl.pallas_call(functools.partial(cross_kernel, count, first), grid_spec=p...  16.3 us
    ppermute x4, starting transfers between devices, outer(): return lax.ppermute(value, 'tm', [(0, 1), (3, 2)])  14.7 us
    unnamed x32, local copies, waits for them, and re-layouts  11.6 us
    ppermute x6, starting transfers between devices, middle(): return lax.ppermute(value, 'tm', [(1, 2), (2, 1)])  7.97 us
    ppermute x6, starting transfers between devices, inner(): return lax.ppermute(value, 'tm', [(1, 0), (2, 3)])  7.74 us
    dynamic_slice x5, local copies, waits for them, and re-layouts, choose(): return block(jnp.asarray(picks, jnp.int32)[z])  6.38 us
  transfers between devices with their start and end apart: 17, of which 8 were waited for; matrix products, arithmetic and copies ran while one was open for 5% of the time, Pallas kernels for 10%

profile of v1, /device:TPU:0, one launch (start us, length us, event | category | flops | bytes accessed | tf_op | source)
XLA Modules:
  0.0 144.5 jit_solution(7002358501812763592)
XLA Ops:
  18.2 1.6 %copy-done = f32[128,8,512]{2,1,0:T(8,128)S(1)} copy-done((f32[128,8,512]{2,1,0:T(8,128)S(1)}, f32[128,8,512]{2,1,0:T(8,128)}, u32[]{:S(2)}) %copy-start) | copy-done | bytes 2097176
  23.3 3.2 %whiten.2 = f32[4,2,2,8,32,128]{5,4,3,2,1,0:T(8,128)S(1)} custom-call(f32[4,32,8,512]{3,2,1,0:T(8,128)S(1)} %bitcast.23, f32[1,512]{1,0:T(1,128)S(1)} %copy-done.11, bf16[2,256,256]{2,1,0:T(8,128)(2,1)S(1)} %copy-done.8, bf16[2,256,256]{2,1,0:T(8,128)(2,1)S(1)} %copy-done.9, bf16[2,256,256]{2,1,0:T(8,128)(2,1)S(1)} %copy-done.10), custom_call_target="tpu_custom_call" | custom-call | flops 2000000000 | bytes 4194304 | tf_op jit(solution)/shard_map/whiten/pallas_call | solution.py:91
  27.3 1.8 %fusion.1 = (f32[2,2,8,32,128]{4,3,2,1,0:T(8,128)S(1)}, f32[2,2,8,32,128]{4,3,2,1,0:T(8,128)}, f32[2,2,8,32,128]{4,3,2,1,0:T(8,128)}, f32[2,2,8,32,128]{4,3,2,1,...) fusion(s32[]{:T(128)S(6)} %select_n.37, ...), kind=kLoop, calls=%fused_computation.15 | loop fusion | flops 786432 | bytes 6815768 | tf_op jit(solution)/shard_map/jit(dynamic_index_in_dim)/squeeze | solution.py:211
  30.4 5.0 %collective-permute-start.15 = (f32[2,2,8,32,128]{4,3,2,1,0:T(8,128)S(1)}, f32[2,2,8,32,128]{4,3,2,1,0:T(8,128)S(1)}, u32[]{:S(2)}, u32[]{:S(2)}) collective-permute-start(f32[2,2,8,32,128]{4,3,2,1,0:T(8,128)S(1)} %get-tuple-element.9), channel_id=1, source_target_pairs={{0,1},{3,2},{4,5},{7,6},{8,9},{11,10},{12,13},{15,14},{16,17},{19,... | collective-permute-start | bytes 1572872 | tf_op jit(solution)/shard_map/ppermute | solution.py:217
  36.7 5.4 %collective-permute-start.6 = (f32[2,2,8,32,128]{4,3,2,1,0:T(8,128)}, f32[2,2,8,32,128]{4,3,2,1,0:T(8,128)}, u32[]{:S(2)}, u32[]{:S(2)}) collective-permute-start(f32[2,2,8,32,128]{4,3,2,1,0:T(8,128)} %get-tuple-element.11), channel_id=1, source_target_pairs={{0,1},{3,2},{4,5},{7,6},{8,9},{11,10},{12,13},{15,14},{16,17},{19,... | collective-permute-start | bytes 1572872 | tf_op jit(solution)/shard_map/ppermute | solution.py:217
  42.1 2.1 %collective-permute-start.1 = (f32[2,2,8,32,128]{4,3,2,1,0:T(8,128)}, f32[2,2,8,32,128]{4,3,2,1,0:T(8,128)}, u32[]{:S(2)}, u32[]{:S(2)}) collective-permute-start(f32[2,2,8,32,128]{4,3,2,1,0:T(8,128)} %get-tuple-element.6), channel_id=1, source_target_pairs={{0,1},{3,2},{4,5},{7,6},{8,9},{11,10},{12,13},{15,14},{16,17},{19,... | collective-permute-start | bytes 1572872 | tf_op jit(solution)/shard_map/ppermute | solution.py:217
  44.2 1.6 %collective-permute-done.14.refs_0_ = f32[2,2,8,32,128]{4,3,2,1,0:T(8,128)S(1)} collective-permute-done((f32[2,2,8,32,128]{4,3,2,1,0:T(8,128)S(1)}, f32[2,2,8,32,128]{4,3,2,1,0:T(8,128)S(1)}, u32[]{:S(2)}, u32[]{:S(2)}) %collective-permute-start.14) | collective-permute-done | bytes 524320 | tf_op jit(solution)/shard_map/ppermute | solution.py:223
  46.6 2.3 %collective-permute-start.4 = (f32[2,2,8,32,128]{4,3,2,1,0:T(8,128)}, f32[2,2,8,32,128]{4,3,2,1,0:T(8,128)}, u32[]{:S(2)}, u32[]{:S(2)}) collective-permute-start(f32[2,2,8,32,128]{4,3,2,1,0:T(8,128)} %get-tuple-element.7), channel_id=1, source_target_pairs={{0,1},{3,2},{4,5},{7,6},{8,9},{11,10},{12,13},{15,14},{16,17},{19,... | collective-permute-start | bytes 1572872 | tf_op jit(solution)/shard_map/ppermute | solution.py:217
  49.7 1.5 %collective-permute-start.9 = (f32[2,2,8,32,128]{4,3,2,1,0:T(8,128)}, f32[2,2,8,32,128]{4,3,2,1,0:T(8,128)}, u32[]{:S(2)}, u32[]{:S(2)}) collective-permute-start(f32[2,2,8,32,128]{4,3,2,1,0:T(8,128)} %get-tuple-element.6), channel_id=1, source_target_pairs={{1,2},{2,1},{5,6},{6,5},{9,10},{10,9},{13,14},{14,13},{17,18},{18,... | collective-permute-start | bytes 1572872 | tf_op jit(solution)/shard_map/ppermute | solution.py:220
  51.1 5.9 %collective-permute-done.16.refs_3_ = f32[2,2,8,32,128]{4,3,2,1,0:T(8,128)S(1)} collective-permute-done((f32[2,2,8,32,128]{4,3,2,1,0:T(8,128)S(1)}, f32[2,2,8,32,128]{4,3,2,1,0:T(8,128)S(1)}, u32[]{:S(2)}, u32[]{:S(2)}) %collective-permute-start.16) | collective-permute-done | bytes 524320 | tf_op jit(solution)/shard_map/ppermute | solution.py:223
  57.9 1.5 %collective-permute-start.11 = (f32[2,2,8,32,128]{4,3,2,1,0:T(8,128)}, f32[2,2,8,32,128]{4,3,2,1,0:T(8,128)}, u32[]{:S(2)}, u32[]{:S(2)}) collective-permute-start(f32[2,2,8,32,128]{4,3,2,1,0:T(8,128)} %get-tuple-element.7), channel_id=1, source_target_pairs={{1,2},{2,1},{5,6},{6,5},{9,10},{10,9},{13,14},{14,13},{17,18},{18,... | collective-permute-start | bytes 1572872 | tf_op jit(solution)/shard_map/ppermute | solution.py:220
  59.4 1.5 %collective-permute-start.12 = (f32[2,2,8,32,128]{4,3,2,1,0:T(8,128)}, f32[2,2,8,32,128]{4,3,2,1,0:T(8,128)}, u32[]{:S(2)}, u32[]{:S(2)}) collective-permute-start(f32[2,2,8,32,128]{4,3,2,1,0:T(8,128)} %get-tuple-element.11), channel_id=1, source_target_pairs={{1,2},{2,1},{5,6},{6,5},{9,10},{10,9},{13,14},{14,13},{17,18},{18,... | collective-permute-start | bytes 1572872 | tf_op jit(solution)/shard_map/ppermute | solution.py:220
  60.9 9.2 %collective-permute-done.1 = f32[2,2,8,32,128]{4,3,2,1,0:T(8,128)} collective-permute-done((f32[2,2,8,32,128]{4,3,2,1,0:T(8,128)}, f32[2,2,8,32,128]{4,3,2,1,0:T(8,128)}, u32[]{:S(2)}, u32[]{:S(2)}) %collective-permute-start.1) | collective-permute-done | bytes 524320 | tf_op jit(solution)/shard_map/ppermute | solution.py:217
  71.6 9.8 %collective-permute-done.4 = f32[2,2,8,32,128]{4,3,2,1,0:T(8,128)} collective-permute-done((f32[2,2,8,32,128]{4,3,2,1,0:T(8,128)}, f32[2,2,8,32,128]{4,3,2,1,0:T(8,128)}, u32[]{:S(2)}, u32[]{:S(2)}) %collective-permute-start.4) | collective-permute-done | bytes 524320 | tf_op jit(solution)/shard_map/ppermute | solution.py:217
  81.3 1.5 %collective-permute-start.5 = (f32[2,2,8,32,128]{4,3,2,1,0:T(8,128)}, f32[2,2,8,32,128]{4,3,2,1,0:T(8,128)}, u32[]{:S(2)}, u32[]{:S(2)}) collective-permute-start(f32[2,2,8,32,128]{4,3,2,1,0:T(8,128)} %collective-permute-done.4), channel_id=1, source_target_pairs={{1,2},{2,1},{5,6},{6,5},{9,10},{10,9},{13,14},{14,13},{17,18},{18,... | collective-permute-start | bytes 1572872 | tf_op jit(solution)/shard_map/ppermute | solution.py:220
  86.2 2.4 %cross.4.refs_6_ = f32[2,2,32,32,128]{4,3,2,1,0:T(8,128)S(1)} custom-call(s32[1]{0:T(128)} %constant.50.clone.1.pick_ref, f32[2,2,8,32,128]{4,3,2,1,0:T(8,128)S(1)} %fusion.13.refs_0_, f32[2,2,8,32,128]{4,3,2,1,0:T(8,128)S(1)} %get-tuple-element.5.refs_1_), custom_call_target="tpu_custom_call" | custom-call | flops 4000000000 | bytes 4194304 | tf_op jit(solution)/shard_map/cross/pallas_call | solution.py:145
  93.3 4.6 %cross.5.refs_6_ = f32[2,2,32,32,128]{4,3,2,1,0:T(8,128)S(1)} custom-call(s32[1]{0:T(128)} %dynamic_slice.40.pick_ref, f32[2,2,8,32,128]{4,3,2,1,0:T(8,128)S(1)} %copy-done.2, f32[2,2,8,32,128]{4,3,2,1,0:T(8,128)S(1)} %copy-done.4, f32[2,2,8,32,128]{4,3,2,1,0:T(8,128)} %collective-permute-done.6.refs_2_.refs_4_, f32[2,2,8,32,128]{4,3,2,1,0:T(8,128)S(1)} %copy-done.6, ...), custom_call_target="tpu_custom_call" | custom-call | flops 4000000000 | bytes 4194304 | tf_op jit(solution)/shard_map/cross/pallas_call | solution.py:145
  99.2 5.3 %collective-permute-done.10.refs_0_ = f32[2,2,8,32,128]{4,3,2,1,0:T(8,128)S(1)} collective-permute-done((f32[2,2,8,32,128]{4,3,2,1,0:T(8,128)}, f32[2,2,8,32,128]{4,3,2,1,0:T(8,128)S(1)}, u32[]{:S(2)}, u32[]{:S(2)}) %collective-permute-start.10) | collective-permute-done | bytes 524320 | tf_op jit(solution)/shard_map/ppermute | solution.py:223
  104.5 11.2 %collective-permute-done.13.refs_3_ = f32[2,2,8,32,128]{4,3,2,1,0:T(8,128)S(1)} collective-permute-done((f32[2,2,8,32,128]{4,3,2,1,0:T(8,128)}, f32[2,2,8,32,128]{4,3,2,1,0:T(8,128)S(1)}, u32[]{:S(2)}, u32[]{:S(2)}) %collective-permute-start.13) | collective-permute-done | bytes 524320 | tf_op jit(solution)/shard_map/ppermute | solution.py:223
  115.8 4.7 %cross.6.refs_6_ = f32[2,2,32,32,128]{4,3,2,1,0:T(8,128)S(1)} custom-call(s32[1]{0:T(128)} %dynamic_slice.40.pick_ref, f32[2,2,8,32,128]{4,3,2,1,0:T(8,128)S(1)} %collective-permute-done.10.refs_0_, f32[2,2,8,32,128]{4,3,2,1,0:T(8,128)} %collective-permute-done.11.refs_1_, f32[2,2,8,32,128]{4,3,2,1,0:T(8,128)} %collective-permute-done.12.refs_2_.refs_4_, ...), custom_call_target="tpu_custom_call" | custom-call | flops 4000000000 | bytes 4194304 | tf_op jit(solution)/shard_map/cross/pallas_call | solution.py:145
  121.9 5.1 %collective-permute-done.3.refs_0_ = f32[2,2,8,32,128]{4,3,2,1,0:T(8,128)S(1)} collective-permute-done((f32[2,2,8,32,128]{4,3,2,1,0:T(8,128)}, f32[2,2,8,32,128]{4,3,2,1,0:T(8,128)S(1)}, u32[]{:S(2)}, u32[]{:S(2)}) %collective-permute-start.3) | collective-permute-done | bytes 524320 | tf_op jit(solution)/shard_map/ppermute | solution.py:223
  127.0 10.3 %collective-permute-done.8.refs_3_ = f32[2,2,8,32,128]{4,3,2,1,0:T(8,128)S(1)} collective-permute-done((f32[2,2,8,32,128]{4,3,2,1,0:T(8,128)}, f32[2,2,8,32,128]{4,3,2,1,0:T(8,128)S(1)}, u32[]{:S(2)}, u32[]{:S(2)}) %collective-permute-start.8) | collective-permute-done | bytes 524320 | tf_op jit(solution)/shard_map/ppermute | solution.py:223
  137.3 4.6 %cross.7.acc = f32[2,2,32,32,128]{4,3,2,1,0:T(8,128)S(1)} custom-call(s32[1]{0:T(128)} %dynamic_slice.40.pick_ref, f32[2,2,8,32,128]{4,3,2,1,0:T(8,128)S(1)} %collective-permute-done.3.refs_0_, f32[2,2,8,32,128]{4,3,2,1,0:T(8,128)} %collective-permute-done.5.refs_1_, f32[2,2,8,32,128]{4,3,2,1,0:T(8,128)S(1)} %collective-permute-done.7.refs_2_.refs_4_, ...), custom_call_target="tpu_custom_call" | custom-call | flops 4000000000 | bytes 4194304 | tf_op jit(solution)/shard_map/cross/pallas_call | solution.py:145
  141.9 2.7 %invert.1 = f32[32,32,256]{2,1,0:T(8,128)} custom-call(f32[2,2,32,32,128]{4,3,2,1,0:T(8,128)S(1)} %cross.7.acc, bf16[2,512,256]{2,1,0:T(8,128)(2,1)S(1)} %copy-done.7), custom_call_target="tpu_custom_call" | custom-call | flops 2000000000 | bytes 3145728 | tf_op jit(solution)/shard_map/invert/pallas_call | solution.py:183
  (58 shorter events, 30.2 us)
Async XLA Ops:
  1.1 25.4 %collective-permute-start = (f32[32,8,512]{2,1,0:T(8,128)S(1)}, f32[32,8,512]{2,1,0:T(8,128)S(1)}, u32[]{:S(2)}, u32[]{:S(2)}) collective-permute-start(f32[32,8,512]{2,1,0:T(8,128)S(1)} %slice.7), channel_id=1, source_target_pairs={{4,0},{8,4},{12,8},{16,12},{20,16},{24,20},{28,24},{5,1},{9,5},{13... | collective-permute-start | bytes 1572872 | tf_op jit(solution)/shard_map/ppermute | solution.py:197
  18.2 1.6 %copy-start = (f32[128,8,512]{2,1,0:T(8,128)S(1)}, f32[128,8,512]{2,1,0:T(8,128)}, u32[]{:S(2)}) copy-start(f32[128,8,512]{2,1,0:T(8,128)} %param.12) | copy-start | bytes 6291460
  27.3 55.5 %copy-start.15 = (s32[4]{0:T(128)S(1)}, s32[4]{0:T(128)}, u32[]{:S(2)}) copy-start(s32[4]{0:T(128)} %constant.62.clone) | copy-start | bytes 52
  29.1 16.7 %collective-permute-start.14 = (f32[2,2,8,32,128]{4,3,2,1,0:T(8,128)S(1)}, f32[2,2,8,32,128]{4,3,2,1,0:T(8,128)S(1)}, u32[]{:S(2)}, u32[]{:S(2)}) collective-permute-start(f32[2,2,8,32,128]{4,3,2,1,0:T(8,128)S(1)} %get-tuple-element.8), channel_id=1, source_target_pairs={{1,0},{2,3},{5,4},{6,7},{9,8},{10,11},{13,12},{14,15},{17,16},{18,... | collective-permute-start | bytes 1572872 | tf_op jit(solution)/shard_map/ppermute | solution.py:223
  30.4 18.5 %collective-permute-start.15 = (f32[2,2,8,32,128]{4,3,2,1,0:T(8,128)S(1)}, f32[2,2,8,32,128]{4,3,2,1,0:T(8,128)S(1)}, u32[]{:S(2)}, u32[]{:S(2)}) collective-permute-start(f32[2,2,8,32,128]{4,3,2,1,0:T(8,128)S(1)} %get-tuple-element.9), channel_id=1, source_target_pairs={{0,1},{3,2},{4,5},{7,6},{8,9},{11,10},{12,13},{15,14},{16,17},{19,... | collective-permute-start | bytes 1572872 | tf_op jit(solution)/shard_map/ppermute | solution.py:217
  35.4 21.7 %collective-permute-start.16 = (f32[2,2,8,32,128]{4,3,2,1,0:T(8,128)S(1)}, f32[2,2,8,32,128]{4,3,2,1,0:T(8,128)S(1)}, u32[]{:S(2)}, u32[]{:S(2)}) collective-permute-start(f32[2,2,8,32,128]{4,3,2,1,0:T(8,128)S(1)} %get-tuple-element.10), channel_id=1, source_target_pairs={{1,0},{2,3},{5,4},{6,7},{9,8},{10,11},{13,12},{14,15},{17,16},{18,... | collective-permute-start | bytes 1572872 | tf_op jit(solution)/shard_map/ppermute | solution.py:223
  36.7 22.7 %collective-permute-start.6 = (f32[2,2,8,32,128]{4,3,2,1,0:T(8,128)}, f32[2,2,8,32,128]{4,3,2,1,0:T(8,128)}, u32[]{:S(2)}, u32[]{:S(2)}) collective-permute-start(f32[2,2,8,32,128]{4,3,2,1,0:T(8,128)} %get-tuple-element.11), channel_id=1, source_target_pairs={{0,1},{3,2},{4,5},{7,6},{8,9},{11,10},{12,13},{15,14},{16,17},{19,... | collective-permute-start | bytes 1572872 | tf_op jit(solution)/shard_map/ppermute | solution.py:217
  42.1 28.0 %collective-permute-start.1 = (f32[2,2,8,32,128]{4,3,2,1,0:T(8,128)}, f32[2,2,8,32,128]{4,3,2,1,0:T(8,128)}, u32[]{:S(2)}, u32[]{:S(2)}) collective-permute-start(f32[2,2,8,32,128]{4,3,2,1,0:T(8,128)} %get-tuple-element.6), channel_id=1, source_target_pairs={{0,1},{3,2},{4,5},{7,6},{8,9},{11,10},{12,13},{15,14},{16,17},{19,... | collective-permute-start | bytes 1572872 | tf_op jit(solution)/shard_map/ppermute | solution.py:217
  46.6 34.7 %collective-permute-start.4 = (f32[2,2,8,32,128]{4,3,2,1,0:T(8,128)}, f32[2,2,8,32,128]{4,3,2,1,0:T(8,128)}, u32[]{:S(2)}, u32[]{:S(2)}) collective-permute-start(f32[2,2,8,32,128]{4,3,2,1,0:T(8,128)} %get-tuple-element.7), channel_id=1, source_target_pairs={{0,1},{3,2},{4,5},{7,6},{8,9},{11,10},{12,13},{15,14},{16,17},{19,... | collective-permute-start | bytes 1572872 | tf_op jit(solution)/shard_map/ppermute | solution.py:217
  49.7 33.8 %collective-permute-start.9 = (f32[2,2,8,32,128]{4,3,2,1,0:T(8,128)}, f32[2,2,8,32,128]{4,3,2,1,0:T(8,128)}, u32[]{:S(2)}, u32[]{:S(2)}) collective-permute-start(f32[2,2,8,32,128]{4,3,2,1,0:T(8,128)} %get-tuple-element.6), channel_id=1, source_target_pairs={{1,2},{2,1},{5,6},{6,5},{9,10},{10,9},{13,14},{14,13},{17,18},{18,... | collective-permute-start | bytes 1572872 | tf_op jit(solution)/shard_map/ppermute | solution.py:220
  57.9 26.9 %collective-permute-start.11 = (f32[2,2,8,32,128]{4,3,2,1,0:T(8,128)}, f32[2,2,8,32,128]{4,3,2,1,0:T(8,128)}, u32[]{:S(2)}, u32[]{:S(2)}) collective-permute-start(f32[2,2,8,32,128]{4,3,2,1,0:T(8,128)} %get-tuple-element.7), channel_id=1, source_target_pairs={{1,2},{2,1},{5,6},{6,5},{9,10},{10,9},{13,14},{14,13},{17,18},{18,... | collective-permute-start | bytes 1572872 | tf_op jit(solution)/shard_map/ppermute | solution.py:220
  59.4 30.5 %collective-permute-start.12 = (f32[2,2,8,32,128]{4,3,2,1,0:T(8,128)}, f32[2,2,8,32,128]{4,3,2,1,0:T(8,128)}, u32[]{:S(2)}, u32[]{:S(2)}) collective-permute-start(f32[2,2,8,32,128]{4,3,2,1,0:T(8,128)} %get-tuple-element.11), channel_id=1, source_target_pairs={{1,2},{2,1},{5,6},{6,5},{9,10},{10,9},{13,14},{14,13},{17,18},{18,... | collective-permute-start | bytes 1572872 | tf_op jit(solution)/shard_map/ppermute | solution.py:220
  70.1 20.5 %collective-permute-start.2 = (f32[2,2,8,32,128]{4,3,2,1,0:T(8,128)}, f32[2,2,8,32,128]{4,3,2,1,0:T(8,128)}, u32[]{:S(2)}, u32[]{:S(2)}) collective-permute-start(f32[2,2,8,32,128]{4,3,2,1,0:T(8,128)} %collective-permute-done.1), channel_id=1, source_target_pairs={{1,2},{2,1},{5,6},{6,5},{9,10},{10,9},{13,14},{14,13},{17,18},{18,... | collective-permute-start | bytes 1572872 | tf_op jit(solution)/shard_map/ppermute | solution.py:220
  81.3 10.6 %collective-permute-start.5 = (f32[2,2,8,32,128]{4,3,2,1,0:T(8,128)}, f32[2,2,8,32,128]{4,3,2,1,0:T(8,128)}, u32[]{:S(2)}, u32[]{:S(2)}) collective-permute-start(f32[2,2,8,32,128]{4,3,2,1,0:T(8,128)} %collective-permute-done.4), channel_id=1, source_target_pairs={{1,2},{2,1},{5,6},{6,5},{9,10},{10,9},{13,14},{14,13},{17,18},{18,... | collective-permute-start | bytes 1572872 | tf_op jit(solution)/shard_map/ppermute | solution.py:220
  83.5 21.0 %collective-permute-start.10 = (f32[2,2,8,32,128]{4,3,2,1,0:T(8,128)}, f32[2,2,8,32,128]{4,3,2,1,0:T(8,128)S(1)}, u32[]{:S(2)}, u32[]{:S(2)}) collective-permute-start(f32[2,2,8,32,128]{4,3,2,1,0:T(8,128)} %collective-permute-done.9.refs_5_), channel_id=1, source_target_pairs={{1,0},{2,3},{5,4},{6,7},{9,8},{10,11},{13,12},{14,15},{17,16},{18,... | collective-permute-start | bytes 1572872 | tf_op jit(solution)/shard_map/ppermute | solution.py:223
  84.8 30.9 %collective-permute-start.13 = (f32[2,2,8,32,128]{4,3,2,1,0:T(8,128)}, f32[2,2,8,32,128]{4,3,2,1,0:T(8,128)S(1)}, u32[]{:S(2)}, u32[]{:S(2)}) collective-permute-start(f32[2,2,8,32,128]{4,3,2,1,0:T(8,128)} %collective-permute-done.11.refs_1_), channel_id=1, source_target_pairs={{1,0},{2,3},{5,4},{6,7},{9,8},{10,11},{13,12},{14,15},{17,16},{18,... | collective-permute-start | bytes 1572872 | tf_op jit(solution)/shard_map/ppermute | solution.py:223
  86.1 7.1 %copy-start.2 = (f32[2,2,8,32,128]{4,3,2,1,0:T(8,128)S(1)}, f32[2,2,8,32,128]{4,3,2,1,0:T(8,128)}, u32[]{:S(2)}) copy-start(f32[2,2,8,32,128]{4,3,2,1,0:T(8,128)} %copy-done.1) | copy-start | bytes 1572868
  86.1 7.1 %copy-start.4 = (f32[2,2,8,32,128]{4,3,2,1,0:T(8,128)S(1)}, f32[2,2,8,32,128]{4,3,2,1,0:T(8,128)}, u32[]{:S(2)}) copy-start(f32[2,2,8,32,128]{4,3,2,1,0:T(8,128)} %copy-done.3) | copy-start | bytes 1572868
  86.2 7.1 %copy-start.6 = (f32[2,2,8,32,128]{4,3,2,1,0:T(8,128)S(1)}, f32[2,2,8,32,128]{4,3,2,1,0:T(8,128)}, u32[]{:S(2)}) copy-start(f32[2,2,8,32,128]{4,3,2,1,0:T(8,128)} %copy-done.5) | copy-start | bytes 1572868
  89.9 31.9 %collective-permute-start.7 = (f32[2,2,8,32,128]{4,3,2,1,0:T(8,128)}, f32[2,2,8,32,128]{4,3,2,1,0:T(8,128)S(1)}, u32[]{:S(2)}, u32[]{:S(2)}) collective-permute-start(f32[2,2,8,32,128]{4,3,2,1,0:T(8,128)} %collective-permute-done.6.refs_2_.refs_4_), channel_id=1, source_target_pairs={{1,2},{2,1},{5,6},{6,5},{9,10},{10,9},{13,14},{14,13},{17,18},{18,... | collective-permute-start | bytes 1572872 | tf_op jit(solution)/shard_map/ppermute | solution.py:220
  90.6 36.4 %collective-permute-start.3 = (f32[2,2,8,32,128]{4,3,2,1,0:T(8,128)}, f32[2,2,8,32,128]{4,3,2,1,0:T(8,128)S(1)}, u32[]{:S(2)}, u32[]{:S(2)}) collective-permute-start(f32[2,2,8,32,128]{4,3,2,1,0:T(8,128)} %collective-permute-done.2.refs_5_), channel_id=1, source_target_pairs={{1,0},{2,3},{5,4},{6,7},{9,8},{10,11},{13,12},{14,15},{17,16},{18,... | collective-permute-start | bytes 1572872 | tf_op jit(solution)/shard_map/ppermute | solution.py:223
  91.9 45.3 %collective-permute-start.8 = (f32[2,2,8,32,128]{4,3,2,1,0:T(8,128)}, f32[2,2,8,32,128]{4,3,2,1,0:T(8,128)S(1)}, u32[]{:S(2)}, u32[]{:S(2)}) collective-permute-start(f32[2,2,8,32,128]{4,3,2,1,0:T(8,128)} %collective-permute-done.5.refs_1_), channel_id=1, source_target_pairs={{1,0},{2,3},{5,4},{6,7},{9,8},{10,11},{13,12},{14,15},{17,16},{18,... | collective-permute-start | bytes 1572872 | tf_op jit(solution)/shard_map/ppermute | solution.py:223
  97.9 1.4 copy-start.14
  121.9 20.0 %copy-start.7 = (bf16[2,512,256]{2,1,0:T(8,128)(2,1)S(1)}, bf16[2,512,256]{2,1,0:T(8,128)(2,1)}, u32[]{:S(2)}) copy-start(bf16[2,512,256]{2,1,0:T(8,128)(2,1)} %constant.63.clone.table) | copy-start | bytes 1572868
  (9 other events, 8.7 us)

commit v2 on v1

v2 whole, which is shorter than its diff:
```python
import functools

import jax
import jax.numpy as jnp
import ml_dtypes
import numpy as np
from jax import lax
from jax.experimental import pallas as pl
from jax.experimental.pallas import tpu as pltpu
from jax.sharding import PartitionSpec as P

NEAR = 32
LAGS = 256
HALF = 8
LANES = 128
VMEM_LIMIT = 48 << 20


def split_table(table):
    high = table.astype(ml_dtypes.bfloat16)
    low = (table - high.astype(np.float64)).astype(ml_dtypes.bfloat16)
    return np.stack([high, low])


def make_tables(win, lags, segs):
    bins = win // 2
    samples = np.arange(win)
    hann = 0.5 - 0.5 * np.cos(2.0 * np.pi * samples / win)
    even, odd = np.arange(2, bins + 1, 2), np.arange(1, bins, 2)
    order = np.concatenate([even, odd])

    def forward(picked):
        phases = 2.0 * np.pi * ((samples[: win // 2, None] * picked[None, :]) % win) / win
        return split_table(np.concatenate([np.cos(phases), -np.sin(phases)], axis=1))

    near = np.abs(order[:, None] - order[None, :]) <= HALF
    band = near / (2.0 * HALF + 1.0) + 0.1 / bins
    lag = np.arange(lags) - lags // 2
    phases = 2.0 * np.pi * ((order[:, None] * lag[None, :]) % win) / win
    halves = np.split(phases, 2)
    inverse = np.stack([split_table(np.concatenate([np.cos(h), -np.sin(h)], axis=0) / segs) for h in halves])
    return {
        "hann": hann.astype(np.float32)[None, :],
        "even": forward(even),
        "odd": forward(odd),
        "band": split_table(band),
        "inverse": inverse,
    }


def dot_split(value, table):
    high = value.astype(jnp.bfloat16)
    low = (value - high.astype(jnp.float32)).astype(jnp.bfloat16)
    dot = functools.partial(jnp.dot, preferred_element_type=jnp.float32)
    return dot(high, table[0]) + (dot(high, table[1]) + dot(low, table[0]))


def whiten_kernel(x_ref, hann, even, odd, band, w_ref, stage):
    channels, segs, win = x_ref.shape
    parts = win // LANES
    for part in range(parts):
        lanes = slice(LANES * part, LANES * part + LANES)
        stage[part] = x_ref[:, :, lanes].reshape(channels * segs, LANES)
    pieces = []
    for s in range(segs):
        pieces.append([
            stage[part, pl.ds(s, channels, stride=segs), :] * hann[:, LANES * part : LANES * part + LANES]
            for part in range(parts)
        ])
    quarter = [jnp.concatenate([piece[part] for piece in pieces], axis=0) for part in range(parts)]
    both = jnp.concatenate([quarter[0] + quarter[2], quarter[1] + quarter[3]], axis=1)
    between = jnp.concatenate([quarter[0] - quarter[2], quarter[1] - quarter[3]], axis=1)
    spectra = (dot_split(both, even), dot_split(between, odd))
    energy = jnp.concatenate(
        [sp[:, :LANES] * sp[:, :LANES] + sp[:, LANES:] * sp[:, LANES:] for sp in spectra], axis=1
    )
    scale = lax.rsqrt(dot_split(energy, band) + 1e-06)
    for half, sp in enumerate(spectra):
        own = scale[:, LANES * half : LANES * half + LANES]
        real, imag = sp[:, :LANES] * own, sp[:, LANES:] * own
        for s in range(segs):
            rows = slice(channels * s, channels * s + channels)
            w_ref[half, 0, s] = real[rows]
            w_ref[half, 1, s] = imag[rows]


def whiten(x, tables):
    blocks, near, segs, win = x.shape
    whole = lambda a: pl.BlockSpec(a.shape, lambda i: (0,) * a.ndim)
    names = ("hann", "even", "odd", "band")
    consts = [jnp.asarray(tables[name]) for name in names]
    return pl.pallas_call(
        whiten_kernel,
        grid=(blocks,),
        in_specs=[pl.BlockSpec((None, near, segs, win), lambda i: (i, 0, 0, 0))] + [whole(c) for c in consts],
        out_specs=pl.BlockSpec((None, 2, 2, segs, near, LANES), lambda i: (i, 0, 0, 0, 0, 0)),
        out_shape=jax.ShapeDtypeStruct((blocks, 2, 2, segs, near, LANES), jnp.float32),
        scratch_shapes=[pltpu.VMEM((win // LANES, near * segs, LANES), jnp.float32)],
        compiler_params=pltpu.CompilerParams(vmem_limit_bytes=VMEM_LIMIT),
        cost_estimate=pl.CostEstimate(flops=blocks * 500_000_000, bytes_accessed=blocks << 20, transcendentals=0),
        name="whiten",
    )(x, *consts)


def groups_of(near, which):
    tiles = near // 8
    inside = [(tile, offset) for tile in range(tiles) for offset in range(1, near - 8 * tile - 7)]
    across = [(tile, offset) for tile in range(tiles) for offset in range(near - 8 * tile - 7, near + 1)]
    return {"inside": inside, "across": across, "all": inside + across}[which]


def products(pair, groups, store):
    segs = pair.shape[1]
    tile = None
    for index, (group, offset) in enumerate(groups):
        if group != tile:
            tile = group
            rows = pl.ds(8 * group, 8)
            real = [pair[0, s, rows, :] for s in range(segs)]
            imag = [pair[1, s, rows, :] for s in range(segs)]
            added = [real[s] + imag[s] for s in range(segs)]
        ahead = pl.ds(8 * group + offset, 8)
        rr = ii = mixed = None
        for s in range(segs):
            other_re, other_im = pair[0, s, ahead, :], pair[1, s, ahead, :]
            terms = (real[s] * other_re, imag[s] * other_im, added[s] * (other_re - other_im))
            if rr is None:
                rr, ii, mixed = terms
            else:
                rr, ii, mixed = rr + terms[0], ii + terms[1], mixed + terms[2]
        store(index, rr + ii, mixed - rr + ii)


def lag_kernel(near, which, count, has_prior, pick_ref, *refs):
    half = pl.program_id(1)
    sides = 1 if which == "inside" else 2
    cands, refs = refs[: sides * count], refs[sides * count :]
    table, refs = refs[0], refs[1:]
    sizes = {"inside": ("inside",), "across": ("across",), "all": ("inside", "across")}[which]
    priors, refs = (refs[: len(sizes)], refs[len(sizes) :]) if has_prior else (None, refs)
    outs, (pair, lhs) = refs[: len(sizes)], refs[len(sizes) :]
    segs = cands[0].shape[1]
    for side in range(sides):
        for part in range(2):
            for s in range(segs):
                value = cands[side * count][part, s]
                for other in range(1, count):
                    value = jnp.where(pick_ref[0] == other, cands[side * count + other][part, s], value)
                pair[part, s, pl.ds(side * near, near), :] = value

    def store(index, real, imag):
        lhs[pl.ds(8 * index, 8), :LANES] = real
        lhs[pl.ds(8 * index, 8), LANES:] = imag

    products(pair, groups_of(near, which), store)
    start = 0
    for index, out in enumerate(outs):
        count_rows = out.shape[0] * 8
        lagged = dot_split(lhs[pl.ds(start, count_rows), :], table).reshape(out.shape)
        start += count_rows

        @pl.when(half == 0)
        def _():
            out[...] = lagged + priors[index][...] if has_prior else lagged

        @pl.when(half != 0)
        def _():
            out[...] += lagged


def lag_sums(which, pick, firsts, seconds, tables, base=None, prior=None, blocks=1, total=1, grown=None):
    count = len(firsts)
    halves, parts, segs, near, lanes = firsts[0].shape[-5:]
    if base is None:
        spec = pl.BlockSpec((None, parts, segs, near, lanes), lambda b, h, p: (h, 0, 0, 0, 0))
        specs = [spec] * count
        specs2 = specs
    else:
        specs = [pl.BlockSpec((None, None, parts, segs, near, lanes), lambda b, h, p: (b, h, 0, 0, 0, 0))]
        specs2 = [pl.BlockSpec((None, None, parts, segs, near, lanes), lambda b, h, p: (b + 1, h, 0, 0, 0, 0))]
    operands = list(firsts)
    in_specs = list(specs)
    sides = 1
    if which != "inside":
        operands += list(seconds)
        in_specs += list(specs2)
        sides = 2
    table = tables["inverse"]
    operands.append(jnp.asarray(table))
    in_specs.append(pl.BlockSpec((None,) + table.shape[1:], lambda b, h, p: (h, 0, 0, 0)))
    kinds = {"inside": ("inside",), "across": ("across",), "all": ("inside", "across")}[which]
    shapes = [(len(groups_of(near, kind)), 8, LAGS) for kind in kinds]
    aliases = {}
    if prior is not None:
        for value, shape in zip(prior, shapes):
            operands.append(value)
            in_specs.append(pl.BlockSpec((None,) + shape, lambda b, h, p: (p[1], 0, 0, 0)))
    kernel = functools.partial(lag_kernel, near, which, count, prior is not None)
    first_block = 0
    if grown is not None:
        first_block = total - blocks
        inner = kernel

        def kernel(pick_ref, *refs):
            seen = sides * count + 1
            return inner(pick_ref, *refs[:seen], *refs[seen + len(grown) :])

        for index, value in enumerate(grown):
            aliases[1 + len(operands)] = index
            operands.append(value)
            in_specs.append(pl.BlockSpec(memory_space=pl.ANY))
    rows = 8 * sum(shape[0] for shape in shapes)
    work = blocks * rows // 8
    return pl.pallas_call(
        kernel,
        grid_spec=pltpu.PrefetchScalarGridSpec(
            num_scalar_prefetch=1,
            grid=(blocks, halves),
            in_specs=in_specs,
            out_specs=[
                pl.BlockSpec((None,) + shape, lambda b, h, p: (b + first_block, 0, 0, 0)) for shape in shapes
            ],
            scratch_shapes=[
                pltpu.VMEM((parts, segs, sides * near, lanes), jnp.float32),
                pltpu.VMEM((rows, 2 * lanes), jnp.float32),
            ],
        ),
        out_shape=[jax.ShapeDtypeStruct((total,) + shape, jnp.float32) for shape in shapes],
        input_output_aliases=aliases,
        compiler_params=pltpu.CompilerParams(vmem_limit_bytes=VMEM_LIMIT),
        cost_estimate=pl.CostEstimate(flops=work * 20_000_000, bytes_accessed=1 << 20, transcendentals=0),
        name="lag_" + which,
    )(pick, *operands)


def place_kernel(near, count, *refs):
    terms, out_ref, stage = refs[: 2 * count], refs[2 * count], refs[2 * count + 1]
    for kind in range(2):
        for index, (tile, offset) in enumerate(groups_of(near, ("inside", "across")[kind])):
            value = terms[kind * count][index]
            for other in range(1, count):
                value = value + terms[kind * count + other][index]
            for part in range(LAGS // LANES):
                stage[part, pl.ds(8 * tile * near + offset - 1, 8, stride=near), :] = value[
                    :, LANES * part : LANES * part + LANES
                ]
    for part in range(LAGS // LANES):
        out_ref[:, :, LANES * part : LANES * part + LANES] = stage[part].reshape(near, near, LANES)


def place(near, inside, across):
    vmem = pl.BlockSpec(memory_space=pltpu.VMEM)
    count = len(inside)
    return pl.pallas_call(
        functools.partial(place_kernel, near, count),
        in_specs=[vmem] * (2 * count),
        out_specs=vmem,
        out_shape=jax.ShapeDtypeStruct((near, near, LAGS), jnp.float32),
        scratch_shapes=[pltpu.VMEM((LAGS // LANES, near * near, LANES), jnp.float32)],
        compiler_params=pltpu.CompilerParams(vmem_limit_bytes=VMEM_LIMIT),
        cost_estimate=pl.CostEstimate(flops=1_000_000_000, bytes_accessed=4 << 20, transcendentals=0),
        name="place",
    )(*inside, *across)


def shifted(value, steps):
    count = lax.axis_size("fibre")
    return lax.ppermute(value, "fibre", [(source, source + steps) for source in range(max(0, -steps), count)])


def line_of_four(traces):
    channels, segs, win = traces.shape
    tables = make_tables(win, LAGS, segs * 4)
    z = lax.axis_index("tm")
    left = z < 2
    blocks = traces.reshape(4, NEAR, segs, win)
    halo = shifted(blocks[0], -1)
    own = whiten(blocks, tables)
    ahead = whiten(halo[None], tables)

    def outer(value):
        return lax.ppermute(value, "tm", [(0, 1), (3, 2)])

    def middle(value):
        return lax.ppermute(value, "tm", [(1, 2), (2, 1)])

    def inner(value):
        return lax.ppermute(value, "tm", [(1, 0), (2, 3)])

    e1 = outer(jnp.where(left, own[3], own[0]))
    e2 = outer(jnp.where(left, ahead[0], own[1]))
    e3 = outer(own[2])
    e4 = outer(jnp.where(left, own[1], own[3]))

    number = lambda value: jnp.asarray(value, jnp.int32)
    scalars = lambda role, at: jnp.stack([number(role), number(at)])
    role = jnp.where(z == 1, 0, 1)
    none = jnp.zeros((2,), jnp.int32)
    mine = lag_sums("all", none, [own], [own], tables, base=0, blocks=3, total=4)
    mine = lag_sums("all", none, [own[3]], [ahead[0]], tables, blocks=1, total=4, grown=mine)
    far, mid, opposite = jnp.where(left, 3, 0), jnp.where(left, 2, 1), jnp.where(left, 0, 3)

    (m1,) = lag_sums("inside", scalars(0, far), [e1], None, tables, prior=mine[:1])
    m1 = middle(m1)
    (m2,) = lag_sums("across", scalars(0, far), [e1], [e2], tables, prior=mine[1:])
    m2 = middle(m2)
    (m3,) = lag_sums("inside", scalars(role, mid), [e3, e2], None, tables, prior=mine[:1])
    m3 = middle(m3)
    (m4,) = lag_sums("across", scalars(role, mid), [e3, e2], [e1, e3], tables, prior=mine[1:])
    m4 = middle(m4)
    near_in, near_out = lag_sums("all", scalars(role, z), [e4, e3], [e3, e4], tables, prior=mine)
    at = lambda value: lax.dynamic_index_in_dim(value, opposite, 0, keepdims=True)
    i1 = inner(m1 + at(mine[0]))
    i2 = inner(m2 + at(mine[1]))
    return place(NEAR, [v[0] for v in (near_in, i1, m3)], [v[0] for v in (near_out, i2, m4)])


def any_line(traces):
    channels, segs, win = traces.shape
    axis = lax.axis_size("tm")
    tables = make_tables(win, LAGS, segs * axis)
    blocks = traces.reshape(channels // NEAR, NEAR, segs, win)
    halo = shifted(blocks[0], -1)
    spectra = whiten(jnp.concatenate([blocks, halo[None]], axis=0), tables)
    count = channels // NEAR
    none = jnp.zeros((2,), jnp.int32)
    inside, across = lag_sums("all", none, [spectra], [spectra], tables, base=0, blocks=count, total=count)
    lagged = jnp.concatenate([place(NEAR, [inside[b]], [across[b]]) for b in range(count)], axis=0)
    return lax.psum_scatter(lagged, "tm", scatter_dimension=0, tiled=True)


def shards(traces):
    if lax.axis_size("tm") == 4 and traces.shape[0] == 4 * NEAR:
        return line_of_four(traces)
    return any_line(traces)


def solution(mesh):
    in_specs = (P("fibre", "tm", None),)
    out_specs = P(("fibre", "tm"), None, None)
    return jax.shard_map(shards, mesh=mesh, in_specs=in_specs, out_specs=out_specs, check_vma=False)
```

time: 145 us -> 112 us (0.77)
  waiting for transfers between devices: 58.5 us -> 15 us
  Pallas kernels: 23 us -> 49.9 us
  starting transfers between devices: 31.7 us -> 19.1 us
  between operations: 9.68 us -> 0.28 us
  local copies, waits for them, and re-layouts: 19.7 us -> 23.8 us
    pallas_call x5 -> x8, Pallas kernels: 19 us -> 45.8 us  [the longest x7 43.9 us: lag_sums(): pl.pallas_call(kernel, grid_spec=pltpu.PrefetchScalarGridSpec(num_scalar_...]
    ppermute x6 -> x2, waiting for transfers between devices: 39.5 us -> 14.9 us  [inner(): return lax.ppermute(value, 'tm', [(1, 0), (2, 3)])]
    ppermute x4, waiting for transfers between devices: 19 us -> 0.01 us  [outer(): return lax.ppermute(value, 'tm', [(0, 1), (3, 2)])]
    unnamed x32 -> x48, local copies, waits for them, and re-layouts: 11.6 us -> 21 us
    dynamic_slice x6 -> x0, local copies, waits for them, and re-layouts: 6.97 us -> none  [the longest x5 6.38 us: choose(): return block(jnp.asarray(picks, jnp.int32)[z])]
    ppermute x6 -> x2, starting transfers between devices: 7.74 us -> 2.76 us  [inner(): return lax.ppermute(value, 'tm', [(1, 0), (2, 3)])]
    ppermute x6 -> x4, starting transfers between devices: 7.97 us -> 3.86 us  [middle(): return lax.ppermute(value, 'tm', [(1, 2), (2, 1)])]
    ppermute x4, starting transfers between devices: 14.7 us -> 11.2 us  [outer(): return lax.ppermute(value, 'tm', [(0, 1), (3, 2)])]
  transfers between devices with their start and end apart: 17 -> 11, of which waited for: 8 -> 1; matrix products, arithmetic and copies ran while one was open for 5% -> 3% of each run, Pallas kernels for 10% -> 43%
where the time goes in v2:
time: 112 us; the launch traced here: 111 us
  Pallas kernels  49.9 us (45%)
  local copies, waits for them, and re-layouts  23.8 us (21%)
  starting transfers between devices  19.1 us (17%)
  waiting for transfers between devices  15 us (13%)
  other arithmetic  2.7 us (2%)
    pallas_call x7, Pallas kernels, lag_sums(): pl.pallas_call(kernel, grid_spec=pltpu.PrefetchScalarGridSpec(num_scalar_...  43.9 us
    unnamed x48, local copies, waits for them, and re-layouts  21 us
    ppermute x2, waiting for transfers between devices, inner(): return lax.ppermute(value, 'tm', [(1, 0), (2, 3)])  14.9 us
    ppermute x4, starting transfers between devices, outer(): return lax.ppermute(value, 'tm', [(0, 1), (3, 2)])  11.2 us
    pallas_call x2, Pallas kernels, whiten(): pl.pallas_call(whiten_kernel, grid=(blocks,), in_specs=[pl.BlockSpec((Non...  4.02 us
    ppermute x4, starting transfers between devices, middle(): return lax.ppermute(value, 'tm', [(1, 2), (2, 1)])  3.86 us
    ppermute x2, starting transfers between devices, inner(): return lax.ppermute(value, 'tm', [(1, 0), (2, 3)])  2.76 us
  transfers between devices with their start and end apart: 11, of which 1 were waited for; matrix products, arithmetic and copies ran while one was open for 3% of the time, Pallas kernels for 43%

profile of v2, /device:TPU:0, one launch (start us, length us, event | category | flops | bytes accessed | tf_op | source)
XLA Modules:
  0.0 110.7 jit_solution(10597452394275413003)
XLA Ops:
  0.0 1.9 %slice.22 = f32[32,8,512]{2,1,0:T(8,128)} slice(f32[128,8,512]{2,1,0:T(8,128)} %param.6), slice={[0:32], [0:8], [0:512]} | slice | bytes 1048576 | tf_op jit(solution)/shard_map/slice | solution.py:277
  3.2 1.6 %copy-done.4 = f32[128,8,512]{2,1,0:T(8,128)S(1)} copy-done((f32[128,8,512]{2,1,0:T(8,128)S(1)}, f32[128,8,512]{2,1,0:T(8,128)}, u32[]{:S(2)}) %copy-start.4) | copy-done | bytes 2097176
  8.3 3.2 %whiten.2.refs_0_.refs_1_ = f32[4,2,2,8,32,128]{5,4,3,2,1,0:T(8,128)S(1)} custom-call(f32[4,32,8,512]{3,2,1,0:T(8,128)S(1)} %bitcast.39, f32[1,512]{1,0:T(1,128)S(1)} %copy-done.22, bf16[2,256,256]{2,1,0:T(8,128)(2,1)S(1)} %copy-done.16, bf16[2,256,256]{2,1,0:T(8,128)(2,1)S(1)} %copy-done.18, bf16[2,256,256]{2,1,0:T(8,128)(2,1)S(1)} %copy-done.20), custom_call_target="tpu_custom_call" | custom-call | flops 2000000000 | bytes 4194304 | tf_op jit(solution)/shard_map/whiten/pallas_call | solution.py:92
  12.4 5.8 %collective-permute-start.1 = (f32[2,2,8,32,128]{4,3,2,1,0:T(8,128)}, f32[2,2,8,32,128]{4,3,2,1,0:T(8,128)}, u32[]{:S(2)}, u32[]{:S(2)}) collective-permute-start(f32[2,2,8,32,128]{4,3,2,1,0:T(8,128)} %get-tuple-element.21), channel_id=1, source_target_pairs={{0,1},{3,2},{4,5},{7,6},{8,9},{11,10},{12,13},{15,14},{16,17},{19,... | collective-permute-start | bytes 1572872 | tf_op jit(solution)/shard_map/ppermute | solution.py:282
  24.0 2.1 %collective-permute-start.3 = (f32[2,2,8,32,128]{4,3,2,1,0:T(8,128)}, f32[2,2,8,32,128]{4,3,2,1,0:T(8,128)}, u32[]{:S(2)}, u32[]{:S(2)}) collective-permute-start(f32[2,2,8,32,128]{4,3,2,1,0:T(8,128)} %get-tuple-element.18), channel_id=1, source_target_pairs={{0,1},{3,2},{4,5},{7,6},{8,9},{11,10},{12,13},{15,14},{16,17},{19,... | collective-permute-start | bytes 1572872 | tf_op jit(solution)/shard_map/ppermute | solution.py:282
  26.1 2.1 %collective-permute-start.6 = (f32[2,2,8,32,128]{4,3,2,1,0:T(8,128)}, f32[2,2,8,32,128]{4,3,2,1,0:T(8,128)}, u32[]{:S(2)}, u32[]{:S(2)}) collective-permute-start(f32[2,2,8,32,128]{4,3,2,1,0:T(8,128)} %get-tuple-element.17), channel_id=1, source_target_pairs={{0,1},{3,2},{4,5},{7,6},{8,9},{11,10},{12,13},{15,14},{16,17},{19,... | collective-permute-start | bytes 1572872 | tf_op jit(solution)/shard_map/ppermute | solution.py:282
  28.2 17.0 %lag_all.3 = (f32[4,48,8,256]{3,2,1,0:T(8,128)S(1)}, f32[4,80,8,256]{3,2,1,0:T(8,128)}) custom-call(s32[2]{0:T(128)S(1)} %broadcast_1_pick_ref.2.pick_ref, f32[4,2,2,8,32,128]{5,4,3,2,1,0:T(8,128)S(1)} %whiten.2.refs_0_.refs_1_, f32[4,2,2,8,32,128]{5,4,3,2,1,0:T(8,128)S(1)} %whiten.2.refs_0_.refs_1_, bf16[2,2,256,256]{3,2,1,0:T(8,128)(2,1)S(1)} %copy-done.12), custom_call_target="tpu_custom_call" | custom-call | flops 7680000000 | bytes 1048576 | tf_op jit(solution)/shard_map/lag_all/pallas_call | solution.py:214
  46.4 1.7 %copy-done = f32[4,80,8,256]{3,2,1,0:T(8,128)S(1)} copy-done((f32[4,80,8,256]{3,2,1,0:T(8,128)S(1)}, f32[4,80,8,256]{3,2,1,0:T(8,128)}, u32[]{:S(2)}) %copy-start) | copy-done | bytes 2621464
  48.1 1.4 %copy-done.6 = f32[4,48,8,256]{3,2,1,0:T(8,128)S(1)} copy-done((f32[4,48,8,256]{3,2,1,0:T(8,128)S(1)}, f32[4,48,8,256]{3,2,1,0:T(8,128)}, u32[]{:S(2)}) %copy-start.6) | copy-done | bytes 1572888
  50.5 5.7 %lag_all.4 = (f32[4,48,8,256]{3,2,1,0:T(8,128)S(1)}, f32[4,80,8,256]{3,2,1,0:T(8,128)S(1)}) custom-call(s32[2]{0:T(128)S(1)} %broadcast_1_pick_ref.2.pick_ref, f32[2,2,8,32,128]{4,3,2,1,0:T(8,128)S(1)} %get-tuple-element.20.refs_0_, f32[2,2,8,32,128]{4,3,2,1,0:T(8,128)S(1)} %bitcast.35, ...), custom_call_target="tpu_custom_call", output_to_operand_aliasing={{0}: (4, {}), {1}: (5, {})} | custom-call | flops 2560000000 | bytes 1048576 | tf_op jit(solution)/shard_map/lag_all/pallas_call | solution.py:214
  56.3 1.5 %copy-done.1 = f32[4,80,8,256]{3,2,1,0:T(8,128)} copy-done((f32[4,80,8,256]{3,2,1,0:T(8,128)}, f32[4,80,8,256]{3,2,1,0:T(8,128)S(1)}, u32[]{:S(2)}) %copy-start.1) | copy-done | bytes 2621464
  58.9 1.7 %copy-done.2 = f32[4,80,8,256]{3,2,1,0:T(8,128)S(1)} copy-done((f32[4,80,8,256]{3,2,1,0:T(8,128)S(1)}, f32[4,80,8,256]{3,2,1,0:T(8,128)}, u32[]{:S(2)}) %copy-start.2) | copy-done | bytes 2621464
  60.7 3.9 %lag_across.2 = f32[1,80,8,256]{3,2,1,0:T(8,128)S(1)} custom-call(s32[2]{0:T(128)S(1)} %pad_add_fusion.1.pick_ref, f32[2,2,8,32,128]{4,3,2,1,0:T(8,128)} %collective-permute-done.3.refs_0_.refs_2_, f32[2,2,8,32,128]{4,3,2,1,0:T(8,128)} %collective-permute-done.6.refs_1_, bf16[2,2,256,256]{3,2,1,0:T(8,128)(2,1)S(1)} %copy-done.13, f32[4,80,8,256]{3,2,1,0:T(8,128)S(1)} %copy-done.2), custom_call_target="tpu_custom_call" | custom-call | flops 1600000000 | bytes 1048576 | tf_op jit(solution)/shard_map/lag_across/pallas_call | solution.py:214
  64.6 1.7 %collective-permute-start.8 = (f32[1,80,8,256]{3,2,1,0:T(8,128)S(1)}, f32[1,80,8,256]{3,2,1,0:T(8,128)}, u32[]{:S(2)}, u32[]{:S(2)}) collective-permute-start(f32[1,80,8,256]{3,2,1,0:T(8,128)S(1)} %lag_across.2), channel_id=1, source_target_pairs={{1,2},{2,1},{5,6},{6,5},{9,10},{10,9},{13,14},{14,13},{17,18},{18,... | collective-permute-start | bytes 1966088 | tf_op jit(solution)/shard_map/ppermute | solution.py:285
  66.3 1.3 %collective-permute-start = (f32[2,2,8,32,128]{4,3,2,1,0:T(8,128)}, f32[2,2,8,32,128]{4,3,2,1,0:T(8,128)S(1)}, u32[]{:S(2)}, u32[]{:S(2)}) collective-permute-start(f32[2,2,8,32,128]{4,3,2,1,0:T(8,128)} %get-tuple-element.19), channel_id=1, source_target_pairs={{0,1},{3,2},{4,5},{7,6},{8,9},{11,10},{12,13},{15,14},{16,17},{19,... | collective-permute-start | bytes 1572872 | tf_op jit(solution)/shard_map/ppermute | solution.py:282
  67.7 1.4 %copy-done.8 = f32[4,48,8,256]{3,2,1,0:T(8,128)S(1)} copy-done((f32[4,48,8,256]{3,2,1,0:T(8,128)S(1)}, f32[4,48,8,256]{3,2,1,0:T(8,128)}, u32[]{:S(2)}) %copy-start.8) | copy-done | bytes 1572888
  70.1 3.1 %lag_inside.2 = f32[1,48,8,256]{3,2,1,0:T(8,128)S(1)} custom-call(s32[2]{0:T(128)S(1)} %pad_add_fusion.1.pick_ref, f32[2,2,8,32,128]{4,3,2,1,0:T(8,128)} %collective-permute-done.3.refs_0_.refs_2_, bf16[2,2,256,256]{3,2,1,0:T(8,128)(2,1)S(1)} %copy-done.14, f32[4,48,8,256]{3,2,1,0:T(8,128)S(1)} %copy-done.8), custom_call_target="tpu_custom_call" | custom-call | flops 960000000 | bytes 1048576 | tf_op jit(solution)/shard_map/lag_inside/pallas_call | solution.py:214
  74.1 4.4 %lag_across.3 = f32[1,80,8,256]{3,2,1,0:T(8,128)S(1)} custom-call(s32[2]{0:T(128)S(1)} %pad_add_fusion.2.pick_ref, f32[2,2,8,32,128]{4,3,2,1,0:T(8,128)} %collective-permute-done.1.refs_1_.refs_2_.refs_0_.refs_3_, f32[2,2,8,32,128]{4,3,2,1,0:T(8,128)} %collective-permute-done.6.refs_1_, f32[2,2,8,32,128]{4,3,2,1,0:T(8,128)} %collective-permute-done.3.refs_0_.refs_2_, ...), custom_call_target="tpu_custom_call" | custom-call | flops 1600000000 | bytes 1048576 | tf_op jit(solution)/shard_map/lag_across/pallas_call | solution.py:214
  80.4 1.3 %collective-permute-start.9 = (f32[1,80,8,256]{3,2,1,0:T(8,128)S(1)}, f32[1,80,8,256]{3,2,1,0:T(8,128)S(1)}, u32[]{:S(2)}, u32[]{:S(2)}) collective-permute-start(f32[1,80,8,256]{3,2,1,0:T(8,128)S(1)} %dynamic-slice_add_fusion), channel_id=1, source_target_pairs={{1,0},{2,3},{5,4},{6,7},{9,8},{10,11},{13,12},{14,15},{17,16},{18,... | collective-permute-start | bytes 1966088 | tf_op jit(solution)/shard_map/ppermute | solution.py:288
  81.7 3.2 %lag_inside.3 = f32[1,48,8,256]{3,2,1,0:T(8,128)S(1)} custom-call(s32[2]{0:T(128)S(1)} %pad_add_fusion.2.pick_ref, f32[2,2,8,32,128]{4,3,2,1,0:T(8,128)} %collective-permute-done.1.refs_1_.refs_2_.refs_0_.refs_3_, f32[2,2,8,32,128]{4,3,2,1,0:T(8,128)} %collective-permute-done.6.refs_1_, bf16[2,2,256,256]{3,2,1,0:T(8,128)(2,1)S(1)} %copy-done.15, ...), custom_call_target="tpu_custom_call" | custom-call | flops 960000000 | bytes 1048576 | tf_op jit(solution)/shard_map/lag_inside/pallas_call | solution.py:214
  85.6 1.5 %collective-permute-start.5 = (f32[1,48,8,256]{3,2,1,0:T(8,128)S(1)}, f32[1,48,8,256]{3,2,1,0:T(8,128)S(1)}, u32[]{:S(2)}, u32[]{:S(2)}) collective-permute-start(f32[1,48,8,256]{3,2,1,0:T(8,128)S(1)} %dynamic-slice_add_fusion.1), channel_id=1, source_target_pairs={{1,0},{2,3},{5,4},{6,7},{9,8},{10,11},{13,12},{14,15},{17,16},{18,... | collective-permute-start | bytes 1179656 | tf_op jit(solution)/shard_map/ppermute | solution.py:288
  87.2 6.6 %lag_all.5 = (f32[1,48,8,256]{3,2,1,0:T(8,128)S(1)}, f32[1,80,8,256]{3,2,1,0:T(8,128)S(1)}) custom-call(s32[2]{0:T(128)S(1)} %pad_add_fusion.pick_ref, f32[2,2,8,32,128]{4,3,2,1,0:T(8,128)S(1)} %collective-permute-done.refs_0_.refs_3_, f32[2,2,8,32,128]{4,3,2,1,0:T(8,128)} %collective-permute-done.1.refs_1_.refs_2_.refs_0_.refs_3_, ...), custom_call_target="tpu_custom_call" | custom-call | flops 2560000000 | bytes 1048576 | tf_op jit(solution)/shard_map/lag_all/pallas_call | solution.py:214
  93.9 14.9 %collective-permute-done.5 = f32[1,48,8,256]{3,2,1,0:T(8,128)S(1)} collective-permute-done((f32[1,48,8,256]{3,2,1,0:T(8,128)S(1)}, f32[1,48,8,256]{3,2,1,0:T(8,128)S(1)}, u32[]{:S(2)}, u32[]{:S(2)}) %collective-permute-start.5) | collective-permute-done | bytes 393248 | tf_op jit(solution)/shard_map/ppermute | solution.py:288
  108.8 1.9 %place.1 = f32[32,32,256]{2,1,0:T(8,128)} custom-call(f32[48,8,256]{2,1,0:T(8,128)S(1)} %bitcast.38, f32[48,8,256]{2,1,0:T(8,128)S(1)} %bitcast.37, f32[48,8,256]{2,1,0:T(8,128)S(1)} %bitcast.36, f32[80,8,256]{2,1,0:T(8,128)S(1)} %bitcast.34, f32[80,8,256]{2,1,0:T(8,128)S(1)} %bitcast.33, f32[80,8,256]{2,1,0:T(8,128)S(1)} %bitcast.32), custom_call_target="tpu_custom_call" | custom-call | flops 1000000000 | bytes 4194304 | tf_op jit(solution)/shard_map/place/pallas_call | solution.py:254
  (65 shorter events, 19.6 us)
Async XLA Ops:
  1.9 16.3 %collective-permute-start.2 = (f32[32,8,512]{2,1,0:T(8,128)}, f32[32,8,512]{2,1,0:T(8,128)S(1)}, u32[]{:S(2)}, u32[]{:S(2)}) collective-permute-start(f32[32,8,512]{2,1,0:T(8,128)} %slice.22), channel_id=1, source_target_pairs={{4,0},{8,4},{12,8},{16,12},{20,16},{24,20},{28,24},{5,1},{9,5},{13... | collective-permute-start | bytes 1572872 | tf_op jit(solution)/shard_map/ppermute | solution.py:268
  3.2 1.6 %copy-start.4 = (f32[128,8,512]{2,1,0:T(8,128)S(1)}, f32[128,8,512]{2,1,0:T(8,128)}, u32[]{:S(2)}) copy-start(f32[128,8,512]{2,1,0:T(8,128)} %param.6) | copy-start | bytes 6291460
  11.5 7.5 %copy-start.17 = (bf16[2,256,256]{2,1,0:T(8,128)(2,1)S(1)}, bf16[2,256,256]{2,1,0:T(8,128)(2,1)}, u32[]{:S(2)}) copy-start(bf16[2,256,256]{2,1,0:T(8,128)(2,1)} %constant.35.clone.even) | copy-start | bytes 786436
  11.5 7.5 %copy-start.23 = (f32[1,512]{1,0:T(1,128)S(1)}, f32[1,512]{1,0:T(1,128)}, u32[]{:S(2)}) copy-start(f32[1,512]{1,0:T(1,128)} %constant.34.clone.hann) | copy-start | bytes 6148
  12.4 61.6 %collective-permute-start.1 = (f32[2,2,8,32,128]{4,3,2,1,0:T(8,128)}, f32[2,2,8,32,128]{4,3,2,1,0:T(8,128)}, u32[]{:S(2)}, u32[]{:S(2)}) collective-permute-start(f32[2,2,8,32,128]{4,3,2,1,0:T(8,128)} %get-tuple-element.21), channel_id=1, source_target_pairs={{0,1},{3,2},{4,5},{7,6},{8,9},{11,10},{12,13},{15,14},{16,17},{19,... | collective-permute-start | bytes 1572872 | tf_op jit(solution)/shard_map/ppermute | solution.py:282
  22.7 5.4 %copy-start.12 = (bf16[2,2,256,256]{3,2,1,0:T(8,128)(2,1)S(1)}, bf16[2,2,256,256]{3,2,1,0:T(8,128)(2,1)}, u32[]{:S(2)}) copy-start(bf16[2,2,256,256]{3,2,1,0:T(8,128)(2,1)} %constant.38.clone.refs_2_.refs_4_.refs_1_) | copy-start | bytes 1572868
  24.0 34.9 %collective-permute-start.3 = (f32[2,2,8,32,128]{4,3,2,1,0:T(8,128)}, f32[2,2,8,32,128]{4,3,2,1,0:T(8,128)}, u32[]{:S(2)}, u32[]{:S(2)}) collective-permute-start(f32[2,2,8,32,128]{4,3,2,1,0:T(8,128)} %get-tuple-element.18), channel_id=1, source_target_pairs={{0,1},{3,2},{4,5},{7,6},{8,9},{11,10},{12,13},{15,14},{16,17},{19,... | collective-permute-start | bytes 1572872 | tf_op jit(solution)/shard_map/ppermute | solution.py:282
  26.1 32.9 %collective-permute-start.6 = (f32[2,2,8,32,128]{4,3,2,1,0:T(8,128)}, f32[2,2,8,32,128]{4,3,2,1,0:T(8,128)}, u32[]{:S(2)}, u32[]{:S(2)}) collective-permute-start(f32[2,2,8,32,128]{4,3,2,1,0:T(8,128)} %get-tuple-element.17), channel_id=1, source_target_pairs={{0,1},{3,2},{4,5},{7,6},{8,9},{11,10},{12,13},{15,14},{16,17},{19,... | collective-permute-start | bytes 1572872 | tf_op jit(solution)/shard_map/ppermute | solution.py:282
  45.1 1.1 %copy-start.5 = (f32[4,48,8,256]{3,2,1,0:T(8,128)}, f32[4,48,8,256]{3,2,1,0:T(8,128)S(1)}, u32[]{:S(2)}) copy-start(f32[4,48,8,256]{3,2,1,0:T(8,128)S(1)} %get-tuple-element.11.refs_3_) | copy-start | bytes 4718596
  46.4 1.7 %copy-start = (f32[4,80,8,256]{3,2,1,0:T(8,128)S(1)}, f32[4,80,8,256]{3,2,1,0:T(8,128)}, u32[]{:S(2)}) copy-start(f32[4,80,8,256]{3,2,1,0:T(8,128)} %get-tuple-element.12.refs_4_) | copy-start | bytes 7864324
  48.1 1.4 %copy-start.6 = (f32[4,48,8,256]{3,2,1,0:T(8,128)S(1)}, f32[4,48,8,256]{3,2,1,0:T(8,128)}, u32[]{:S(2)}) copy-start(f32[4,48,8,256]{3,2,1,0:T(8,128)} %copy-done.5) | copy-start | bytes 4718596
  56.3 1.5 %copy-start.1 = (f32[4,80,8,256]{3,2,1,0:T(8,128)}, f32[4,80,8,256]{3,2,1,0:T(8,128)S(1)}, u32[]{:S(2)}) copy-start(f32[4,80,8,256]{3,2,1,0:T(8,128)S(1)} %get-tuple-element.14.refs_6_.refs_3_.refs_5_) | copy-start | bytes 7864324
  58.9 1.7 %copy-start.2 = (f32[4,80,8,256]{3,2,1,0:T(8,128)S(1)}, f32[4,80,8,256]{3,2,1,0:T(8,128)}, u32[]{:S(2)}) copy-start(f32[4,80,8,256]{3,2,1,0:T(8,128)} %copy-done.1) | copy-start | bytes 7864324
  64.6 9.4 %copy-start.3 = (f32[4,80,8,256]{3,2,1,0:T(8,128)S(1)}, f32[4,80,8,256]{3,2,1,0:T(8,128)}, u32[]{:S(2)}) copy-start(f32[4,80,8,256]{3,2,1,0:T(8,128)} %copy-done.1) | copy-start | bytes 7864324
  64.6 14.6 %collective-permute-start.8 = (f32[1,80,8,256]{3,2,1,0:T(8,128)S(1)}, f32[1,80,8,256]{3,2,1,0:T(8,128)}, u32[]{:S(2)}, u32[]{:S(2)}) collective-permute-start(f32[1,80,8,256]{3,2,1,0:T(8,128)S(1)} %lag_across.2), channel_id=1, source_target_pairs={{1,2},{2,1},{5,6},{6,5},{9,10},{10,9},{13,14},{14,13},{17,18},{18,... | collective-permute-start | bytes 1966088 | tf_op jit(solution)/shard_map/ppermute | solution.py:285
  66.3 20.8 %collective-permute-start = (f32[2,2,8,32,128]{4,3,2,1,0:T(8,128)}, f32[2,2,8,32,128]{4,3,2,1,0:T(8,128)S(1)}, u32[]{:S(2)}, u32[]{:S(2)}) collective-permute-start(f32[2,2,8,32,128]{4,3,2,1,0:T(8,128)} %get-tuple-element.19), channel_id=1, source_target_pairs={{0,1},{3,2},{4,5},{7,6},{8,9},{11,10},{12,13},{15,14},{16,17},{19,... | collective-permute-start | bytes 1572872 | tf_op jit(solution)/shard_map/ppermute | solution.py:282
  67.7 1.4 %copy-start.8 = (f32[4,48,8,256]{3,2,1,0:T(8,128)S(1)}, f32[4,48,8,256]{3,2,1,0:T(8,128)}, u32[]{:S(2)}) copy-start(f32[4,48,8,256]{3,2,1,0:T(8,128)} %copy-done.7) | copy-start | bytes 4718596
  70.1 3.9 %copy-start.15 = (bf16[2,2,256,256]{3,2,1,0:T(8,128)(2,1)S(1)}, bf16[2,2,256,256]{3,2,1,0:T(8,128)(2,1)}, u32[]{:S(2)}) copy-start(bf16[2,2,256,256]{3,2,1,0:T(8,128)(2,1)} %constant.38.clone.refs_2_.refs_4_.refs_1_) | copy-start | bytes 1572868
  73.2 8.5 %copy-start.9 = (f32[4,48,8,256]{3,2,1,0:T(8,128)S(1)}, f32[4,48,8,256]{3,2,1,0:T(8,128)}, u32[]{:S(2)}) copy-start(f32[4,48,8,256]{3,2,1,0:T(8,128)} %copy-done.7) | copy-start | bytes 4718596
  73.2 12.4 %collective-permute-start.4 = (f32[1,48,8,256]{3,2,1,0:T(8,128)S(1)}, f32[1,48,8,256]{3,2,1,0:T(8,128)S(1)}, u32[]{:S(2)}, u32[]{:S(2)}) collective-permute-start(f32[1,48,8,256]{3,2,1,0:T(8,128)S(1)} %lag_inside.2), channel_id=1, source_target_pairs={{1,2},{2,1},{5,6},{6,5},{9,10},{10,9},{13,14},{14,13},{17,18},{18,... | collective-permute-start | bytes 1179656 | tf_op jit(solution)/shard_map/ppermute | solution.py:285
  78.5 15.4 %collective-permute-start.10 = (f32[1,80,8,256]{3,2,1,0:T(8,128)S(1)}, f32[1,80,8,256]{3,2,1,0:T(8,128)S(1)}, u32[]{:S(2)}, u32[]{:S(2)}) collective-permute-start(f32[1,80,8,256]{3,2,1,0:T(8,128)S(1)} %lag_across.3), channel_id=1, source_target_pairs={{1,2},{2,1},{5,6},{6,5},{9,10},{10,9},{13,14},{14,13},{17,18},{18,... | collective-permute-start | bytes 1966088 | tf_op jit(solution)/shard_map/ppermute | solution.py:285
  80.4 28.5 %collective-permute-start.9 = (f32[1,80,8,256]{3,2,1,0:T(8,128)S(1)}, f32[1,80,8,256]{3,2,1,0:T(8,128)S(1)}, u32[]{:S(2)}, u32[]{:S(2)}) collective-permute-start(f32[1,80,8,256]{3,2,1,0:T(8,128)S(1)} %dynamic-slice_add_fusion), channel_id=1, source_target_pairs={{1,0},{2,3},{5,4},{6,7},{9,8},{10,11},{13,12},{14,15},{17,16},{18,... | collective-permute-start | bytes 1966088 | tf_op jit(solution)/shard_map/ppermute | solution.py:288
  84.9 9.0 %collective-permute-start.7 = (f32[1,48,8,256]{3,2,1,0:T(8,128)S(1)}, f32[1,48,8,256]{3,2,1,0:T(8,128)S(1)}, u32[]{:S(2)}, u32[]{:S(2)}) collective-permute-start(f32[1,48,8,256]{3,2,1,0:T(8,128)S(1)} %lag_inside.3), channel_id=1, source_target_pairs={{1,2},{2,1},{5,6},{6,5},{9,10},{10,9},{13,14},{14,13},{17,18},{18,... | collective-permute-start | bytes 1179656 | tf_op jit(solution)/shard_map/ppermute | solution.py:285
  85.6 23.2 %collective-permute-start.5 = (f32[1,48,8,256]{3,2,1,0:T(8,128)S(1)}, f32[1,48,8,256]{3,2,1,0:T(8,128)S(1)}, u32[]{:S(2)}, u32[]{:S(2)}) collective-permute-start(f32[1,48,8,256]{3,2,1,0:T(8,128)S(1)} %dynamic-slice_add_fusion.1), channel_id=1, source_target_pairs={{1,0},{2,3},{5,4},{6,7},{9,8},{10,11},{13,12},{14,15},{17,16},{18,... | collective-permute-start | bytes 1179656 | tf_op jit(solution)/shard_map/ppermute | solution.py:288
  (11 other events, 10.5 us)

commit v3 on v2

v3 whole, which is shorter than its diff:
```python
import functools

import jax
import jax.numpy as jnp
import ml_dtypes
import numpy as np
from jax import lax
from jax.experimental import pallas as pl
from jax.experimental.pallas import tpu as pltpu
from jax.sharding import PartitionSpec as P

NEAR = 32
LAGS = 256
HALF = 8
LANES = 128
VMEM_LIMIT = 60 << 20


def split_table(table):
    high = table.astype(ml_dtypes.bfloat16)
    low = (table - high.astype(np.float64)).astype(ml_dtypes.bfloat16)
    return np.stack([high, low])


def make_tables(win, lags, segs):
    bins = win // 2
    samples = np.arange(win)
    hann = 0.5 - 0.5 * np.cos(2.0 * np.pi * samples / win)
    even, odd = np.arange(2, bins + 1, 2), np.arange(1, bins, 2)
    order = np.concatenate([even, odd])

    def forward(picked):
        phases = 2.0 * np.pi * ((samples[: win // 2, None] * picked[None, :]) % win) / win
        return split_table(np.concatenate([np.cos(phases), -np.sin(phases)], axis=1))

    near = np.abs(order[:, None] - order[None, :]) <= HALF
    band = near / (2.0 * HALF + 1.0) + 0.1 / bins
    lag = np.arange(lags) - lags // 2
    phases = 2.0 * np.pi * ((order[:, None] * lag[None, :]) % win) / win
    halves = np.split(phases, 2)
    rows = [part for h in halves for part in (np.cos(h), -np.sin(h))]
    high, low = split_table(np.concatenate(rows, axis=0) / segs)
    inverse = np.concatenate([high, low, high], axis=0)
    return {
        "hann": hann.astype(np.float32)[None, :],
        "even": forward(even),
        "odd": forward(odd),
        "band": split_table(band),
        "inverse": inverse,
    }


def dot_split(value, table):
    high = value.astype(jnp.bfloat16)
    low = (value - high.astype(jnp.float32)).astype(jnp.bfloat16)
    dot = functools.partial(jnp.dot, preferred_element_type=jnp.float32)
    return dot(high, table[0]) + (dot(high, table[1]) + dot(low, table[0]))


def whiten_kernel(x_ref, hann, even, odd, band, w_ref, stage):
    channels, segs, win = x_ref.shape
    parts = win // LANES
    for part in range(parts):
        lanes = slice(LANES * part, LANES * part + LANES)
        stage[part] = x_ref[:, :, lanes].reshape(channels * segs, LANES)
    pieces = []
    for s in range(segs):
        pieces.append([
            stage[part, pl.ds(s, channels, stride=segs), :] * hann[:, LANES * part : LANES * part + LANES]
            for part in range(parts)
        ])
    quarter = [jnp.concatenate([piece[part] for piece in pieces], axis=0) for part in range(parts)]
    both = jnp.concatenate([quarter[0] + quarter[2], quarter[1] + quarter[3]], axis=1)
    between = jnp.concatenate([quarter[0] - quarter[2], quarter[1] - quarter[3]], axis=1)
    spectra = (dot_split(both, even), dot_split(between, odd))
    energy = jnp.concatenate(
        [sp[:, :LANES] * sp[:, :LANES] + sp[:, LANES:] * sp[:, LANES:] for sp in spectra], axis=1
    )
    scale = lax.rsqrt(dot_split(energy, band) + 1e-06)
    for half, sp in enumerate(spectra):
        own = scale[:, LANES * half : LANES * half + LANES]
        real, imag = sp[:, :LANES] * own, sp[:, LANES:] * own
        for s in range(segs):
            rows = slice(channels * s, channels * s + channels)
            w_ref[half, 0, s] = real[rows]
            w_ref[half, 1, s] = imag[rows]


def whiten(x, tables, picks):
    blocks, near, segs, win = x.shape
    names = ("hann", "even", "odd", "band")
    consts = [jnp.asarray(tables[name]) for name in names]
    count = len(picks)

    def kernel(x_any, *refs):
        tabs, outs = refs[:4], refs[4 : 4 + count]
        staged, blocks_in, sems = refs[4 + count :]
        copies = []
        for index, pick in enumerate(picks):
            place = pick(lax.axis_index("tm")) if callable(pick) else pick
            copies.append(pltpu.make_async_copy(x_any.at[place], blocks_in.at[index], sems.at[index]))
            copies[-1].start()
        for index in range(count):
            copies[index].wait()
            whiten_kernel(blocks_in.at[index], *tabs, outs[index], staged)

    vmem = pl.BlockSpec(memory_space=pltpu.VMEM)
    shape = jax.ShapeDtypeStruct((2, 2, segs, near, LANES), jnp.float32)
    return pl.pallas_call(
        kernel,
        in_specs=[pl.BlockSpec(memory_space=pl.ANY)] + [vmem] * len(consts),
        out_specs=[vmem] * count,
        out_shape=[shape] * count,
        scratch_shapes=[
            pltpu.VMEM((win // LANES, near * segs, LANES), jnp.float32),
            pltpu.VMEM((count, near, segs, win), jnp.float32),
            pltpu.SemaphoreType.DMA((count,)),
        ],
        compiler_params=pltpu.CompilerParams(vmem_limit_bytes=VMEM_LIMIT),
        cost_estimate=pl.CostEstimate(flops=count * 500_000_000, bytes_accessed=count << 20, transcendentals=0),
        name="whiten",
    )(x, *consts)


def groups_of(near, which):
    tiles = near // 8
    inside = [(tile, offset) for tile in range(tiles) for offset in range(1, near - 8 * tile - 7)]
    across = [(tile, offset) for tile in range(tiles) for offset in range(near - 8 * tile - 7, near + 1)]
    return {"inside": inside, "across": across, "all": inside + across}[which]


def products(pair, half, lhs, groups, fresh, batch=4):
    segs = pair.shape[2]
    index_of = {group: index for index, group in enumerate(groups)}
    tiles = sorted({tile for tile, _ in groups})
    for begin in range(0, segs, batch):
        span = range(begin, min(begin + batch, segs))
        real = {t: [pair[half, 0, s, pl.ds(8 * t, 8), :] for s in span] for t in tiles}
        imag = {t: [pair[half, 1, s, pl.ds(8 * t, 8), :] for s in span] for t in tiles}
        added = {t: [re + im for re, im in zip(real[t], imag[t])] for t in tiles}
        for row in range(1, 8 * len(tiles) + NEAR):
            units = [(t, row - 8 * t) for t in tiles if (t, row - 8 * t) in index_of]
            if not units:
                continue
            sums = {}
            for at, s in enumerate(span):
                other_re = pair[half, 0, s, pl.ds(row, 8), :]
                other_im = pair[half, 1, s, pl.ds(row, 8), :]
                apart = other_re - other_im
                for unit in units:
                    t = unit[0]
                    terms = (real[t][at] * other_re, imag[t][at] * other_im, added[t][at] * apart)
                    sums[unit] = terms if at == 0 else tuple(old + new for old, new in zip(sums[unit], terms))
            for unit in units:
                rr, ii, mixed = sums[unit]
                cross_re, cross_im = rr + ii, mixed - rr + ii
                rows = pl.ds(8 * index_of[unit], 8)
                if not (fresh and begin == 0):
                    cross_re = cross_re + lhs[half, rows, :LANES]
                    cross_im = cross_im + lhs[half, rows, LANES:]
                lhs[half, rows, :LANES] = cross_re
                lhs[half, rows, LANES:] = cross_im


def lag_sums(which, sources, tables, role=None):
    table = jnp.asarray(tables["inverse"])
    sample = sources[0][0][0]
    halves, parts, segs, near, lanes = sample.shape
    groups = groups_of(near, which)
    kinds = {"inside": ("inside",), "across": ("across",), "all": ("inside", "across")}[which]
    sides = 1 if which == "inside" else 2
    operands, layout = [], []
    for source in sources:
        layout.append([])
        for side in range(sides):
            places = []
            for value in source[side]:
                known = [i for i, other in enumerate(operands) if other is value]
                if not known:
                    operands.append(value)
                places.append(known[0] if known else len(operands) - 1)
            layout[-1].append(places)
    shapes = [(len(groups_of(near, kind)), 8, LAGS) for kind in kinds]
    rows = 8 * len(groups)
    chunk = 16

    def kernel(*refs):
        cands, table_any = refs[: len(operands)], refs[len(operands)]
        outs = refs[len(operands) + 1 : len(operands) + 1 + len(kinds)]
        pair, lhs, table_ref, result, in_sems, table_sem, out_sems = refs[len(operands) + 1 + len(kinds) :]
        pick = role(lax.axis_index("tm")) if role is not None else None

        def copy(number, side, half, place):
            return pltpu.make_async_copy(
                cands[place].at[half],
                pair.at[number, half, :, :, pl.ds(side * near, near), :],
                in_sems.at[number, half, side],
            )

        for half in range(halves):
            for number, source in enumerate(layout):
                for side, places in enumerate(source):
                    if len(places) == 1:
                        copy(number, side, half, places[0]).start()
                        continue
                    for choice, place in enumerate(places):

                        @pl.when(pick == choice)
                        def _():
                            copy(number, side, half, place).start()

            if half == 0:
                table_copy = pltpu.make_async_copy(table_any, table_ref, table_sem)
                table_copy.start()

        def each_half(half, _):
            for number, source in enumerate(layout):
                for side, places in enumerate(source):
                    copy(number, side, half, places[0]).wait()
                products(pair.at[number], half, lhs, groups, number == 0)
            return 0

        lax.fori_loop(0, halves, each_half, 0)
        table_copy.wait()
        copies = []
        base = 0
        for out, shape in zip(outs, shapes):
            for begin in range(0, shape[0], chunk):
                size = min(chunk, shape[0] - begin)
                span = pl.ds(8 * (base + begin), 8 * size)
                value = jnp.concatenate([lhs[half, span, :] for half in range(halves)], axis=1)
                high = value.astype(jnp.bfloat16)
                low = (value - high.astype(jnp.float32)).astype(jnp.bfloat16)
                lagged = jnp.dot(
                    jnp.concatenate([high, high, low], axis=1), table_ref[...], preferred_element_type=jnp.float32
                )
                result[pl.ds(base + begin, size)] = lagged.reshape(size, 8, LAGS)
                copies.append(
                    pltpu.make_async_copy(
                        result.at[pl.ds(base + begin, size)], out.at[pl.ds(begin, size)], out_sems.at[len(copies)]
                    )
                )
                copies[-1].start()
            base += shape[0]
        for done in copies:
            done.wait()

    anywhere = pl.BlockSpec(memory_space=pl.ANY)
    chunks = sum(-(-shape[0] // chunk) for shape in shapes)
    work = rows * len(sources) // 8
    return pl.pallas_call(
        kernel,
        in_specs=[anywhere] * (len(operands) + 1),
        out_specs=[anywhere] * len(kinds),
        out_shape=[jax.ShapeDtypeStruct(shape, jnp.float32) for shape in shapes],
        scratch_shapes=[
            pltpu.VMEM((len(sources), halves, parts, segs, sides * near, lanes), jnp.float32),
            pltpu.VMEM((halves, rows, 2 * lanes), jnp.float32),
            pltpu.VMEM(table.shape, table.dtype),
            pltpu.VMEM((len(groups), 8, LAGS), jnp.float32),
            pltpu.SemaphoreType.DMA((len(sources), halves, 2)),
            pltpu.SemaphoreType.DMA,
            pltpu.SemaphoreType.DMA((chunks,)),
        ],
        compiler_params=pltpu.CompilerParams(vmem_limit_bytes=VMEM_LIMIT),
        cost_estimate=pl.CostEstimate(flops=work * 16_000_000, bytes_accessed=1 << 20, transcendentals=0),
        name="lag_" + which,
    )(*operands, table)


def place_kernel(near, count, *refs):
    terms, out_ref, stage = refs[: 2 * count], refs[2 * count], refs[2 * count + 1]
    for kind in range(2):
        for index, (tile, offset) in enumerate(groups_of(near, ("inside", "across")[kind])):
            value = terms[kind * count][index]
            for other in range(1, count):
                value = value + terms[kind * count + other][index]
            for part in range(LAGS // LANES):
                stage[part, pl.ds(8 * tile * near + offset - 1, 8, stride=near), :] = value[
                    :, LANES * part : LANES * part + LANES
                ]
    for part in range(LAGS // LANES):
        out_ref[:, :, LANES * part : LANES * part + LANES] = stage[part].reshape(near, near, LANES)


def place(near, inside, across):
    vmem = pl.BlockSpec(memory_space=pltpu.VMEM)
    count = len(inside)
    return pl.pallas_call(
        functools.partial(place_kernel, near, count),
        in_specs=[vmem] * (2 * count),
        out_specs=vmem,
        out_shape=jax.ShapeDtypeStruct((near, near, LAGS), jnp.float32),
        scratch_shapes=[pltpu.VMEM((LAGS // LANES, near * near, LANES), jnp.float32)],
        compiler_params=pltpu.CompilerParams(vmem_limit_bytes=VMEM_LIMIT),
        cost_estimate=pl.CostEstimate(flops=1_000_000_000, bytes_accessed=4 << 20, transcendentals=0),
        name="place",
    )(*inside, *across)


def shifted(value, steps):
    count = lax.axis_size("fibre")
    return lax.ppermute(value, "fibre", [(source, source + steps) for source in range(max(0, -steps), count)])


def line_of_four(traces):
    channels, segs, win = traces.shape
    tables = make_tables(win, LAGS, segs * 4)
    left = lax.axis_index("tm") < 2
    blocks = traces.reshape(4, NEAR, segs, win)
    fibres = lax.axis_size("fibre")

    def outer(value):
        return lax.ppermute(value, "tm", [(0, 1), (3, 2)])

    def outer_next(value):
        pairs = [(4 * fibre + 4, 4 * fibre + 1) for fibre in range(fibres - 1)]
        pairs += [(4 * fibre + 3, 4 * fibre + 2) for fibre in range(fibres)]
        return lax.ppermute(value, ("fibre", "tm"), pairs)

    def middle(value):
        return lax.ppermute(value, "tm", [(1, 2), (2, 1)])

    def inner(value):
        return lax.ppermute(value, "tm", [(1, 0), (2, 3)])

    (far,) = whiten(blocks, tables, [lambda z: jnp.where(z < 2, 3, 0)])
    e1 = outer(far)
    (next_far,) = whiten(blocks, tables, [lambda z: jnp.where(z < 2, 0, 1)])
    e2 = outer_next(next_far)
    halo = shifted(blocks[0], -1)
    own = whiten(blocks, tables, [0, 1, 2, 3])
    e3 = outer(own[2])
    e4 = outer(jnp.where(left, own[1], own[3]))
    own += whiten(halo[None], tables, [0])

    role = lambda z: jnp.where(z < 2, 0, 1)
    (m1,) = lag_sums("inside", [([far], None), ([e1], None)], tables)
    m1 = middle(m1)
    (m2,) = lag_sums("across", [([own[3], own[0]], [own[4], own[1]]), ([e1], [e2])], tables, role)
    m2 = middle(m2)
    opposite = lag_sums("all", [([own[0], own[3]], [own[1], own[4]])], tables, role)
    (m3,) = lag_sums("inside", [([own[2], own[1]], None), ([e3, e2], None)], tables, role)
    m3 = middle(m3)
    (m4,) = lag_sums("across", [([own[2], own[1]], [own[3], own[2]]), ([e3, e2], [e1, e3])], tables, role)
    m4 = middle(m4)
    near = lag_sums(
        "all", [(own[:4], own[1:]), ([e4, e4, e3, e4], [e3, e3, e4, e3])], tables, lambda z: z
    )
    i1 = inner(m1 + opposite[0])
    i2 = inner(m2 + opposite[1])
    return place(NEAR, [near[0], i1, m3], [near[1], i2, m4])


def any_line(traces):
    channels, segs, win = traces.shape
    tables = make_tables(win, LAGS, segs * lax.axis_size("tm"))
    count = channels // NEAR
    blocks = traces.reshape(count, NEAR, segs, win)
    halo = shifted(blocks[0], -1)
    spectra = whiten(blocks, tables, list(range(count))) + whiten(halo[None], tables, [0])
    pieces = []
    for index in range(count):
        inside, across = lag_sums("all", [([spectra[index]], [spectra[index + 1]])], tables)
        pieces.append(place(NEAR, [inside], [across]))
    return lax.psum_scatter(jnp.concatenate(pieces, axis=0), "tm", scatter_dimension=0, tiled=True)


def shards(traces):
    if lax.axis_size("tm") == 4 and traces.shape[0] == 4 * NEAR:
        return line_of_four(traces)
    return any_line(traces)


def solution(mesh):
    in_specs = (P("fibre", "tm", None),)
    out_specs = P(("fibre", "tm"), None, None)
    return jax.shard_map(shards, mesh=mesh, in_specs=in_specs, out_specs=out_specs, check_vma=False)
```

time: 112 us -> 99.4 us (0.89)
  local copies, waits for them, and re-layouts: 23.8 us -> 4.44 us
  starting transfers between devices: 19.1 us -> 28.6 us
  waiting for transfers between devices: 15 us -> 13.6 us
  other arithmetic: 2.7 us -> 1.31 us
    unnamed x48 -> x22, local copies, waits for them, and re-layouts: 21 us -> 3.36 us
    ppermute x4 -> x3, starting transfers between devices: 11.2 us -> 20.9 us  [outer(): return lax.ppermute(value, 'tm', [(0, 1), (3, 2)])]
    ppermute x2, waiting for transfers between devices: 14.9 us -> 13 us  [inner(): return lax.ppermute(value, 'tm', [(1, 0), (2, 3)])]
    pallas_call x1, Pallas kernels: 1.93 us -> 3.83 us  [place(): pl.pallas_call(functools.partial(place_kernel, near, count), in_specs=[vm...]
    pallas_call x9 -> x10, Pallas kernels: 47.9 us -> 46.5 us  [the longest x6 29.3 us: lag_sums(): pl.pallas_call(kernel, in_specs=[anywhere] * (len(operands) + 1), out_spe...]
    select_n x1, other arithmetic: 1.23 us -> 0.08 us  [line_of_four(): e4 = outer(jnp.where(left, own[1], own[3]))]
  transfers between devices with their start and end apart: 11 -> 11, of which waited for: 1 -> 2; matrix products, arithmetic and copies ran while one was open for 3% -> 1% of each run, Pallas kernels for 43% -> 47%
where the time goes in v3:
time: 99.4 us; the launch traced here: 98.6 us
  Pallas kernels  50.3 us (51%)
  starting transfers between devices  28.6 us (29%)
  waiting for transfers between devices  13.6 us (14%)
  local copies, waits for them, and re-layouts  4.44 us (4%)
  other arithmetic  1.31 us (1%)
    pallas_call x6, Pallas kernels, lag_sums(): pl.pallas_call(kernel, in_specs=[anywhere] * (len(operands) + 1), out_spe...  29.3 us
    ppermute x3, starting transfers between devices, outer(): return lax.ppermute(value, 'tm', [(0, 1), (3, 2)])  20.9 us
    pallas_call x4, Pallas kernels, whiten(): pl.pallas_call(kernel, in_specs=[pl.BlockSpec(memory_space=pl.ANY)] + [vm...  17.2 us
    ppermute x2, waiting for transfers between devices, inner(): return lax.ppermute(value, 'tm', [(1, 0), (2, 3)])  13 us
    pallas_call x1, Pallas kernels, place(): pl.pallas_call(functools.partial(place_kernel, near, count), in_specs=[vm...  3.83 us
    unnamed x22, local copies, waits for them, and re-layouts  3.36 us
    ppermute x2, starting transfers between devices, inner(): return lax.ppermute(value, 'tm', [(1, 0), (2, 3)])  2.9 us
    ppermute x4, starting transfers between devices, middle(): return lax.ppermute(value, 'tm', [(1, 2), (2, 1)])  2.78 us
  transfers between devices with their start and end apart: 11, of which 2 were waited for; matrix products, arithmetic and copies ran while one was open for 1% of the time, Pallas kernels for 47%

profile of v3, /device:TPU:0, one launch (start us, length us, event | category | flops | bytes accessed | tf_op | source)
XLA Modules:
  0.0 98.6 jit_solution(7419459654625694248)
XLA Ops:
  0.0 1.1 %slice.4 = f32[32,8,512]{2,1,0:T(8,128)S(1)} slice(f32[128,8,512]{2,1,0:T(8,128)} %param.6), slice={[0:32], [0:8], [0:512]} | slice | bytes 1048576 | tf_op jit(solution)/shard_map/slice | solution.py:331
  1.1 1.3 %collective-permute-start = (f32[32,8,512]{2,1,0:T(8,128)S(1)}, f32[32,8,512]{2,1,0:T(8,128)S(1)}, u32[]{:S(2)}, u32[]{:S(2)}) collective-permute-start(f32[32,8,512]{2,1,0:T(8,128)S(1)} %slice.4), channel_id=1, source_target_pairs={{4,0},{8,4},{12,8},{16,12},{20,16},{24,20},{28,24},{5,1},{9,5},{13... | collective-permute-start | bytes 1572872 | tf_op jit(solution)/shard_map/ppermute | solution.py:303
  2.4 3.8 %whiten.7 = f32[2,2,8,32,128]{4,3,2,1,0:T(8,128)} custom-call(f32[4,32,8,512]{3,2,1,0:T(8,128)} %bitcast.2, f32[1,512]{1,0:T(1,128)} %constant.16.clone.refs_0_, bf16[2,256,256]{2,1,0:T(8,128)(2,1)} %constant.17.clone.refs_1_, bf16[2,256,256]{2,1,0:T(8,128)(2,1)} %constant.18.clone.refs_2_, bf16[2,256,256]{2,1,0:T(8,128)(2,1)} %constant.19.clone.refs_3_), custom_call_target="tpu_custom_call" | custom-call | flops 500000000 | bytes 1048576 | tf_op jit(solution)/shard_map/whiten/pallas_call | solution.py:109
  6.9 3.8 %whiten.6.refs_0_ = f32[2,2,8,32,128]{4,3,2,1,0:T(8,128)} custom-call(f32[4,32,8,512]{3,2,1,0:T(8,128)} %bitcast.3, f32[1,512]{1,0:T(1,128)} %constant.16.clone.refs_0_, bf16[2,256,256]{2,1,0:T(8,128)(2,1)} %constant.17.clone.refs_1_, bf16[2,256,256]{2,1,0:T(8,128)(2,1)} %constant.18.clone.refs_2_, bf16[2,256,256]{2,1,0:T(8,128)(2,1)} %constant.19.clone.refs_3_), custom_call_target="tpu_custom_call" | custom-call | flops 500000000 | bytes 1048576 | tf_op jit(solution)/shard_map/whiten/pallas_call | solution.py:109
  10.7 5.6 %collective-permute-start.3 = (f32[2,2,8,32,128]{4,3,2,1,0:T(8,128)}, f32[2,2,8,32,128]{4,3,2,1,0:T(8,128)S(1)}, u32[]{:S(2)}, u32[]{:S(2)}) collective-permute-start(f32[2,2,8,32,128]{4,3,2,1,0:T(8,128)} %whiten.6.refs_0_), channel_id=1, source_target_pairs={{0,1},{3,2},{4,5},{7,6},{8,9},{11,10},{12,13},{15,14},{16,17},{19,... | collective-permute-start | bytes 1572872 | tf_op jit(solution)/shard_map/ppermute | solution.py:314
  16.2 5.9 %whiten.4 = (f32[2,2,8,32,128]{4,3,2,1,0:T(8,128)}, f32[2,2,8,32,128]{4,3,2,1,0:T(8,128)}, f32[2,2,8,32,128]{4,3,2,1,0:T(8,128)}, f32[2,2,8,32,128]{4,3,2,1,0:T(8,128)}) custom-call(f32[4,32,8,512]{3,2,1,0:T(8,128)} %bitcast.4, f32[1,512]{1,0:T(1,128)} %constant.16.clone.refs_0_, bf16[2,256,256]{2,1,0:T(8,128)(2,1)} %constant.17.clone.refs_1_, ...), custom_call_target="tpu_custom_call" | custom-call | flops 2000000000 | bytes 4194304 | tf_op jit(solution)/shard_map/whiten/pallas_call | solution.py:109
  22.1 1.3 %collective-permute-start.2 = (f32[2,2,8,32,128]{4,3,2,1,0:T(8,128)}, f32[2,2,8,32,128]{4,3,2,1,0:T(8,128)S(1)}, u32[]{:S(2)}, u32[]{:S(2)}) collective-permute-start(f32[2,2,8,32,128]{4,3,2,1,0:T(8,128)} %get-tuple-element.15.refs_2_.refs_0_), channel_id=1, source_target_pairs={{0,1},{3,2},{4,5},{7,6},{8,9},{11,10},{12,13},{15,14},{16,17},{19,... | collective-permute-start | bytes 1572872 | tf_op jit(solution)/shard_map/ppermute | solution.py:314
  23.5 0.8 copy-done.10
  24.2 3.8 %whiten.5.refs_4_.refs_3_.refs_2_ = f32[2,2,8,32,128]{4,3,2,1,0:T(8,128)} custom-call(f32[1,32,8,512]{3,2,1,0:T(8,128)} %bitcast.5, f32[1,512]{1,0:T(1,128)} %constant.16.clone.refs_0_, bf16[2,256,256]{2,1,0:T(8,128)(2,1)} %constant.17.clone.refs_1_, bf16[2,256,256]{2,1,0:T(8,128)(2,1)} %constant.18.clone.refs_2_, bf16[2,256,256]{2,1,0:T(8,128)(2,1)} %constant.19.clone.refs_3_), custom_call_target="tpu_custom_call" | custom-call | flops 500000000 | bytes 1048576 | tf_op jit(solution)/shard_map/whiten/pallas_call | solution.py:109
  29.5 5.0 %lag_across.2 = f32[80,8,256]{2,1,0:T(8,128)} custom-call(f32[2,2,8,32,128]{4,3,2,1,0:T(8,128)} %get-tuple-element.16.refs_3_.refs_1_.refs_0_.refs_2_, f32[2,2,8,32,128]{4,3,2,1,0:T(8,128)} %get-tuple-element.13.refs_0_.refs_1_, f32[2,2,8,32,128]{4,3,2,1,0:T(8,128)} %whiten.5.refs_4_.refs_3_.refs_2_, ...), custom_call_target="tpu_custom_call" | custom-call | flops 2560000000 | bytes 1048576 | tf_op jit(solution)/shard_map/lag_across/pallas_call | solution.py:251
  34.5 0.7 collective-permute-start.8
  35.3 14.0 %collective-permute-start.1 = (f32[2,2,8,32,128]{4,3,2,1,0:T(8,128)S(1)}, f32[2,2,8,32,128]{4,3,2,1,0:T(8,128)}, u32[]{:S(2)}, u32[]{:S(2)}) collective-permute-start(f32[2,2,8,32,128]{4,3,2,1,0:T(8,128)S(1)} %broadcast_select_fusion), channel_id=1, source_target_pairs={{0,1},{3,2},{4,5},{7,6},{8,9},{11,10},{12,13},{15,14},{16,17},{19,... | collective-permute-start | bytes 1572872 | tf_op jit(solution)/shard_map/ppermute | solution.py:314
  49.3 3.7 %lag_inside.2 = f32[48,8,256]{2,1,0:T(8,128)} custom-call(f32[2,2,8,32,128]{4,3,2,1,0:T(8,128)} %whiten.6.refs_0_, f32[2,2,8,32,128]{4,3,2,1,0:T(8,128)} %copy-done.9, bf16[1536,256]{1,0:T(8,128)(2,1)} %constant.20.clone.refs_7_.refs_2_.refs_4_.refs_6_), custom_call_target="tpu_custom_call" | custom-call | flops 1536000000 | bytes 1048576 | tf_op jit(solution)/shard_map/lag_inside/pallas_call | solution.py:251
  53.8 0.8 copy-done.7
  54.6 4.9 %lag_across.3 = f32[80,8,256]{2,1,0:T(8,128)} custom-call(f32[2,2,8,32,128]{4,3,2,1,0:T(8,128)} %get-tuple-element.15.refs_2_.refs_0_, f32[2,2,8,32,128]{4,3,2,1,0:T(8,128)} %get-tuple-element.14.refs_1_.refs_2_.refs_3_, f32[2,2,8,32,128]{4,3,2,1,0:T(8,128)} %get-tuple-element.16.refs_3_.refs_1_.refs_0_.refs_2_, f32[2,2,8,32,128]{4,3,2,1,0:T(8,128)} %copy-done.7, ...), custom_call_target="tpu_custom_call" | custom-call | flops 2560000000 | bytes 1048576 | tf_op jit(solution)/shard_map/lag_across/pallas_call | solution.py:251
  60.2 5.0 %lag_all.3 = (f32[48,8,256]{2,1,0:T(8,128)}, f32[80,8,256]{2,1,0:T(8,128)}) custom-call(f32[2,2,8,32,128]{4,3,2,1,0:T(8,128)} %get-tuple-element.13.refs_0_.refs_1_, f32[2,2,8,32,128]{4,3,2,1,0:T(8,128)} %get-tuple-element.16.refs_3_.refs_1_.refs_0_.refs_2_, f32[2,2,8,32,128]{4,3,2,1,0:T(8,128)} %get-tuple-element.14.refs_1_.refs_2_.refs_3_, ...), custom_call_target="tpu_custom_call" | custom-call | flops 2048000000 | bytes 1048576 | tf_op jit(solution)/shard_map/lag_all/pallas_call | solution.py:251
  65.2 1.2 %add.7 = f32[80,8,256]{2,1,0:T(8,128)S(1)} add(f32[80,8,256]{2,1,0:T(8,128)S(1)} %collective-permute-done.8, f32[80,8,256]{2,1,0:T(8,128)} %get-tuple-element.20) | non-fusion elementwise | flops 163840 | bytes 1966080 | tf_op jit(solution)/shard_map/add | solution.py:351
  66.4 1.6 %collective-permute-start.9 = (f32[80,8,256]{2,1,0:T(8,128)S(1)}, f32[80,8,256]{2,1,0:T(8,128)S(1)}, u32[]{:S(2)}, u32[]{:S(2)}) collective-permute-start(f32[80,8,256]{2,1,0:T(8,128)S(1)} %add.7), channel_id=1, source_target_pairs={{1,0},{2,3},{5,4},{6,7},{9,8},{10,11},{13,12},{14,15},{17,16},{18,... | collective-permute-start | bytes 1966088 | tf_op jit(solution)/shard_map/ppermute | solution.py:325
  68.0 3.9 %lag_inside.3 = f32[48,8,256]{2,1,0:T(8,128)} custom-call(f32[2,2,8,32,128]{4,3,2,1,0:T(8,128)} %get-tuple-element.15.refs_2_.refs_0_, f32[2,2,8,32,128]{4,3,2,1,0:T(8,128)} %get-tuple-element.14.refs_1_.refs_2_.refs_3_, f32[2,2,8,32,128]{4,3,2,1,0:T(8,128)} %copy-done.7, f32[2,2,8,32,128]{4,3,2,1,0:T(8,128)} %copy-done.8, ...), custom_call_target="tpu_custom_call" | custom-call | flops 1536000000 | bytes 1048576 | tf_op jit(solution)/shard_map/lag_inside/pallas_call | solution.py:251
  72.7 1.3 %collective-permute-start.5 = (f32[48,8,256]{2,1,0:T(8,128)S(1)}, f32[48,8,256]{2,1,0:T(8,128)S(1)}, u32[]{:S(2)}, u32[]{:S(2)}) collective-permute-start(f32[48,8,256]{2,1,0:T(8,128)S(1)} %add.6), channel_id=1, source_target_pairs={{1,0},{2,3},{5,4},{6,7},{9,8},{10,11},{13,12},{14,15},{17,16},{18,... | collective-permute-start | bytes 1179656 | tf_op jit(solution)/shard_map/ppermute | solution.py:325
  74.0 6.7 %lag_all.2 = (f32[48,8,256]{2,1,0:T(8,128)}, f32[80,8,256]{2,1,0:T(8,128)}) custom-call(f32[2,2,8,32,128]{4,3,2,1,0:T(8,128)} %get-tuple-element.13.refs_0_.refs_1_, f32[2,2,8,32,128]{4,3,2,1,0:T(8,128)} %get-tuple-element.14.refs_1_.refs_2_.refs_3_, f32[2,2,8,32,128]{4,3,2,1,0:T(8,128)} %get-tuple-element.15.refs_2_.refs_0_, ...), custom_call_target="tpu_custom_call" | custom-call | flops 4096000000 | bytes 1048576 | tf_op jit(solution)/shard_map/lag_all/pallas_call | solution.py:251
  80.8 13.0 %collective-permute-done.5.refs_1_ = f32[48,8,256]{2,1,0:T(8,128)S(1)} collective-permute-done((f32[48,8,256]{2,1,0:T(8,128)S(1)}, f32[48,8,256]{2,1,0:T(8,128)S(1)}, u32[]{:S(2)}, u32[]{:S(2)}) %collective-permute-start.5) | collective-permute-done | bytes 393248 | tf_op jit(solution)/shard_map/ppermute | solution.py:325
  93.8 0.7 copy-done.5
  94.8 3.8 %place.1 = f32[32,32,256]{2,1,0:T(8,128)} custom-call(f32[48,8,256]{2,1,0:T(8,128)} %get-tuple-element.17.refs_0_, f32[48,8,256]{2,1,0:T(8,128)} %copy-done.5, f32[48,8,256]{2,1,0:T(8,128)} %copy-done.4, f32[80,8,256]{2,1,0:T(8,128)} %get-tuple-element.19.refs_3_, f32[80,8,256]{2,1,0:T(8,128)} %copy-done.1, f32[80,8,256]{2,1,0:T(8,128)} %copy-done), custom_call_target="tpu_custom_call" | custom-call | flops 1000000000 | bytes 4194304 | tf_op jit(solution)/shard_map/place/pallas_call | solution.py:289
  (35 shorter events, 4.6 us)
Async XLA Ops:
  1.1 22.4 %collective-permute-start = (f32[32,8,512]{2,1,0:T(8,128)S(1)}, f32[32,8,512]{2,1,0:T(8,128)S(1)}, u32[]{:S(2)}, u32[]{:S(2)}) collective-permute-start(f32[32,8,512]{2,1,0:T(8,128)S(1)} %slice.4), channel_id=1, source_target_pairs={{4,0},{8,4},{12,8},{16,12},{20,16},{24,20},{28,24},{5,1},{9,5},{13... | collective-permute-start | bytes 1572872 | tf_op jit(solution)/shard_map/ppermute | solution.py:303
  6.2 21.8 %collective-permute-start.6 = (f32[2,2,8,32,128]{4,3,2,1,0:T(8,128)}, f32[2,2,8,32,128]{4,3,2,1,0:T(8,128)S(1)}, u32[]{:S(2)}, u32[]{:S(2)}) collective-permute-start(f32[2,2,8,32,128]{4,3,2,1,0:T(8,128)} %whiten.7), channel_id=1, source_target_pairs={{4,1},{8,5},{12,9},{16,13},{20,17},{24,21},{28,25},{3,2},{7,6},{11... | collective-permute-start | bytes 1572872 | tf_op jit(solution)/shard_map/ppermute | solution.py:319
  10.7 18.0 %collective-permute-start.3 = (f32[2,2,8,32,128]{4,3,2,1,0:T(8,128)}, f32[2,2,8,32,128]{4,3,2,1,0:T(8,128)S(1)}, u32[]{:S(2)}, u32[]{:S(2)}) collective-permute-start(f32[2,2,8,32,128]{4,3,2,1,0:T(8,128)} %whiten.6.refs_0_), channel_id=1, source_target_pairs={{0,1},{3,2},{4,5},{7,6},{8,9},{11,10},{12,13},{15,14},{16,17},{19,... | collective-permute-start | bytes 1572872 | tf_op jit(solution)/shard_map/ppermute | solution.py:314
  22.1 31.7 %collective-permute-start.2 = (f32[2,2,8,32,128]{4,3,2,1,0:T(8,128)}, f32[2,2,8,32,128]{4,3,2,1,0:T(8,128)S(1)}, u32[]{:S(2)}, u32[]{:S(2)}) collective-permute-start(f32[2,2,8,32,128]{4,3,2,1,0:T(8,128)} %get-tuple-element.15.refs_2_.refs_0_), channel_id=1, source_target_pairs={{0,1},{3,2},{4,5},{7,6},{8,9},{11,10},{12,13},{15,14},{16,17},{19,... | collective-permute-start | bytes 1572872 | tf_op jit(solution)/shard_map/ppermute | solution.py:314
  23.5 0.8 copy-start.10
  28.0 0.8 copy-start.8
  28.7 0.8 copy-start.9
  29.5 5.8 %copy-start.2 = (f32[2,2,8,32,128]{4,3,2,1,0:T(8,128)S(1)}, f32[2,2,8,32,128]{4,3,2,1,0:T(8,128)}, u32[]{:S(2)}) copy-start(f32[2,2,8,32,128]{4,3,2,1,0:T(8,128)} %get-tuple-element.14.refs_1_.refs_2_.refs_3_) | copy-start | bytes 1572868
  29.5 5.8 %copy-start.3 = (f32[2,2,8,32,128]{4,3,2,1,0:T(8,128)S(1)}, f32[2,2,8,32,128]{4,3,2,1,0:T(8,128)}, u32[]{:S(2)}) copy-start(f32[2,2,8,32,128]{4,3,2,1,0:T(8,128)} %get-tuple-element.16.refs_3_.refs_1_.refs_0_.refs_2_) | copy-start | bytes 1572868
  34.5 30.7 %collective-permute-start.8 = (f32[80,8,256]{2,1,0:T(8,128)}, f32[80,8,256]{2,1,0:T(8,128)S(1)}, u32[]{:S(2)}, u32[]{:S(2)}) collective-permute-start(f32[80,8,256]{2,1,0:T(8,128)} %lag_across.2), channel_id=1, source_target_pairs={{1,2},{2,1},{5,6},{6,5},{9,10},{10,9},{13,14},{14,13},{17,18},{18,... | collective-permute-start | bytes 1966088 | tf_op jit(solution)/shard_map/ppermute | solution.py:322
  35.3 38.7 %collective-permute-start.1 = (f32[2,2,8,32,128]{4,3,2,1,0:T(8,128)S(1)}, f32[2,2,8,32,128]{4,3,2,1,0:T(8,128)}, u32[]{:S(2)}, u32[]{:S(2)}) collective-permute-start(f32[2,2,8,32,128]{4,3,2,1,0:T(8,128)S(1)} %broadcast_select_fusion), channel_id=1, source_target_pairs={{0,1},{3,2},{4,5},{7,6},{8,9},{11,10},{12,13},{15,14},{16,17},{19,... | collective-permute-start | bytes 1572872 | tf_op jit(solution)/shard_map/ppermute | solution.py:314
  53.1 19.6 %collective-permute-start.4 = (f32[48,8,256]{2,1,0:T(8,128)}, f32[48,8,256]{2,1,0:T(8,128)S(1)}, u32[]{:S(2)}, u32[]{:S(2)}) collective-permute-start(f32[48,8,256]{2,1,0:T(8,128)} %lag_inside.2), channel_id=1, source_target_pairs={{1,2},{2,1},{5,6},{6,5},{9,10},{10,9},{13,14},{14,13},{17,18},{18,... | collective-permute-start | bytes 1179656 | tf_op jit(solution)/shard_map/ppermute | solution.py:322
  53.8 0.8 copy-start.7
  59.5 21.3 %collective-permute-start.10 = (f32[80,8,256]{2,1,0:T(8,128)}, f32[80,8,256]{2,1,0:T(8,128)S(1)}, u32[]{:S(2)}, u32[]{:S(2)}) collective-permute-start(f32[80,8,256]{2,1,0:T(8,128)} %lag_across.3), channel_id=1, source_target_pairs={{1,2},{2,1},{5,6},{6,5},{9,10},{10,9},{13,14},{14,13},{17,18},{18,... | collective-permute-start | bytes 1966088 | tf_op jit(solution)/shard_map/ppermute | solution.py:322
  66.4 6.3 %copy-start.6 = (f32[48,8,256]{2,1,0:T(8,128)S(1)}, f32[48,8,256]{2,1,0:T(8,128)}, u32[]{:S(2)}) copy-start(f32[48,8,256]{2,1,0:T(8,128)} %get-tuple-element.18) | copy-start | bytes 1179652
  66.4 27.4 %collective-permute-start.9 = (f32[80,8,256]{2,1,0:T(8,128)S(1)}, f32[80,8,256]{2,1,0:T(8,128)S(1)}, u32[]{:S(2)}, u32[]{:S(2)}) collective-permute-start(f32[80,8,256]{2,1,0:T(8,128)S(1)} %add.7), channel_id=1, source_target_pairs={{1,0},{2,3},{5,4},{6,7},{9,8},{10,11},{13,12},{14,15},{17,16},{18,... | collective-permute-start | bytes 1966088 | tf_op jit(solution)/shard_map/ppermute | solution.py:325
  72.0 8.8 %collective-permute-start.7 = (f32[48,8,256]{2,1,0:T(8,128)}, f32[48,8,256]{2,1,0:T(8,128)S(1)}, u32[]{:S(2)}, u32[]{:S(2)}) collective-permute-start(f32[48,8,256]{2,1,0:T(8,128)} %lag_inside.3), channel_id=1, source_target_pairs={{1,2},{2,1},{5,6},{6,5},{9,10},{10,9},{13,14},{14,13},{17,18},{18,... | collective-permute-start | bytes 1179656 | tf_op jit(solution)/shard_map/ppermute | solution.py:322
  72.7 21.0 %collective-permute-start.5 = (f32[48,8,256]{2,1,0:T(8,128)S(1)}, f32[48,8,256]{2,1,0:T(8,128)S(1)}, u32[]{:S(2)}, u32[]{:S(2)}) collective-permute-start(f32[48,8,256]{2,1,0:T(8,128)S(1)} %add.6), channel_id=1, source_target_pairs={{1,0},{2,3},{5,4},{6,7},{9,8},{10,11},{13,12},{14,15},{17,16},{18,... | collective-permute-start | bytes 1179656 | tf_op jit(solution)/shard_map/ppermute | solution.py:325
  80.8 13.0 %copy-start.4 = (f32[48,8,256]{2,1,0:T(8,128)}, f32[48,8,256]{2,1,0:T(8,128)S(1)}, u32[]{:S(2)}) copy-start(f32[48,8,256]{2,1,0:T(8,128)S(1)} %collective-permute-done.7.refs_2_) | copy-start | bytes 1179652
  80.8 13.0 %copy-start = (f32[80,8,256]{2,1,0:T(8,128)}, f32[80,8,256]{2,1,0:T(8,128)S(1)}, u32[]{:S(2)}) copy-start(f32[80,8,256]{2,1,0:T(8,128)S(1)} %collective-permute-done.10.refs_5_) | copy-start | bytes 1966084
  93.8 0.8 copy-start.5
  93.8 1.0 %copy-start.1 = (f32[80,8,256]{2,1,0:T(8,128)}, f32[80,8,256]{2,1,0:T(8,128)S(1)}, u32[]{:S(2)}) copy-start(f32[80,8,256]{2,1,0:T(8,128)S(1)} %collective-permute-done.9.refs_4_) | copy-start | bytes 1966084

commit v4 on v3

v4 whole, which is shorter than its diff:
```python
import functools

import jax
import jax.numpy as jnp
import ml_dtypes
import numpy as np
from jax import lax
from jax.experimental import pallas as pl
from jax.experimental.pallas import tpu as pltpu
from jax.sharding import PartitionSpec as P

NEAR = 32
LAGS = 256
HALF = 8
LANES = 128
VMEM_LIMIT = 64 << 20
COST = 10_000_000_000


def split_table(table):
    high = table.astype(ml_dtypes.bfloat16)
    low = (table - high.astype(np.float64)).astype(ml_dtypes.bfloat16)
    return np.concatenate([high, low, high], axis=0)


def make_tables(win, lags, segs):
    bins = win // 2
    samples = np.arange(win)
    hann = 0.5 - 0.5 * np.cos(2.0 * np.pi * samples / win)
    even, odd = np.arange(2, bins + 1, 2), np.arange(1, bins, 2)
    order = np.concatenate([even, odd])

    def forward(picked):
        phases = 2.0 * np.pi * ((samples[: win // 2, None] * picked[None, :]) % win) / win
        return split_table(np.concatenate([np.cos(phases), -np.sin(phases)], axis=1))

    near = np.abs(order[:, None] - order[None, :]) <= HALF
    band = near / (2.0 * HALF + 1.0) + 0.1 / bins
    lag = np.arange(lags) - lags // 2
    phases = 2.0 * np.pi * ((order[:, None] * lag[None, :]) % win) / win
    rows = [part for half in np.split(phases, 2) for part in (np.cos(half), -np.sin(half))]
    return {
        "hann": np.tile(hann.astype(np.float32)[None, :], (8, 1)),
        "forward": np.stack([forward(even), forward(odd), split_table(band)]),
        "inverse": split_table(np.concatenate(rows, axis=0) / segs),
    }


def dot_split(value, table):
    high = value.astype(jnp.bfloat16)
    low = (value - high.astype(jnp.float32)).astype(jnp.bfloat16)
    return jnp.dot(jnp.concatenate([high, high, low], axis=1), table, preferred_element_type=jnp.float32)


def whiten_block(x_ref, hann, forward, w_ref, stage):
    channels, segs, win = x_ref.shape
    parts = win // LANES
    for part in range(parts):
        lanes = slice(LANES * part, LANES * part + LANES)
        stage[part] = x_ref[:, :, lanes].reshape(channels * segs, LANES)
    pieces = []
    for s in range(segs):
        pieces.append([
            stage[part, pl.ds(s, channels, stride=segs), :] * hann[0:1, LANES * part : LANES * part + LANES]
            for part in range(parts)
        ])
    quarter = [jnp.concatenate([piece[part] for piece in pieces], axis=0) for part in range(parts)]
    both = jnp.concatenate([quarter[0] + quarter[2], quarter[1] + quarter[3]], axis=1)
    between = jnp.concatenate([quarter[0] - quarter[2], quarter[1] - quarter[3]], axis=1)
    spectra = (dot_split(both, forward[0]), dot_split(between, forward[1]))
    energy = jnp.concatenate(
        [sp[:, :LANES] * sp[:, :LANES] + sp[:, LANES:] * sp[:, LANES:] for sp in spectra], axis=1
    )
    scale = lax.rsqrt(dot_split(energy, forward[2]) + 1e-06)
    for half, sp in enumerate(spectra):
        own = scale[:, LANES * half : LANES * half + LANES]
        real, imag = sp[:, :LANES] * own, sp[:, LANES:] * own
        for s in range(segs):
            rows = slice(channels * s, channels * s + channels)
            w_ref[half, 0, s] = real[rows]
            w_ref[half, 1, s] = imag[rows]


def whiten(x, tables, count):
    near, segs, win = x.shape[1:]
    consts = [jnp.asarray(tables["hann"]), jnp.asarray(tables["forward"])]

    def kernel(*refs):
        x_any, hann_any, forward_any = refs[:3]
        outs, refs = refs[3 : 3 + count], refs[3 + count :]
        stage, hann, forward, blocks_in, blocks_out, sems, out_sems = refs
        loads = [pltpu.make_async_copy(x_any.at[b], blocks_in.at[b], sems.at[b]) for b in range(count)]
        tabs = [
            pltpu.make_async_copy(hann_any, hann, sems.at[count]),
            pltpu.make_async_copy(forward_any, forward, sems.at[count + 1]),
        ]
        for load in tabs + loads:
            load.start()
        for load in tabs:
            load.wait()
        stores = []
        for index in range(count):
            loads[index].wait()
            whiten_block(blocks_in.at[index], hann, forward, blocks_out.at[index], stage)
            stores.append(pltpu.make_async_copy(blocks_out.at[index], outs[index], out_sems.at[index]))
            stores[-1].start()
        for store in stores:
            store.wait()

    shape = (2, 2, segs, near, LANES)
    far_memory = pl.BlockSpec(memory_space=pltpu.HBM)
    return pl.pallas_call(
        kernel,
        in_specs=[far_memory] * 3,
        out_specs=[far_memory] * count,
        out_shape=[jax.ShapeDtypeStruct(shape, jnp.float32)] * count,
        scratch_shapes=[
            pltpu.VMEM((win // LANES, near * segs, LANES), jnp.float32),
            pltpu.VMEM(consts[0].shape, consts[0].dtype),
            pltpu.VMEM(consts[1].shape, consts[1].dtype),
            pltpu.VMEM((count, near, segs, win), jnp.float32),
            pltpu.VMEM((count,) + shape, jnp.float32),
            pltpu.SemaphoreType.DMA((count + 2,)),
            pltpu.SemaphoreType.DMA((count,)),
        ],
        compiler_params=pltpu.CompilerParams(vmem_limit_bytes=VMEM_LIMIT),
        cost_estimate=pl.CostEstimate(flops=COST, bytes_accessed=1000, transcendentals=0),
        name="whiten",
    )(x, *consts)


def whiten_first(x, tables, before=None):
    near, segs, win = x.shape[1:]
    consts = [jnp.asarray(tables["hann"]), jnp.asarray(tables["forward"])]
    first = before is None
    count = 1 if first else 6
    passed = [] if first else [before]

    def kernel(*refs):
        x_any, hann_any, forward_any = refs[:3]
        refs = refs[3 + len(passed) :]
        outs, refs = refs[:count], refs[count:]
        stage, hann, forward, blocks_in, blocks_out, sems, out_sems = refs
        z = lax.axis_index("tm")
        end = (z == 0) | (z == 3)

        def load_tables():
            tabs = [
                pltpu.make_async_copy(hann_any, hann, sems.at[4]),
                pltpu.make_async_copy(forward_any, forward, sems.at[5]),
            ]
            for tab in tabs:
                tab.start()
            return tabs

        def one(load, slot):
            load.wait()
            whiten_block(blocks_in.at[slot], hann, forward, blocks_out.at[slot], stage)

        def all_four(tabs):
            loads = [pltpu.make_async_copy(x_any.at[b], blocks_in.at[b], sems.at[b]) for b in range(4)]
            for load in loads:
                load.start()
            for tab in tabs:
                tab.wait()
            stores = []
            for b in range(4):
                one(loads[b], b)
                stores.append(pltpu.make_async_copy(blocks_out.at[b], outs[b], out_sems.at[b]))
                stores[-1].start()
            for at, sources in enumerate(((0, 1), (1, 3))):
                for side, source in enumerate(sources):

                    @pl.when(z < 2 if side == 0 else z >= 2)
                    def _():
                        pltpu.make_async_copy(
                            blocks_out.at[source], outs[4 + at], out_sems.at[4 + at]
                        ).start()

                stores.append(
                    pltpu.make_async_copy(blocks_out.at[sources[0]], outs[4 + at], out_sems.at[4 + at])
                )
            for store in stores:
                store.wait()

        if first:

            @pl.when(end)
            def _():
                load = pltpu.make_async_copy(x_any.at[jnp.where(z < 2, 3, 0)], blocks_in.at[4], sems.at[6])
                load.start()
                for tab in load_tables():
                    tab.wait()
                one(load, 4)
                store = pltpu.make_async_copy(blocks_out.at[4], outs[0], out_sems.at[6])
                store.start()
                store.wait()

        else:
            all_four(load_tables())

    shape = (2, 2, segs, near, LANES)
    far_memory = pl.BlockSpec(memory_space=pltpu.HBM)
    return pl.pallas_call(
        kernel,
        in_specs=[far_memory] * (3 + len(passed)),
        out_specs=[far_memory] * count,
        out_shape=[jax.ShapeDtypeStruct(shape, jnp.float32)] * count,
        scratch_shapes=[
            pltpu.VMEM((win // LANES, near * segs, LANES), jnp.float32),
            pltpu.VMEM(consts[0].shape, consts[0].dtype),
            pltpu.VMEM(consts[1].shape, consts[1].dtype),
            pltpu.VMEM((5, near, segs, win), jnp.float32),
            pltpu.VMEM((5,) + shape, jnp.float32),
            pltpu.SemaphoreType.DMA((7,)),
            pltpu.SemaphoreType.DMA((7,)),
        ],
        compiler_params=pltpu.CompilerParams(vmem_limit_bytes=VMEM_LIMIT),
        cost_estimate=pl.CostEstimate(flops=COST, bytes_accessed=1000, transcendentals=0),
        name="whiten_first" if first else "whiten_rest",
    )(x, *consts, *passed)


def groups_of(near, which):
    tiles = near // 8
    inside = [(tile, offset) for tile in range(tiles) for offset in range(1, near - 8 * tile - 7)]
    across = [(tile, offset) for tile in range(tiles) for offset in range(near - 8 * tile - 7, near + 1)]
    return {"inside": inside, "across": across, "all": inside + across}[which]


def products(pair, half, lhs, groups, fresh, batch=4):
    segs = pair.shape[2]
    index_of = {group: index for index, group in enumerate(groups)}
    tiles = sorted({tile for tile, _ in groups})
    for begin in range(0, segs, batch):
        span = range(begin, min(begin + batch, segs))
        real = {t: [pair[half, 0, s, pl.ds(8 * t, 8), :] for s in span] for t in tiles}
        imag = {t: [pair[half, 1, s, pl.ds(8 * t, 8), :] for s in span] for t in tiles}
        added = {t: [re + im for re, im in zip(real[t], imag[t])] for t in tiles}
        for row in range(1, 8 * len(tiles) + NEAR):
            units = [(t, row - 8 * t) for t in tiles if (t, row - 8 * t) in index_of]
            if not units:
                continue
            sums = {}
            for at, s in enumerate(span):
                other_re = pair[half, 0, s, pl.ds(row, 8), :]
                other_im = pair[half, 1, s, pl.ds(row, 8), :]
                apart = other_re - other_im
                for unit in units:
                    t = unit[0]
                    terms = (real[t][at] * other_re, imag[t][at] * other_im, added[t][at] * apart)
                    sums[unit] = terms if at == 0 else tuple(old + new for old, new in zip(sums[unit], terms))
            for unit in units:
                rr, ii, mixed = sums[unit]
                cross_re, cross_im = rr + ii, mixed - rr + ii
                rows = pl.ds(8 * index_of[unit], 8)
                if not (fresh and begin == 0):
                    cross_re = cross_re + lhs[half, rows, :LANES]
                    cross_im = cross_im + lhs[half, rows, LANES:]
                lhs[half, rows, :LANES] = cross_re
                lhs[half, rows, LANES:] = cross_im


def lag_sums(which, sources, tables, role=None, prior=(), after=(), cost=COST, inner=False):
    table = jnp.asarray(tables["inverse"])
    sample = sources[0][0][0]
    halves, parts, segs, near, lanes = sample.shape
    groups = groups_of(near, which)
    sides = 1 if which == "inside" else 2
    operands, layout = [], []
    for source in sources:
        layout.append([])
        for side in range(sides):
            places = []
            for value in source[side]:
                known = [i for i, other in enumerate(operands) if other is value]
                if not known:
                    operands.append(value)
                places.append(known[0] if known else len(operands) - 1)
            layout[-1].append(places)
    shape = (len(groups), 8, LAGS)
    rows = 8 * len(groups)
    chunk = 16

    def kernel(*refs):
        if not inner:
            return work(*refs)
        z = lax.axis_index("tm")
        pl.when((z == 1) | (z == 2))(lambda: work(*refs))

    def work(*refs):
        cands, table_any = refs[: len(operands)], refs[len(operands)]
        refs = refs[len(operands) + 1 :]
        priors, refs = refs[: len(prior)], refs[len(prior) + len(after) :]
        out, pair, lhs, table_ref, result, in_sems, table_sem, prior_sem, out_sems = refs
        pick = role(lax.axis_index("tm")) if role is not None else None

        def copy(number, side, half, place):
            return pltpu.make_async_copy(
                cands[place].at[half],
                pair.at[number, half, :, :, pl.ds(side * near, near), :],
                in_sems.at[number, half, side],
            )

        for half in range(halves):
            for number, source in enumerate(layout):
                for side, places in enumerate(source):
                    if len(places) == 1:
                        copy(number, side, half, places[0]).start()
                        continue
                    for choice, place in enumerate(places):

                        @pl.when(pick == choice)
                        def _():
                            copy(number, side, half, place).start()

            if half == 0:
                table_copy = pltpu.make_async_copy(table_any, table_ref, table_sem)
                table_copy.start()
        if prior:
            prior_copy = pltpu.make_async_copy(priors[0], result, prior_sem)
            prior_copy.start()

        def each_half(half, _):
            for number, source in enumerate(layout):
                for side, places in enumerate(source):
                    copy(number, side, half, places[0]).wait()
                products(pair.at[number], half, lhs, groups, number == 0)
            return 0

        lax.fori_loop(0, halves, each_half, 0)
        table_copy.wait()
        if prior:
            prior_copy.wait()
        copies = []
        for begin in range(0, shape[0], chunk):
            size = min(chunk, shape[0] - begin)
            span = pl.ds(8 * begin, 8 * size)
            value = jnp.concatenate([lhs[half, span, :] for half in range(halves)], axis=1)
            lagged = dot_split(value, table_ref[...]).reshape(size, 8, LAGS)
            place = pl.ds(begin, size)
            result[place] = result[place] + lagged if prior else lagged
            copies.append(pltpu.make_async_copy(result.at[place], out.at[place], out_sems.at[len(copies)]))
            copies[-1].start()
        for done in copies:
            done.wait()

    far_memory = pl.BlockSpec(memory_space=pltpu.HBM)
    chunks = -(-shape[0] // chunk)
    return pl.pallas_call(
        kernel,
        in_specs=[far_memory] * (len(operands) + 1 + len(prior) + len(after)),
        out_specs=far_memory,
        out_shape=jax.ShapeDtypeStruct(shape, jnp.float32),
        scratch_shapes=[
            pltpu.VMEM((len(sources), halves, parts, segs, sides * near, lanes), jnp.float32),
            pltpu.VMEM((halves, rows, 2 * lanes), jnp.float32),
            pltpu.VMEM(table.shape, table.dtype),
            pltpu.VMEM(shape, jnp.float32),
            pltpu.SemaphoreType.DMA((len(sources), halves, 2)),
            pltpu.SemaphoreType.DMA,
            pltpu.SemaphoreType.DMA,
            pltpu.SemaphoreType.DMA((chunks,)),
        ],
        compiler_params=pltpu.CompilerParams(vmem_limit_bytes=VMEM_LIMIT),
        cost_estimate=pl.CostEstimate(flops=cost, bytes_accessed=1000, transcendentals=0),
        name="lag_" + which,
    )(*operands, table, *prior, *after)


def place(near, inside, across):
    count = len(inside)
    begins = [[begin for _, begin in terms] for terms in (inside, across)]
    kinds = ("inside", "across")
    parts = LAGS // LANES
    tiles = near // 8

    def kernel(*refs):
        terms, out = (refs[:count], refs[count : 2 * count]), refs[2 * count]
        buffers, (stage, in_sems, out_sems) = refs[2 * count + 1 : 2 * count + 3], refs[2 * count + 3 :]
        loads, groups = {}, {}
        for tile in range(tiles):
            for kind in range(2):
                known = groups_of(near, kinds[kind])
                mine = [index for index, group in enumerate(known) if group[0] == tile]
                groups[tile, kind] = [(index, known[index][1]) for index in mine]
                if not mine:
                    continue
                span = pl.ds(mine[0], len(mine))
                for term in range(count):
                    loads[tile, kind, term] = pltpu.make_async_copy(
                        terms[kind][term].at[pl.ds(begins[kind][term] + mine[0], len(mine))], buffers[kind].at[term, span], in_sems.at[tile, kind, term]
                    )
                    loads[tile, kind, term].start()
        stores = []
        for tile in range(tiles):
            for kind in range(2):
                for term in range(count):
                    if (tile, kind, term) in loads:
                        loads[tile, kind, term].wait()
                for index, offset in groups[tile, kind]:
                    value = buffers[kind][0, index]
                    for term in range(1, count):
                        value = value + buffers[kind][term, index]
                    for part in range(parts):
                        stage[part, pl.ds(8 * tile * near + offset - 1, 8, stride=near), :] = value[
                            :, LANES * part : LANES * part + LANES
                        ]
            for part in range(parts):
                stores.append(
                    pltpu.make_async_copy(
                        stage.at[part].reshape(near, near, LANES).at[pl.ds(8 * tile, 8)],
                        out.at[pl.ds(8 * tile, 8), :, pl.ds(LANES * part, LANES)],
                        out_sems.at[tile, part],
                    )
                )
                stores[-1].start()
        for store in stores:
            store.wait()

    far_memory = pl.BlockSpec(memory_space=pltpu.HBM)
    return pl.pallas_call(
        kernel,
        in_specs=[far_memory] * (2 * count),
        out_specs=far_memory,
        out_shape=jax.ShapeDtypeStruct((near, near, LAGS), jnp.float32),
        scratch_shapes=[pltpu.VMEM((count, len(groups_of(near, kind)), 8, LAGS), jnp.float32) for kind in kinds]
        + [
            pltpu.VMEM((parts, near * near, LANES), jnp.float32),
            pltpu.SemaphoreType.DMA((tiles, 2, count)),
            pltpu.SemaphoreType.DMA((tiles, parts)),
        ],
        compiler_params=pltpu.CompilerParams(vmem_limit_bytes=VMEM_LIMIT),
        cost_estimate=pl.CostEstimate(flops=COST, bytes_accessed=1000, transcendentals=0),
        name="place",
    )(*[value for value, _ in inside + across])


def shifted(value, steps):
    count = lax.axis_size("fibre")
    return lax.ppermute(value, "fibre", [(source, source + steps) for source in range(max(0, -steps), count)])


def line_of_four(traces):
    channels, segs, win = traces.shape
    tables = make_tables(win, LAGS, segs * 4)
    blocks = traces.reshape(4, NEAR, segs, win)
    fibres = lax.axis_size("fibre")

    def outer(value):
        return lax.ppermute(value, "tm", [(0, 1), (3, 2)])

    def outer_next(value):
        pairs = [(4 * fibre + 4, 4 * fibre + 1) for fibre in range(fibres - 1)]
        pairs += [(4 * fibre + 3, 4 * fibre + 2) for fibre in range(fibres)]
        return lax.ppermute(value, ("fibre", "tm"), pairs)

    def middle(value):
        return lax.ppermute(value, "tm", [(1, 2), (2, 1)])

    def inner(value):
        return lax.ppermute(value, "tm", [(1, 0), (2, 3)])

    (far,) = whiten_first(blocks, tables)
    e1 = outer(far)
    *own, next_far, last = whiten_first(blocks, tables, far)
    e2 = outer_next(next_far)
    own.append(shifted(own[0], -1))
    e3 = outer(own[2])

    role = lambda z: jnp.where(z < 2, 0, 1)
    jobs = functools.partial(lag_sums, tables=tables, inner=True)
    back_in = jobs("inside", [([own[0], own[3]], None)], role=role, cost=1_000_000)
    m1 = jobs("inside", [([own[3], own[0]], None), ([e1], None)], role=role, after=[back_in])
    m1_in = middle(m1)
    base = jobs("across", [([own[3], own[0]], [own[4], own[1]])], role=role, after=[m1])
    m2 = jobs("across", [([e1], [e2])], prior=[base])
    m2_in = middle(m2)
    m1_in, _ = lax.optimization_barrier((m1_in, m2))
    first = m1_in + back_in
    i1 = inner(first)
    last, _ = lax.optimization_barrier((last, first))
    e4 = outer(last)
    m3 = jobs("all", [([own[2], own[1]], [own[3], own[2]]), ([e3, e2], [e1, e3])], role=role, after=[first])
    m3_in = middle(m3)
    back_out = jobs("across", [([own[0], own[3]], [own[1], own[4]])], role=role, after=[m3])
    m2_in, _ = lax.optimization_barrier((m2_in, back_out))
    second = m2_in + back_out
    i2 = inner(second)
    near = lag_sums(
        "all", [(own[:4], own[1:]), ([e4, e4, e3, e4], [e3, e3, e4, e3])], tables, lambda z: z, after=[second]
    )
    start = m1.shape[0]
    return place(NEAR, [(near, 0), (i1, 0), (m3_in, 0)], [(near, start), (i2, 0), (m3_in, start)])


def any_line(traces):
    channels, segs, win = traces.shape
    tables = make_tables(win, LAGS, segs * lax.axis_size("tm"))
    count = channels // NEAR
    blocks = traces.reshape(count, NEAR, segs, win)
    halo = shifted(blocks[0], -1)
    spectra = whiten(blocks, tables, count) + whiten(halo[None], tables, 1)
    start = len(groups_of(NEAR, "inside"))
    pieces = []
    for index in range(count):
        sums = lag_sums("all", [([spectra[index]], [spectra[index + 1]])], tables)
        pieces.append(place(NEAR, [(sums, 0)], [(sums, start)]))
    return lax.psum_scatter(jnp.concatenate(pieces, axis=0), "tm", scatter_dimension=0, tiled=True)


def shards(traces):
    if lax.axis_size("tm") == 4 and traces.shape[0] == 4 * NEAR:
        return line_of_four(traces)
    return any_line(traces)


def solution(mesh):
    in_specs = (P("fibre", "tm", None),)
    out_specs = P(("fibre", "tm"), None, None)
    return jax.shard_map(shards, mesh=mesh, in_specs=in_specs, out_specs=out_specs, check_vma=False)
```

time: 99.4 us -> 80.4 us (0.81)
  Pallas kernels: 50.3 us -> 19.3 us
  starting transfers between devices: 28.6 us -> 37.7 us
  waiting for transfers between devices: 13.6 us -> 18.5 us
  local copies, waits for them, and re-layouts: 4.44 us -> 0 us
  other arithmetic: 1.31 us -> 4.19 us
    pallas_call x11 -> x10, Pallas kernels: 50.3 us -> 19.3 us  [the longest x2 8.76 us: whiten_first(): pl.pallas_call(kernel, in_specs=[far_memory] * (3 + len(passed)), out_spe...]
    ppermute x3, starting transfers between devices: 20.9 us -> 27.8 us  [outer(): return lax.ppermute(value, 'tm', [(0, 1), (3, 2)])]
    ppermute x3, waiting for transfers between devices: 0.63 us -> 4.85 us  [outer(): return lax.ppermute(value, 'tm', [(0, 1), (3, 2)])]
    unnamed x22 -> x0, local copies, waits for them, and re-layouts: 3.36 us -> none
    add x2, other arithmetic: 1.23 us -> 4.19 us  [the longest x1 2.22 us: line_of_four(): second = m2_in + back_out]
    ppermute x4 -> x3, starting transfers between devices: 2.78 us -> 4.6 us  [middle(): return lax.ppermute(value, 'tm', [(1, 2), (2, 1)])]
    slice x1 -> x0, local copies, waits for them, and re-layouts: 1.08 us -> none  [line_of_four(): halo = shifted(blocks[0], -1)]
  transfers between devices with their start and end apart: 11 -> 10, of which waited for: 2 -> 3; matrix products, arithmetic and copies ran while one was open for 1% -> 5% of each run, Pallas kernels for 47% -> 16%
where the time goes in v4:
time: 80.4 us; the launch traced here: 79.9 us
  starting transfers between devices  37.7 us (47%)
  Pallas kernels  19.3 us (24%)
  waiting for transfers between devices  18.5 us (23%)
  other arithmetic  4.19 us (5%)
    ppermute x3, starting transfers between devices, outer(): return lax.ppermute(value, 'tm', [(0, 1), (3, 2)])  27.8 us
    ppermute x2, waiting for transfers between devices, inner(): return lax.ppermute(value, 'tm', [(1, 0), (2, 3)])  13.6 us
    pallas_call x2, Pallas kernels, whiten_first(): pl.pallas_call(kernel, in_specs=[far_memory] * (3 + len(passed)), out_spe...  8.76 us
    pallas_call x7, Pallas kernels, lag_sums(): pl.pallas_call(kernel, in_specs=[far_memory] * (len(operands) + 1 + len(p...  7.39 us
    ppermute x3, waiting for transfers between devices, outer(): return lax.ppermute(value, 'tm', [(0, 1), (3, 2)])  4.85 us
    ppermute x3, starting transfers between devices, middle(): return lax.ppermute(value, 'tm', [(1, 2), (2, 1)])  4.6 us
    pallas_call x1, Pallas kernels, place(): pl.pallas_call(kernel, in_specs=[far_memory] * (2 * count), out_specs=far...  3.14 us
    ppermute x2, starting transfers between devices, inner(): return lax.ppermute(value, 'tm', [(1, 0), (2, 3)])  2.56 us
  transfers between devices with their start and end apart: 10, of which 3 were waited for; matrix products, arithmetic and copies ran while one was open for 5% of the time, Pallas kernels for 16%

profile of v4, /device:TPU:0, one launch (start us, length us, event | category | flops | bytes accessed | tf_op | source)
XLA Modules:
  0.0 79.9 jit_solution(7295392290488310812)
XLA Ops:
  0.0 3.2 %whiten_first.1.refs_3_ = f32[2,2,8,32,128]{4,3,2,1,0:T(8,128)} custom-call(f32[4,32,8,512]{3,2,1,0:T(8,128)} %bitcast.1, f32[8,512]{1,0:T(8,128)} %constant.6.clone.refs_1_, bf16[3,768,256]{2,1,0:T(8,128)(2,1)} %constant.7.clone.refs_2_), custom_call_target="tpu_custom_call" | custom-call | flops 10000000000 | bytes 1000 | tf_op jit(solution)/shard_map/whiten_first/pallas_call | solution.py:204
  3.2 2.7 %collective-permute-start.1 = (f32[2,2,8,32,128]{4,3,2,1,0:T(8,128)}, f32[2,2,8,32,128]{4,3,2,1,0:T(8,128)}, u32[]{:S(2)}, u32[]{:S(2)}) collective-permute-start(f32[2,2,8,32,128]{4,3,2,1,0:T(8,128)} %whiten_first.1.refs_3_), channel_id=1, source_target_pairs={{0,1},{3,2},{4,5},{7,6},{8,9},{11,10},{12,13},{15,14},{16,17},{19,... | collective-permute-start | bytes 1572872 | tf_op jit(solution)/shard_map/ppermute | solution.py:451
  5.9 5.6 %whiten_rest.1 = (f32[2,2,8,32,128]{4,3,2,1,0:T(8,128)}, f32[2,2,8,32,128]{4,3,2,1,0:T(8,128)}, f32[2,2,8,32,128]{4,3,2,1,0:T(8,128)}, f32[2,2,8,32,128]{4,3,2,1...) custom-call(f32[4,32,8,512]{3,2,1,0:T(8,128)} %bitcast.2, f32[8,512]{1,0:T(8,128)} %constant.6.clone.refs_1_, ...), custom_call_target="tpu_custom_call" | custom-call | flops 10000000000 | bytes 1000 | tf_op jit(solution)/shard_map/whiten_rest/pallas_call | solution.py:204
  11.5 1.3 %collective-permute-start = (f32[2,2,8,32,128]{4,3,2,1,0:T(8,128)}, f32[2,2,8,32,128]{4,3,2,1,0:T(8,128)}, u32[]{:S(2)}, u32[]{:S(2)}) collective-permute-start(f32[2,2,8,32,128]{4,3,2,1,0:T(8,128)} %get-tuple-element.14.refs_0_.refs_1_), channel_id=1, source_target_pairs={{4,0},{8,4},{12,8},{16,12},{20,16},{24,20},{28,24},{5,1},{9,5},{13... | collective-permute-start | bytes 1572872 | tf_op jit(solution)/shard_map/ppermute | solution.py:441
  12.8 1.4 %collective-permute-start.3 = (f32[2,2,8,32,128]{4,3,2,1,0:T(8,128)}, f32[2,2,8,32,128]{4,3,2,1,0:T(8,128)}, u32[]{:S(2)}, u32[]{:S(2)}) collective-permute-start(f32[2,2,8,32,128]{4,3,2,1,0:T(8,128)} %get-tuple-element.19), channel_id=1, source_target_pairs={{4,1},{8,5},{12,9},{16,13},{20,17},{24,21},{28,25},{3,2},{7,6},{11... | collective-permute-start | bytes 1572872 | tf_op jit(solution)/shard_map/ppermute | solution.py:456
  14.2 2.1 %collective-permute-start.5 = (f32[2,2,8,32,128]{4,3,2,1,0:T(8,128)}, f32[2,2,8,32,128]{4,3,2,1,0:T(8,128)}, u32[]{:S(2)}, u32[]{:S(2)}) collective-permute-start(f32[2,2,8,32,128]{4,3,2,1,0:T(8,128)} %get-tuple-element.16.refs_0_.refs_2_), channel_id=1, source_target_pairs={{0,1},{3,2},{4,5},{7,6},{8,9},{11,10},{12,13},{15,14},{16,17},{19,... | collective-permute-start | bytes 1572872 | tf_op jit(solution)/shard_map/ppermute | solution.py:451
  16.4 1.3 %collective-permute-done.1.refs_2_.refs_0_.refs_5_ = f32[2,2,8,32,128]{4,3,2,1,0:T(8,128)} collective-permute-done((f32[2,2,8,32,128]{4,3,2,1,0:T(8,128)}, f32[2,2,8,32,128]{4,3,2,1,0:T(8,128)}, u32[]{:S(2)}, u32[]{:S(2)}) %collective-permute-start.1) | collective-permute-done | bytes 524320 | tf_op jit(solution)/shard_map/ppermute | solution.py:451
  17.7 0.1 lag_inside.3.refs_5_
  17.8 1.4 %collective-permute-start.2 = (f32[48,8,256]{2,1,0:T(8,128)}, f32[48,8,256]{2,1,0:T(8,128)}, u32[]{:S(2)}, u32[]{:S(2)}) collective-permute-start(f32[48,8,256]{2,1,0:T(8,128)} %lag_inside.3.refs_5_), channel_id=1, source_target_pairs={{1,2},{2,1},{5,6},{6,5},{9,10},{10,9},{13,14},{14,13},{17,18},{18,... | collective-permute-start | bytes 1179656 | tf_op jit(solution)/shard_map/ppermute | solution.py:459
  19.2 0.1 lag_across.3.refs_3_
  19.3 0.1 lag_across.4
  19.4 1.5 %collective-permute-start.6 = (f32[80,8,256]{2,1,0:T(8,128)}, f32[80,8,256]{2,1,0:T(8,128)}, u32[]{:S(2)}, u32[]{:S(2)}) collective-permute-start(f32[80,8,256]{2,1,0:T(8,128)} %lag_across.4), channel_id=1, source_target_pairs={{1,2},{2,1},{5,6},{6,5},{9,10},{10,9},{13,14},{14,13},{17,18},{18,... | collective-permute-start | bytes 1966088 | tf_op jit(solution)/shard_map/ppermute | solution.py:459
  21.0 2.0 %add.6.refs_7_ = f32[48,8,256]{2,1,0:T(8,128)} add(f32[48,8,256]{2,1,0:T(8,128)} %collective-permute-done.2, f32[48,8,256]{2,1,0:T(8,128)} %lag_inside.2.refs_4_) | non-fusion elementwise | flops 98304 | bytes 1179648 | tf_op jit(solution)/shard_map/add | solution.py:480
  23.0 1.3 %collective-permute-start.7 = (f32[48,8,256]{2,1,0:T(8,128)}, f32[48,8,256]{2,1,0:T(8,128)}, u32[]{:S(2)}, u32[]{:S(2)}) collective-permute-start(f32[48,8,256]{2,1,0:T(8,128)} %add.6.refs_7_), channel_id=1, source_target_pairs={{1,0},{2,3},{5,4},{6,7},{9,8},{10,11},{13,12},{14,15},{17,16},{18,... | collective-permute-start | bytes 1179656 | tf_op jit(solution)/shard_map/ppermute | solution.py:462
  24.2 23.0 %collective-permute-start.4 = (f32[2,2,8,32,128]{4,3,2,1,0:T(8,128)}, f32[2,2,8,32,128]{4,3,2,1,0:T(8,128)}, u32[]{:S(2)}, u32[]{:S(2)}) collective-permute-start(f32[2,2,8,32,128]{4,3,2,1,0:T(8,128)} %get-tuple-element.21), channel_id=1, source_target_pairs={{0,1},{3,2},{4,5},{7,6},{8,9},{11,10},{12,13},{15,14},{16,17},{19,... | collective-permute-start | bytes 1572872 | tf_op jit(solution)/shard_map/ppermute | solution.py:451
  47.3 0.2 lag_all.2.refs_5_
  47.4 1.6 %collective-permute-start.8 = (f32[128,8,256]{2,1,0:T(8,128)}, f32[128,8,256]{2,1,0:T(8,128)}, u32[]{:S(2)}, u32[]{:S(2)}) collective-permute-start(f32[128,8,256]{2,1,0:T(8,128)} %lag_all.2.refs_5_), channel_id=1, source_target_pairs={{1,2},{2,1},{5,6},{6,5},{9,10},{10,9},{13,14},{14,13},{17,18},{18,... | collective-permute-start | bytes 3145736 | tf_op jit(solution)/shard_map/ppermute | solution.py:459
  49.1 0.1 lag_across.5
  49.2 2.2 %add.7.refs_8_ = f32[80,8,256]{2,1,0:T(8,128)} add(f32[80,8,256]{2,1,0:T(8,128)} %collective-permute-done.6, f32[80,8,256]{2,1,0:T(8,128)} %lag_across.5) | non-fusion elementwise | flops 163840 | bytes 1966080 | tf_op jit(solution)/shard_map/add | solution.py:488
  51.4 1.3 %collective-permute-start.9 = (f32[80,8,256]{2,1,0:T(8,128)}, f32[80,8,256]{2,1,0:T(8,128)}, u32[]{:S(2)}, u32[]{:S(2)}) collective-permute-start(f32[80,8,256]{2,1,0:T(8,128)} %add.7.refs_8_), channel_id=1, source_target_pairs={{1,0},{2,3},{5,4},{6,7},{9,8},{10,11},{13,12},{14,15},{17,16},{18,... | collective-permute-start | bytes 1966088 | tf_op jit(solution)/shard_map/ppermute | solution.py:462
  52.7 3.6 %collective-permute-done.4.refs_5_ = f32[2,2,8,32,128]{4,3,2,1,0:T(8,128)} collective-permute-done((f32[2,2,8,32,128]{4,3,2,1,0:T(8,128)}, f32[2,2,8,32,128]{4,3,2,1,0:T(8,128)}, u32[]{:S(2)}, u32[]{:S(2)}) %collective-permute-start.4) | collective-permute-done | bytes 524320 | tf_op jit(solution)/shard_map/ppermute | solution.py:451
  56.3 6.7 %lag_all.3.refs_0_.refs_3_ = f32[128,8,256]{2,1,0:T(8,128)} custom-call(f32[2,2,8,32,128]{4,3,2,1,0:T(8,128)} %get-tuple-element.14.refs_0_.refs_1_, f32[2,2,8,32,128]{4,3,2,1,0:T(8,128)} %get-tuple-element.15.refs_3_.refs_1_.refs_2_, f32[2,2,8,32,128]{4,3,2,1,0:T(8,128)} %get-tuple-element.16.refs_0_.refs_2_, ...), custom_call_target="tpu_custom_call" | custom-call | flops 10000000000 | bytes 1000 | tf_op jit(solution)/shard_map/lag_all/pallas_call | solution.py:350
  63.0 13.6 %collective-permute-done.9.refs_4_ = f32[80,8,256]{2,1,0:T(8,128)} collective-permute-done((f32[80,8,256]{2,1,0:T(8,128)}, f32[80,8,256]{2,1,0:T(8,128)}, u32[]{:S(2)}, u32[]{:S(2)}) %collective-permute-start.9) | collective-permute-done | bytes 655392 | tf_op jit(solution)/shard_map/ppermute | solution.py:462
  76.6 3.1 %place.1 = f32[32,32,256]{2,1,0:T(8,128)} custom-call(f32[128,8,256]{2,1,0:T(8,128)} %lag_all.3.refs_0_.refs_3_, f32[48,8,256]{2,1,0:T(8,128)} %collective-permute-done.7.refs_1_, f32[128,8,256]{2,1,0:T(8,128)} %collective-permute-done.8.refs_2_.refs_5_, f32[128,8,256]{2,1,0:T(8,128)} %lag_all.3.refs_0_.refs_3_, ...), custom_call_target="tpu_custom_call" | custom-call | flops 10000000000 | bytes 1000 | tf_op jit(solution)/shard_map/place/pallas_call | solution.py:422
  (8 shorter events, 0.1 us)
Async XLA Ops:
  3.2 14.5 %collective-permute-start.1 = (f32[2,2,8,32,128]{4,3,2,1,0:T(8,128)}, f32[2,2,8,32,128]{4,3,2,1,0:T(8,128)}, u32[]{:S(2)}, u32[]{:S(2)}) collective-permute-start(f32[2,2,8,32,128]{4,3,2,1,0:T(8,128)} %whiten_first.1.refs_3_), channel_id=1, source_target_pairs={{0,1},{3,2},{4,5},{7,6},{8,9},{11,10},{12,13},{15,14},{16,17},{19,... | collective-permute-start | bytes 1572872 | tf_op jit(solution)/shard_map/ppermute | solution.py:451
  11.5 7.7 %collective-permute-start = (f32[2,2,8,32,128]{4,3,2,1,0:T(8,128)}, f32[2,2,8,32,128]{4,3,2,1,0:T(8,128)}, u32[]{:S(2)}, u32[]{:S(2)}) collective-permute-start(f32[2,2,8,32,128]{4,3,2,1,0:T(8,128)} %get-tuple-element.14.refs_0_.refs_1_), channel_id=1, source_target_pairs={{4,0},{8,4},{12,8},{16,12},{20,16},{24,20},{28,24},{5,1},{9,5},{13... | collective-permute-start | bytes 1572872 | tf_op jit(solution)/shard_map/ppermute | solution.py:441
  12.8 6.5 %collective-permute-start.3 = (f32[2,2,8,32,128]{4,3,2,1,0:T(8,128)}, f32[2,2,8,32,128]{4,3,2,1,0:T(8,128)}, u32[]{:S(2)}, u32[]{:S(2)}) collective-permute-start(f32[2,2,8,32,128]{4,3,2,1,0:T(8,128)} %get-tuple-element.19), channel_id=1, source_target_pairs={{4,1},{8,5},{12,9},{16,13},{20,17},{24,21},{28,25},{3,2},{7,6},{11... | collective-permute-start | bytes 1572872 | tf_op jit(solution)/shard_map/ppermute | solution.py:456
  14.2 33.1 %collective-permute-start.5 = (f32[2,2,8,32,128]{4,3,2,1,0:T(8,128)}, f32[2,2,8,32,128]{4,3,2,1,0:T(8,128)}, u32[]{:S(2)}, u32[]{:S(2)}) collective-permute-start(f32[2,2,8,32,128]{4,3,2,1,0:T(8,128)} %get-tuple-element.16.refs_0_.refs_2_), channel_id=1, source_target_pairs={{0,1},{3,2},{4,5},{7,6},{8,9},{11,10},{12,13},{15,14},{16,17},{19,... | collective-permute-start | bytes 1572872 | tf_op jit(solution)/shard_map/ppermute | solution.py:451
  17.8 3.2 %collective-permute-start.2 = (f32[48,8,256]{2,1,0:T(8,128)}, f32[48,8,256]{2,1,0:T(8,128)}, u32[]{:S(2)}, u32[]{:S(2)}) collective-permute-start(f32[48,8,256]{2,1,0:T(8,128)} %lag_inside.3.refs_5_), channel_id=1, source_target_pairs={{1,2},{2,1},{5,6},{6,5},{9,10},{10,9},{13,14},{14,13},{17,18},{18,... | collective-permute-start | bytes 1179656 | tf_op jit(solution)/shard_map/ppermute | solution.py:459
  19.4 29.8 %collective-permute-start.6 = (f32[80,8,256]{2,1,0:T(8,128)}, f32[80,8,256]{2,1,0:T(8,128)}, u32[]{:S(2)}, u32[]{:S(2)}) collective-permute-start(f32[80,8,256]{2,1,0:T(8,128)} %lag_across.4), channel_id=1, source_target_pairs={{1,2},{2,1},{5,6},{6,5},{9,10},{10,9},{13,14},{14,13},{17,18},{18,... | collective-permute-start | bytes 1966088 | tf_op jit(solution)/shard_map/ppermute | solution.py:459
  23.0 40.1 %collective-permute-start.7 = (f32[48,8,256]{2,1,0:T(8,128)}, f32[48,8,256]{2,1,0:T(8,128)}, u32[]{:S(2)}, u32[]{:S(2)}) collective-permute-start(f32[48,8,256]{2,1,0:T(8,128)} %add.6.refs_7_), channel_id=1, source_target_pairs={{1,0},{2,3},{5,4},{6,7},{9,8},{10,11},{13,12},{14,15},{17,16},{18,... | collective-permute-start | bytes 1179656 | tf_op jit(solution)/shard_map/ppermute | solution.py:462
  24.2 32.1 %collective-permute-start.4 = (f32[2,2,8,32,128]{4,3,2,1,0:T(8,128)}, f32[2,2,8,32,128]{4,3,2,1,0:T(8,128)}, u32[]{:S(2)}, u32[]{:S(2)}) collective-permute-start(f32[2,2,8,32,128]{4,3,2,1,0:T(8,128)} %get-tuple-element.21), channel_id=1, source_target_pairs={{0,1},{3,2},{4,5},{7,6},{8,9},{11,10},{12,13},{15,14},{16,17},{19,... | collective-permute-start | bytes 1572872 | tf_op jit(solution)/shard_map/ppermute | solution.py:451
  47.4 29.2 %collective-permute-start.8 = (f32[128,8,256]{2,1,0:T(8,128)}, f32[128,8,256]{2,1,0:T(8,128)}, u32[]{:S(2)}, u32[]{:S(2)}) collective-permute-start(f32[128,8,256]{2,1,0:T(8,128)} %lag_all.2.refs_5_), channel_id=1, source_target_pairs={{1,2},{2,1},{5,6},{6,5},{9,10},{10,9},{13,14},{14,13},{17,18},{18,... | collective-permute-start | bytes 3145736 | tf_op jit(solution)/shard_map/ppermute | solution.py:459
  51.4 25.2 %collective-permute-start.9 = (f32[80,8,256]{2,1,0:T(8,128)}, f32[80,8,256]{2,1,0:T(8,128)}, u32[]{:S(2)}, u32[]{:S(2)}) collective-permute-start(f32[80,8,256]{2,1,0:T(8,128)} %add.7.refs_8_), channel_id=1, source_target_pairs={{1,0},{2,3},{5,4},{6,7},{9,8},{10,11},{13,12},{14,15},{17,16},{18,... | collective-permute-start | bytes 1966088 | tf_op jit(solution)/shard_map/ppermute | solution.py:462

commit v5 on v4

--- a/solution.py
+++ b/solution.py
@@ -57,7 +57,7 @@
     parts = win // LANES
     for part in range(parts):
         lanes = slice(LANES * part, LANES * part + LANES)
-        stage[part] = x_ref[:, :, lanes].reshape(channels * segs, LANES)
+        stage[part, pl.ds(0, channels * segs)] = x_ref[:, :, lanes].reshape(channels * segs, LANES)
     pieces = []
     for s in range(segs):
         pieces.append([
@@ -187,14 +187,27 @@
 
             @pl.when(end)
             def _():
-                load = pltpu.make_async_copy(x_any.at[jnp.where(z < 2, 3, 0)], blocks_in.at[4], sems.at[6])
-                load.start()
-                for tab in load_tables():
+                place = jnp.where(z < 2, 3, 0)
+                step = near // 2
+                spans = [pl.ds(0, step), pl.ds(step, step)]
+                loads = [
+                    pltpu.make_async_copy(x_any.at[place, span], blocks_in.at[4, span], sems.at[index])
+                    for index, span in enumerate(spans)
+                ]
+                loads[0].start()
+                tabs = load_tables()
+                loads[1].start()
+                for tab in tabs:
                     tab.wait()
-                one(load, 4)
-                store = pltpu.make_async_copy(blocks_out.at[4], outs[0], out_sems.at[6])
-                store.start()
-                store.wait()
+                stores = []
+                for index, span in enumerate(spans):
+                    loads[index].wait()
+                    target = blocks_out.at[4, :, :, :, span]
+                    whiten_block(blocks_in.at[4, span], hann, forward, target, stage)
+                    stores.append(pltpu.make_async_copy(target, outs[0].at[:, :, :, span], out_sems.at[index]))
+                    stores[-1].start()
+                for store in stores:
+                    store.wait()
 
         else:
             all_four(load_tables())
@@ -314,9 +327,8 @@
                         def _():
                             copy(number, side, half, place).start()
 
-            if half == 0:
-                table_copy = pltpu.make_async_copy(table_any, table_ref, table_sem)
-                table_copy.start()
+        table_copy = pltpu.make_async_copy(table_any, table_ref, table_sem)
+        table_copy.start()
         if prior:
             prior_copy = pltpu.make_async_copy(priors[0], result, prior_sem)
             prior_copy.start()
@@ -370,14 +382,18 @@
 
 def place(near, inside, across):
     count = len(inside)
-    begins = [[begin for _, begin in terms] for terms in (inside, across)]
+    terms = [[term if isinstance(term, list) else [term] for term in kind] for kind in (inside, across)]
+    operands = [value for kind in terms for term in kind for value, _ in term]
     kinds = ("inside", "across")
     parts = LAGS // LANES
     tiles = near // 8
 
     def kernel(*refs):
-        terms, out = (refs[:count], refs[count : 2 * count]), refs[2 * count]
-        buffers, (stage, in_sems, out_sems) = refs[2 * count + 1 : 2 * count + 3], refs[2 * count + 3 :]
+        given, refs = list(refs[: len(operands)]), refs[len(operands) :]
+        sources = [[[(given.pop(0), begin) for _, begin in term] for term in kind] for kind in terms]
+        out, buffers, (stage, in_sems, out_sems) = refs[0], refs[1:3], refs[3:]
+        z = lax.axis_index("tm")
+        end = (z == 0) | (z == 3)
         loads, groups = {}, {}
         for tile in range(tiles):
             for kind in range(2):
@@ -388,10 +404,20 @@
                     continue
                 span = pl.ds(mine[0], len(mine))
                 for term in range(count):
-                    loads[tile, kind, term] = pltpu.make_async_copy(
-                        terms[kind][term].at[pl.ds(begins[kind][term] + mine[0], len(mine))], buffers[kind].at[term, span], in_sems.at[tile, kind, term]
-                    )
-                    loads[tile, kind, term].start()
+                    copies = [
+                        pltpu.make_async_copy(
+                            value.at[pl.ds(begin + mine[0], len(mine))],
+                            buffers[kind].at[term, span],
+                            in_sems.at[tile, kind, term],
+                        )
+                        for value, begin in sources[kind][term]
+                    ]
+                    loads[tile, kind, term] = copies[0]
+                    if len(copies) == 1:
+                        copies[0].start()
+                    else:
+                        pl.when(end)(copies[0].start)
+                        pl.when(jnp.logical_not(end))(copies[1].start)
         stores = []
         for tile in range(tiles):
             for kind in range(2):
@@ -421,7 +447,7 @@
     far_memory = pl.BlockSpec(memory_space=pltpu.HBM)
     return pl.pallas_call(
         kernel,
-        in_specs=[far_memory] * (2 * count),
+        in_specs=[far_memory] * len(operands),
         out_specs=far_memory,
         out_shape=jax.ShapeDtypeStruct((near, near, LAGS), jnp.float32),
         scratch_shapes=[pltpu.VMEM((count, len(groups_of(near, kind)), 8, LAGS), jnp.float32) for kind in kinds]
@@ -433,7 +459,7 @@
         compiler_params=pltpu.CompilerParams(vmem_limit_bytes=VMEM_LIMIT),
         cost_estimate=pl.CostEstimate(flops=COST, bytes_accessed=1000, transcendentals=0),
         name="place",
-    )(*[value for value, _ in inside + across])
+    )(*operands)
 
 
 def shifted(value, steps):
@@ -483,15 +509,13 @@
     e4 = outer(last)
     m3 = jobs("all", [([own[2], own[1]], [own[3], own[2]]), ([e3, e2], [e1, e3])], role=role, after=[first])
     m3_in = middle(m3)
-    back_out = jobs("across", [([own[0], own[3]], [own[1], own[4]])], role=role, after=[m3])
-    m2_in, _ = lax.optimization_barrier((m2_in, back_out))
-    second = m2_in + back_out
+    second = jobs("across", [([own[0], own[3]], [own[1], own[4]])], role=role, prior=[m2_in], after=[m3])
     i2 = inner(second)
     near = lag_sums(
         "all", [(own[:4], own[1:]), ([e4, e4, e3, e4], [e3, e3, e4, e3])], tables, lambda z: z, after=[second]
     )
     start = m1.shape[0]
-    return place(NEAR, [(near, 0), (i1, 0), (m3_in, 0)], [(near, start), (i2, 0), (m3_in, start)])
+    return place(NEAR, [(near, 0), [(i1, 0), (m3_in, 0)]], [(near, start), [(i2, 0), (m3_in, start)]])
 
 
 def any_line(traces):

time: 80.4 us -> 78.6 us (0.978)
  other arithmetic: 4.19 us -> 1.97 us
    add x1 -> x0, other arithmetic: 2.22 us -> none  [line_of_four(): second = m2_in + back_out]
    ppermute x3, waiting for transfers between devices: 4.85 us -> 7.06 us  [outer(): return lax.ppermute(value, 'tm', [(0, 1), (3, 2)])]
    ppermute x2, waiting for transfers between devices: 13.6 us -> 11.7 us  [inner(): return lax.ppermute(value, 'tm', [(1, 0), (2, 3)])]
  transfers between devices with their start and end apart: 10 -> 10, of which waited for: 3 -> 3; matrix products, arithmetic and copies ran while one was open for 5% -> 3% of each run, Pallas kernels for 16% -> 17%
where the time goes in v5:
time: 78.6 us; the launch traced here: 77.8 us
  starting transfers between devices  37.7 us (48%)
  Pallas kernels  19.1 us (24%)
  waiting for transfers between devices  18.8 us (24%)
  other arithmetic  1.97 us (3%)
    ppermute x3, starting transfers between devices, outer(): return lax.ppermute(value, 'tm', [(0, 1), (3, 2)])  27.8 us
    ppermute x2, waiting for transfers between devices, inner(): return lax.ppermute(value, 'tm', [(1, 0), (2, 3)])  11.7 us
    pallas_call x2, Pallas kernels, whiten_first(): pl.pallas_call(kernel, in_specs=[far_memory] * (3 + len(passed)), out_spe...  8.77 us
    pallas_call x7, Pallas kernels, lag_sums(): pl.pallas_call(kernel, in_specs=[far_memory] * (len(operands) + 1 + len(p...  7.42 us
    ppermute x3, waiting for transfers between devices, outer(): return lax.ppermute(value, 'tm', [(0, 1), (3, 2)])  7.06 us
    ppermute x3, starting transfers between devices, middle(): return lax.ppermute(value, 'tm', [(1, 2), (2, 1)])  4.6 us
    pallas_call x1, Pallas kernels, place(): pl.pallas_call(kernel, in_specs=[far_memory] * len(operands), out_specs=f...  2.87 us
    ppermute x2, starting transfers between devices, inner(): return lax.ppermute(value, 'tm', [(1, 0), (2, 3)])  2.57 us
  transfers between devices with their start and end apart: 10, of which 3 were waited for; matrix products, arithmetic and copies ran while one was open for 3% of the time, Pallas kernels for 17%

profile of v5, /device:TPU:0, one launch (start us, length us, event | category | flops | bytes accessed | tf_op | source)
XLA Modules:
  0.0 77.8 jit_solution(7073419920922666689)
XLA Ops:
  0.0 3.2 %whiten_first.1.refs_3_ = f32[2,2,8,32,128]{4,3,2,1,0:T(8,128)} custom-call(f32[4,32,8,512]{3,2,1,0:T(8,128)} %bitcast.1, f32[8,512]{1,0:T(8,128)} %constant.6.clone.refs_1_, bf16[3,768,256]{2,1,0:T(8,128)(2,1)} %constant.7.clone.refs_2_), custom_call_target="tpu_custom_call" | custom-call | flops 10000000000 | bytes 1000 | tf_op jit(solution)/shard_map/whiten_first/pallas_call | solution.py:217
  3.2 2.6 %collective-permute-start.1 = (f32[2,2,8,32,128]{4,3,2,1,0:T(8,128)}, f32[2,2,8,32,128]{4,3,2,1,0:T(8,128)}, u32[]{:S(2)}, u32[]{:S(2)}) collective-permute-start(f32[2,2,8,32,128]{4,3,2,1,0:T(8,128)} %whiten_first.1.refs_3_), channel_id=1, source_target_pairs={{0,1},{3,2},{4,5},{7,6},{8,9},{11,10},{12,13},{15,14},{16,17},{19,... | collective-permute-start | bytes 1572872 | tf_op jit(solution)/shard_map/ppermute | solution.py:477
  5.9 5.6 %whiten_rest.1 = (f32[2,2,8,32,128]{4,3,2,1,0:T(8,128)}, f32[2,2,8,32,128]{4,3,2,1,0:T(8,128)}, f32[2,2,8,32,128]{4,3,2,1,0:T(8,128)}, f32[2,2,8,32,128]{4,3,2,1...) custom-call(f32[4,32,8,512]{3,2,1,0:T(8,128)} %bitcast.2, f32[8,512]{1,0:T(8,128)} %constant.6.clone.refs_1_, ...), custom_call_target="tpu_custom_call" | custom-call | flops 10000000000 | bytes 1000 | tf_op jit(solution)/shard_map/whiten_rest/pallas_call | solution.py:217
  11.4 1.4 %collective-permute-start.3 = (f32[2,2,8,32,128]{4,3,2,1,0:T(8,128)}, f32[2,2,8,32,128]{4,3,2,1,0:T(8,128)}, u32[]{:S(2)}, u32[]{:S(2)}) collective-permute-start(f32[2,2,8,32,128]{4,3,2,1,0:T(8,128)} %get-tuple-element.18), channel_id=1, source_target_pairs={{4,1},{8,5},{12,9},{16,13},{20,17},{24,21},{28,25},{3,2},{7,6},{11... | collective-permute-start | bytes 1572872 | tf_op jit(solution)/shard_map/ppermute | solution.py:482
  12.9 2.1 %collective-permute-start.5 = (f32[2,2,8,32,128]{4,3,2,1,0:T(8,128)}, f32[2,2,8,32,128]{4,3,2,1,0:T(8,128)}, u32[]{:S(2)}, u32[]{:S(2)}) collective-permute-start(f32[2,2,8,32,128]{4,3,2,1,0:T(8,128)} %get-tuple-element.15.refs_0_.refs_2_), channel_id=1, source_target_pairs={{0,1},{3,2},{4,5},{7,6},{8,9},{11,10},{12,13},{15,14},{16,17},{19,... | collective-permute-start | bytes 1572872 | tf_op jit(solution)/shard_map/ppermute | solution.py:477
  15.0 1.3 %collective-permute-start = (f32[2,2,8,32,128]{4,3,2,1,0:T(8,128)}, f32[2,2,8,32,128]{4,3,2,1,0:T(8,128)}, u32[]{:S(2)}, u32[]{:S(2)}) collective-permute-start(f32[2,2,8,32,128]{4,3,2,1,0:T(8,128)} %get-tuple-element.13.refs_0_.refs_1_), channel_id=1, source_target_pairs={{4,0},{8,4},{12,8},{16,12},{20,16},{24,20},{28,24},{5,1},{9,5},{13... | collective-permute-start | bytes 1572872 | tf_op jit(solution)/shard_map/ppermute | solution.py:467
  16.3 0.1 lag_inside.2.refs_4_
  16.4 1.3 %collective-permute-done.1.refs_2_.refs_0_.refs_5_ = f32[2,2,8,32,128]{4,3,2,1,0:T(8,128)} collective-permute-done((f32[2,2,8,32,128]{4,3,2,1,0:T(8,128)}, f32[2,2,8,32,128]{4,3,2,1,0:T(8,128)}, u32[]{:S(2)}, u32[]{:S(2)}) %collective-permute-start.1) | collective-permute-done | bytes 524320 | tf_op jit(solution)/shard_map/ppermute | solution.py:477
  17.6 0.1 lag_inside.3.refs_5_
  17.8 1.4 %collective-permute-start.2 = (f32[48,8,256]{2,1,0:T(8,128)}, f32[48,8,256]{2,1,0:T(8,128)}, u32[]{:S(2)}, u32[]{:S(2)}) collective-permute-start(f32[48,8,256]{2,1,0:T(8,128)} %lag_inside.3.refs_5_), channel_id=1, source_target_pairs={{1,2},{2,1},{5,6},{6,5},{9,10},{10,9},{13,14},{14,13},{17,18},{18,... | collective-permute-start | bytes 1179656 | tf_op jit(solution)/shard_map/ppermute | solution.py:485
  19.2 0.1 lag_across.3.refs_3_
  19.3 0.1 lag_across.4
  19.4 1.5 %collective-permute-start.6 = (f32[80,8,256]{2,1,0:T(8,128)}, f32[80,8,256]{2,1,0:T(8,128)}, u32[]{:S(2)}, u32[]{:S(2)}) collective-permute-start(f32[80,8,256]{2,1,0:T(8,128)} %lag_across.4), channel_id=1, source_target_pairs={{1,2},{2,1},{5,6},{6,5},{9,10},{10,9},{13,14},{14,13},{17,18},{18,... | collective-permute-start | bytes 1966088 | tf_op jit(solution)/shard_map/ppermute | solution.py:485
  21.0 2.0 %add.3.refs_7_ = f32[48,8,256]{2,1,0:T(8,128)} add(f32[48,8,256]{2,1,0:T(8,128)} %collective-permute-done.2, f32[48,8,256]{2,1,0:T(8,128)} %lag_inside.2.refs_4_) | non-fusion elementwise | flops 98304 | bytes 1179648 | tf_op jit(solution)/shard_map/add | solution.py:506
  22.9 1.3 %collective-permute-start.7 = (f32[48,8,256]{2,1,0:T(8,128)}, f32[48,8,256]{2,1,0:T(8,128)}, u32[]{:S(2)}, u32[]{:S(2)}) collective-permute-start(f32[48,8,256]{2,1,0:T(8,128)} %add.3.refs_7_), channel_id=1, source_target_pairs={{1,0},{2,3},{5,4},{6,7},{9,8},{10,11},{13,12},{14,15},{17,16},{18,... | collective-permute-start | bytes 1179656 | tf_op jit(solution)/shard_map/ppermute | solution.py:488
  24.2 23.1 %collective-permute-start.4 = (f32[2,2,8,32,128]{4,3,2,1,0:T(8,128)}, f32[2,2,8,32,128]{4,3,2,1,0:T(8,128)}, u32[]{:S(2)}, u32[]{:S(2)}) collective-permute-start(f32[2,2,8,32,128]{4,3,2,1,0:T(8,128)} %get-tuple-element.20), channel_id=1, source_target_pairs={{0,1},{3,2},{4,5},{7,6},{8,9},{11,10},{12,13},{15,14},{16,17},{19,... | collective-permute-start | bytes 1572872 | tf_op jit(solution)/shard_map/ppermute | solution.py:477
  47.3 0.2 lag_all.2.refs_6_
  47.5 1.6 %collective-permute-start.8 = (f32[128,8,256]{2,1,0:T(8,128)}, f32[128,8,256]{2,1,0:T(8,128)}, u32[]{:S(2)}, u32[]{:S(2)}) collective-permute-start(f32[128,8,256]{2,1,0:T(8,128)} %lag_all.2.refs_6_), channel_id=1, source_target_pairs={{1,2},{2,1},{5,6},{6,5},{9,10},{10,9},{13,14},{14,13},{17,18},{18,... | collective-permute-start | bytes 3145736 | tf_op jit(solution)/shard_map/ppermute | solution.py:485
  49.1 0.1 lag_across.5.refs_8_
  49.2 1.3 %collective-permute-start.9 = (f32[80,8,256]{2,1,0:T(8,128)}, f32[80,8,256]{2,1,0:T(8,128)}, u32[]{:S(2)}, u32[]{:S(2)}) collective-permute-start(f32[80,8,256]{2,1,0:T(8,128)} %lag_across.5.refs_8_), channel_id=1, source_target_pairs={{1,0},{2,3},{5,4},{6,7},{9,8},{10,11},{13,12},{14,15},{17,16},{18,... | collective-permute-start | bytes 1966088 | tf_op jit(solution)/shard_map/ppermute | solution.py:488
  50.5 5.8 %collective-permute-done.4.refs_5_ = f32[2,2,8,32,128]{4,3,2,1,0:T(8,128)} collective-permute-done((f32[2,2,8,32,128]{4,3,2,1,0:T(8,128)}, f32[2,2,8,32,128]{4,3,2,1,0:T(8,128)}, u32[]{:S(2)}, u32[]{:S(2)}) %collective-permute-start.4) | collective-permute-done | bytes 524320 | tf_op jit(solution)/shard_map/ppermute | solution.py:477
  56.3 6.7 %lag_all.3.refs_0_.refs_3_ = f32[128,8,256]{2,1,0:T(8,128)} custom-call(f32[2,2,8,32,128]{4,3,2,1,0:T(8,128)} %get-tuple-element.13.refs_0_.refs_1_, f32[2,2,8,32,128]{4,3,2,1,0:T(8,128)} %get-tuple-element.14.refs_3_.refs_1_.refs_2_, f32[2,2,8,32,128]{4,3,2,1,0:T(8,128)} %get-tuple-element.15.refs_0_.refs_2_, ...), custom_call_target="tpu_custom_call" | custom-call | flops 10000000000 | bytes 1000 | tf_op jit(solution)/shard_map/lag_all/pallas_call | solution.py:362
  63.1 11.7 %collective-permute-done.9.refs_4_ = f32[80,8,256]{2,1,0:T(8,128)} collective-permute-done((f32[80,8,256]{2,1,0:T(8,128)}, f32[80,8,256]{2,1,0:T(8,128)}, u32[]{:S(2)}, u32[]{:S(2)}) %collective-permute-start.9) | collective-permute-done | bytes 655392 | tf_op jit(solution)/shard_map/ppermute | solution.py:488
  74.8 2.9 %place.1 = f32[32,32,256]{2,1,0:T(8,128)} custom-call(f32[128,8,256]{2,1,0:T(8,128)} %lag_all.3.refs_0_.refs_3_, f32[48,8,256]{2,1,0:T(8,128)} %collective-permute-done.7.refs_1_, f32[128,8,256]{2,1,0:T(8,128)} %collective-permute-done.8.refs_2_.refs_5_, f32[128,8,256]{2,1,0:T(8,128)} %lag_all.3.refs_0_.refs_3_, ...), custom_call_target="tpu_custom_call" | custom-call | flops 10000000000 | bytes 1000 | tf_op jit(solution)/shard_map/place/pallas_call | solution.py:448
  (7 shorter events, 0.0 us)
Async XLA Ops:
  3.2 14.4 %collective-permute-start.1 = (f32[2,2,8,32,128]{4,3,2,1,0:T(8,128)}, f32[2,2,8,32,128]{4,3,2,1,0:T(8,128)}, u32[]{:S(2)}, u32[]{:S(2)}) collective-permute-start(f32[2,2,8,32,128]{4,3,2,1,0:T(8,128)} %whiten_first.1.refs_3_), channel_id=1, source_target_pairs={{0,1},{3,2},{4,5},{7,6},{8,9},{11,10},{12,13},{15,14},{16,17},{19,... | collective-permute-start | bytes 1572872 | tf_op jit(solution)/shard_map/ppermute | solution.py:477
  11.4 7.9 %collective-permute-start.3 = (f32[2,2,8,32,128]{4,3,2,1,0:T(8,128)}, f32[2,2,8,32,128]{4,3,2,1,0:T(8,128)}, u32[]{:S(2)}, u32[]{:S(2)}) collective-permute-start(f32[2,2,8,32,128]{4,3,2,1,0:T(8,128)} %get-tuple-element.18), channel_id=1, source_target_pairs={{4,1},{8,5},{12,9},{16,13},{20,17},{24,21},{28,25},{3,2},{7,6},{11... | collective-permute-start | bytes 1572872 | tf_op jit(solution)/shard_map/ppermute | solution.py:482
  12.9 34.4 %collective-permute-start.5 = (f32[2,2,8,32,128]{4,3,2,1,0:T(8,128)}, f32[2,2,8,32,128]{4,3,2,1,0:T(8,128)}, u32[]{:S(2)}, u32[]{:S(2)}) collective-permute-start(f32[2,2,8,32,128]{4,3,2,1,0:T(8,128)} %get-tuple-element.15.refs_0_.refs_2_), channel_id=1, source_target_pairs={{0,1},{3,2},{4,5},{7,6},{8,9},{11,10},{12,13},{15,14},{16,17},{19,... | collective-permute-start | bytes 1572872 | tf_op jit(solution)/shard_map/ppermute | solution.py:477
  15.0 4.2 %collective-permute-start = (f32[2,2,8,32,128]{4,3,2,1,0:T(8,128)}, f32[2,2,8,32,128]{4,3,2,1,0:T(8,128)}, u32[]{:S(2)}, u32[]{:S(2)}) collective-permute-start(f32[2,2,8,32,128]{4,3,2,1,0:T(8,128)} %get-tuple-element.13.refs_0_.refs_1_), channel_id=1, source_target_pairs={{4,0},{8,4},{12,8},{16,12},{20,16},{24,20},{28,24},{5,1},{9,5},{13... | collective-permute-start | bytes 1572872 | tf_op jit(solution)/shard_map/ppermute | solution.py:467
  17.8 3.2 %collective-permute-start.2 = (f32[48,8,256]{2,1,0:T(8,128)}, f32[48,8,256]{2,1,0:T(8,128)}, u32[]{:S(2)}, u32[]{:S(2)}) collective-permute-start(f32[48,8,256]{2,1,0:T(8,128)} %lag_inside.3.refs_5_), channel_id=1, source_target_pairs={{1,2},{2,1},{5,6},{6,5},{9,10},{10,9},{13,14},{14,13},{17,18},{18,... | collective-permute-start | bytes 1179656 | tf_op jit(solution)/shard_map/ppermute | solution.py:485
  19.4 29.7 %collective-permute-start.6 = (f32[80,8,256]{2,1,0:T(8,128)}, f32[80,8,256]{2,1,0:T(8,128)}, u32[]{:S(2)}, u32[]{:S(2)}) collective-permute-start(f32[80,8,256]{2,1,0:T(8,128)} %lag_across.4), channel_id=1, source_target_pairs={{1,2},{2,1},{5,6},{6,5},{9,10},{10,9},{13,14},{14,13},{17,18},{18,... | collective-permute-start | bytes 1966088 | tf_op jit(solution)/shard_map/ppermute | solution.py:485
  22.9 40.1 %collective-permute-start.7 = (f32[48,8,256]{2,1,0:T(8,128)}, f32[48,8,256]{2,1,0:T(8,128)}, u32[]{:S(2)}, u32[]{:S(2)}) collective-permute-start(f32[48,8,256]{2,1,0:T(8,128)} %add.3.refs_7_), channel_id=1, source_target_pairs={{1,0},{2,3},{5,4},{6,7},{9,8},{10,11},{13,12},{14,15},{17,16},{18,... | collective-permute-start | bytes 1179656 | tf_op jit(solution)/shard_map/ppermute | solution.py:488
  24.2 32.1 %collective-permute-start.4 = (f32[2,2,8,32,128]{4,3,2,1,0:T(8,128)}, f32[2,2,8,32,128]{4,3,2,1,0:T(8,128)}, u32[]{:S(2)}, u32[]{:S(2)}) collective-permute-start(f32[2,2,8,32,128]{4,3,2,1,0:T(8,128)} %get-tuple-element.20), channel_id=1, source_target_pairs={{0,1},{3,2},{4,5},{7,6},{8,9},{11,10},{12,13},{15,14},{16,17},{19,... | collective-permute-start | bytes 1572872 | tf_op jit(solution)/shard_map/ppermute | solution.py:477
  47.5 27.3 %collective-permute-start.8 = (f32[128,8,256]{2,1,0:T(8,128)}, f32[128,8,256]{2,1,0:T(8,128)}, u32[]{:S(2)}, u32[]{:S(2)}) collective-permute-start(f32[128,8,256]{2,1,0:T(8,128)} %lag_all.2.refs_6_), channel_id=1, source_target_pairs={{1,2},{2,1},{5,6},{6,5},{9,10},{10,9},{13,14},{14,13},{17,18},{18,... | collective-permute-start | bytes 3145736 | tf_op jit(solution)/shard_map/ppermute | solution.py:485
  49.2 25.5 %collective-permute-start.9 = (f32[80,8,256]{2,1,0:T(8,128)}, f32[80,8,256]{2,1,0:T(8,128)}, u32[]{:S(2)}, u32[]{:S(2)}) collective-permute-start(f32[80,8,256]{2,1,0:T(8,128)} %lag_across.5.refs_8_), channel_id=1, source_target_pairs={{1,0},{2,3},{5,4},{6,7},{9,8},{10,11},{13,12},{14,15},{17,16},{18,... | collective-permute-start | bytes 1966088 | tf_op jit(solution)/shard_map/ppermute | solution.py:488

commit v6 on v5

--- a/solution.py
+++ b/solution.py
@@ -129,109 +129,104 @@
     )(x, *consts)
 
 
-def whiten_first(x, tables, before=None):
+def take_far(x):
+    chunks = 4
+    step = x.shape[1] // chunks
+
+    def kernel(x_any, out, held, in_sems, out_sems):
+        z = lax.axis_index("tm")
+
+        @pl.when((z == 0) | (z == 3))
+        def _():
+            place = jnp.where(z < 2, 3, 0)
+            spans = [pl.ds(step * chunk, step) for chunk in range(chunks)]
+            loads = [
+                pltpu.make_async_copy(x_any.at[place, span], held.at[span], in_sems.at[chunk])
+                for chunk, span in enumerate(spans)
+            ]
+            stores = [
+                pltpu.make_async_copy(held.at[span], out.at[span], out_sems.at[chunk])
+                for chunk, span in enumerate(spans)
+            ]
+            for load in loads:
+                load.start()
+            for load, store in zip(loads, stores):
+                load.wait()
+                store.start()
+            for store in stores:
+                store.wait()
+
+    far_memory = pl.BlockSpec(memory_space=pltpu.HBM)
+    return pl.pallas_call(
+        kernel,
+        in_specs=[far_memory],
+        out_specs=far_memory,
+        out_shape=jax.ShapeDtypeStruct(x.shape[1:], jnp.float32),
+        scratch_shapes=[
+            pltpu.VMEM(x.shape[1:], jnp.float32),
+            pltpu.SemaphoreType.DMA((chunks,)),
+            pltpu.SemaphoreType.DMA((chunks,)),
+        ],
+        compiler_params=pltpu.CompilerParams(vmem_limit_bytes=VMEM_LIMIT),
+        cost_estimate=pl.CostEstimate(flops=COST, bytes_accessed=1000, transcendentals=0),
+        name="take_far",
+    )(x)
+
+
+def whiten_own(x, tables, after):
     near, segs, win = x.shape[1:]
     consts = [jnp.asarray(tables["hann"]), jnp.asarray(tables["forward"])]
-    first = before is None
-    count = 1 if first else 6
-    passed = [] if first else [before]
-
-    def kernel(*refs):
-        x_any, hann_any, forward_any = refs[:3]
-        refs = refs[3 + len(passed) :]
-        outs, refs = refs[:count], refs[count:]
-        stage, hann, forward, blocks_in, blocks_out, sems, out_sems = refs
+    copies = ((0, 1), (1, 3))
+
+    def kernel(x_any, hann_any, forward_any, _, *refs):
+        outs, (stage, hann, forward, blocks_in, blocks_out, sems, out_sems) = refs[:6], refs[6:]
         z = lax.axis_index("tm")
-        end = (z == 0) | (z == 3)
-
-        def load_tables():
-            tabs = [
-                pltpu.make_async_copy(hann_any, hann, sems.at[4]),
-                pltpu.make_async_copy(forward_any, forward, sems.at[5]),
-            ]
-            for tab in tabs:
-                tab.start()
-            return tabs
-
-        def one(load, slot):
-            load.wait()
-            whiten_block(blocks_in.at[slot], hann, forward, blocks_out.at[slot], stage)
-
-        def all_four(tabs):
-            loads = [pltpu.make_async_copy(x_any.at[b], blocks_in.at[b], sems.at[b]) for b in range(4)]
-            for load in loads:
-                load.start()
-            for tab in tabs:
-                tab.wait()
-            stores = []
-            for b in range(4):
-                one(loads[b], b)
-                stores.append(pltpu.make_async_copy(blocks_out.at[b], outs[b], out_sems.at[b]))
-                stores[-1].start()
-            for at, sources in enumerate(((0, 1), (1, 3))):
-                for side, source in enumerate(sources):
-
-                    @pl.when(z < 2 if side == 0 else z >= 2)
-                    def _():
-                        pltpu.make_async_copy(
-                            blocks_out.at[source], outs[4 + at], out_sems.at[4 + at]
-                        ).start()
-
-                stores.append(
-                    pltpu.make_async_copy(blocks_out.at[sources[0]], outs[4 + at], out_sems.at[4 + at])
-                )
-            for store in stores:
-                store.wait()
-
-        if first:
-
-            @pl.when(end)
-            def _():
-                place = jnp.where(z < 2, 3, 0)
-                step = near // 2
-                spans = [pl.ds(0, step), pl.ds(step, step)]
-                loads = [
-                    pltpu.make_async_copy(x_any.at[place, span], blocks_in.at[4, span], sems.at[index])
-                    for index, span in enumerate(spans)
-                ]
-                loads[0].start()
-                tabs = load_tables()
-                loads[1].start()
-                for tab in tabs:
-                    tab.wait()
-                stores = []
-                for index, span in enumerate(spans):
-                    loads[index].wait()
-                    target = blocks_out.at[4, :, :, :, span]
-                    whiten_block(blocks_in.at[4, span], hann, forward, target, stage)
-                    stores.append(pltpu.make_async_copy(target, outs[0].at[:, :, :, span], out_sems.at[index]))
-                    stores[-1].start()
-                for store in stores:
-                    store.wait()
-
-        else:
-            all_four(load_tables())
+        loads = [pltpu.make_async_copy(x_any.at[b], blocks_in.at[b], sems.at[b]) for b in range(4)]
+        tabs = [
+            pltpu.make_async_copy(hann_any, hann, sems.at[4]),
+            pltpu.make_async_copy(forward_any, forward, sems.at[5]),
+        ]
+        for load in loads[:1] + tabs + loads[1:]:
+            load.start()
+        for tab in tabs:
+            tab.wait()
+        stores = []
+        for b in range(4):
+            loads[b].wait()
+            whiten_block(blocks_in.at[b], hann, forward, blocks_out.at[b], stage)
+            stores.append(pltpu.make_async_copy(blocks_out.at[b], outs[b], out_sems.at[b]))
+            stores[-1].start()
+        for at, sources in enumerate(copies):
+            for side, source in enumerate(sources):
+
+                @pl.when(z < 2 if side == 0 else z >= 2)
+                def _():
+                    pltpu.make_async_copy(blocks_out.at[source], outs[4 + at], out_sems.at[4 + at]).start()
+
+            stores.append(pltpu.make_async_copy(blocks_out.at[sources[0]], outs[4 + at], out_sems.at[4 + at]))
+        for store in stores:
+            store.wait()
 
     shape = (2, 2, segs, near, LANES)
     far_memory = pl.BlockSpec(memory_space=pltpu.HBM)
     return pl.pallas_call(
         kernel,
-        in_specs=[far_memory] * (3 + len(passed)),
-        out_specs=[far_memory] * count,
-        out_shape=[jax.ShapeDtypeStruct(shape, jnp.float32)] * count,
+        in_specs=[far_memory] * 4,
+        out_specs=[far_memory] * 6,
+        out_shape=[jax.ShapeDtypeStruct(shape, jnp.float32)] * 6,
         scratch_shapes=[
             pltpu.VMEM((win // LANES, near * segs, LANES), jnp.float32),
             pltpu.VMEM(consts[0].shape, consts[0].dtype),
             pltpu.VMEM(consts[1].shape, consts[1].dtype),
-            pltpu.VMEM((5, near, segs, win), jnp.float32),
-            pltpu.VMEM((5,) + shape, jnp.float32),
-            pltpu.SemaphoreType.DMA((7,)),
-            pltpu.SemaphoreType.DMA((7,)),
+            pltpu.VMEM((4, near, segs, win), jnp.float32),
+            pltpu.VMEM((4,) + shape, jnp.float32),
+            pltpu.SemaphoreType.DMA((6,)),
+            pltpu.SemaphoreType.DMA((6,)),
         ],
         compiler_params=pltpu.CompilerParams(vmem_limit_bytes=VMEM_LIMIT),
         cost_estimate=pl.CostEstimate(flops=COST, bytes_accessed=1000, transcendentals=0),
-        name="whiten_first" if first else "whiten_rest",
-    )(x, *consts, *passed)
+        name="whiten_own",
+    )(x, *consts, after)
 
 
 def groups_of(near, which):
@@ -274,7 +269,7 @@
                 lhs[half, rows, LANES:] = cross_im
 
 
-def lag_sums(which, sources, tables, role=None, prior=(), after=(), cost=COST, inner=False):
+def lag_sums(which, sources, tables, role=None, prior=(), after=(), cost=COST, inner=False, raw=None):
     table = jnp.asarray(tables["inverse"])
     sample = sources[0][0][0]
     halves, parts, segs, near, lanes = sample.shape
@@ -292,6 +287,8 @@
                 places.append(known[0] if known else len(operands) - 1)
             layout[-1].append(places)
     shape = (len(groups), 8, LAGS)
+    total = len(sources) + (raw is not None)
+    extras = [] if raw is None else [raw, jnp.asarray(tables["hann"]), jnp.asarray(tables["forward"])]
     rows = 8 * len(groups)
     chunk = 16
 
@@ -305,7 +302,20 @@
         cands, table_any = refs[: len(operands)], refs[len(operands)]
         refs = refs[len(operands) + 1 :]
         priors, refs = refs[: len(prior)], refs[len(prior) + len(after) :]
-        out, pair, lhs, table_ref, result, in_sems, table_sem, prior_sem, out_sems = refs
+        samples, refs = refs[: len(extras)], refs[len(extras) :]
+        out, refs = refs[0], refs[1:]
+        if raw is not None:
+            white, refs = refs[0], refs[1:]
+        pair, lhs, table_ref, result, in_sems, table_sem, prior_sem, out_sems = refs[:8]
+        if raw is not None:
+            stage, raw_sems = refs[8], refs[-1]
+            held = refs[9:-1]
+            raw_copies = [
+                pltpu.make_async_copy(source, place, raw_sems.at[index])
+                for index, (source, place) in enumerate(zip(samples, held))
+            ]
+            for raw_copy in raw_copies:
+                raw_copy.start()
         pick = role(lax.axis_index("tm")) if role is not None else None
 
         def copy(number, side, half, place):
@@ -333,11 +343,20 @@
             prior_copy = pltpu.make_async_copy(priors[0], result, prior_sem)
             prior_copy.start()
 
+        if raw is not None:
+            for raw_copy in raw_copies:
+                raw_copy.wait()
+            whiten_block(held[0], held[1], held[2], pair.at[total - 1], stage)
+            white_copy = pltpu.make_async_copy(pair.at[total - 1], white, raw_sems.at[len(extras)])
+            white_copy.start()
+
         def each_half(half, _):
             for number, source in enumerate(layout):
                 for side, places in enumerate(source):
                     copy(number, side, half, places[0]).wait()
                 products(pair.at[number], half, lhs, groups, number == 0)
+            if raw is not None:
+                products(pair.at[total - 1], half, lhs, groups, False)
             return 0
 
         lax.fori_loop(0, halves, each_half, 0)
@@ -356,16 +375,24 @@
             copies[-1].start()
         for done in copies:
             done.wait()
+        if raw is not None:
+            white_copy.wait()
 
     far_memory = pl.BlockSpec(memory_space=pltpu.HBM)
     chunks = -(-shape[0] // chunk)
-    return pl.pallas_call(
+    results, spare = [jax.ShapeDtypeStruct(shape, jnp.float32)], []
+    if raw is not None:
+        results.append(jax.ShapeDtypeStruct(sample.shape, jnp.float32))
+        spare = [pltpu.VMEM((raw.shape[2] // LANES, near * segs, LANES), jnp.float32)]
+        spare += [pltpu.VMEM(value.shape, value.dtype) for value in extras]
+        spare.append(pltpu.SemaphoreType.DMA((len(extras) + 1,)))
+    outputs = pl.pallas_call(
         kernel,
-        in_specs=[far_memory] * (len(operands) + 1 + len(prior) + len(after)),
-        out_specs=far_memory,
-        out_shape=jax.ShapeDtypeStruct(shape, jnp.float32),
+        in_specs=[far_memory] * (len(operands) + 1 + len(prior) + len(after) + len(extras)),
+        out_specs=[far_memory] * len(results),
+        out_shape=results,
         scratch_shapes=[
-            pltpu.VMEM((len(sources), halves, parts, segs, sides * near, lanes), jnp.float32),
+            pltpu.VMEM((total, halves, parts, segs, sides * near, lanes), jnp.float32),
             pltpu.VMEM((halves, rows, 2 * lanes), jnp.float32),
             pltpu.VMEM(table.shape, table.dtype),
             pltpu.VMEM(shape, jnp.float32),
@@ -373,11 +400,13 @@
             pltpu.SemaphoreType.DMA,
             pltpu.SemaphoreType.DMA,
             pltpu.SemaphoreType.DMA((chunks,)),
-        ],
+        ]
+        + spare,
         compiler_params=pltpu.CompilerParams(vmem_limit_bytes=VMEM_LIMIT),
         cost_estimate=pl.CostEstimate(flops=cost, bytes_accessed=1000, transcendentals=0),
         name="lag_" + which,
-    )(*operands, table, *prior, *after)
+    )(*operands, table, *prior, *after, *extras)
+    return outputs[0] if raw is None else outputs
 
 
 def place(near, inside, across):
@@ -487,9 +516,9 @@
     def inner(value):
         return lax.ppermute(value, "tm", [(1, 0), (2, 3)])
 
-    (far,) = whiten_first(blocks, tables)
+    far = take_far(blocks)
     e1 = outer(far)
-    *own, next_far, last = whiten_first(blocks, tables, far)
+    *own, next_far, last = whiten_own(blocks, tables, far)
     e2 = outer_next(next_far)
     own.append(shifted(own[0], -1))
     e3 = outer(own[2])
@@ -497,7 +526,7 @@
     role = lambda z: jnp.where(z < 2, 0, 1)
     jobs = functools.partial(lag_sums, tables=tables, inner=True)
     back_in = jobs("inside", [([own[0], own[3]], None)], role=role, cost=1_000_000)
-    m1 = jobs("inside", [([own[3], own[0]], None), ([e1], None)], role=role, after=[back_in])
+    m1, e1 = jobs("inside", [([own[3], own[0]], None)], role=role, after=[back_in], raw=e1)
     m1_in = middle(m1)
     base = jobs("across", [([own[3], own[0]], [own[4], own[1]])], role=role, after=[m1])
     m2 = jobs("across", [([e1], [e2])], prior=[base])

time: 78.6 us -> 77.7 us (0.989)
  Pallas kernels: 19.1 us -> 17.7 us
    pallas_call x2, Pallas kernels: 8.77 us -> 7.46 us  [the longest x1 5.65 us: whiten_own(): pl.pallas_call(kernel, in_specs=[far_memory] * 4, out_specs=[far_memory]...]
where the time goes in v6:
time: 77.7 us; the launch traced here: 76.6 us
  starting transfers between devices  37.7 us (49%)
  waiting for transfers between devices  18.9 us (24%)
  Pallas kernels  17.7 us (23%)
  other arithmetic  1.97 us (3%)
    ppermute x3, starting transfers between devices, outer(): return lax.ppermute(value, 'tm', [(0, 1), (3, 2)])  27.8 us
    ppermute x2, waiting for transfers between devices, inner(): return lax.ppermute(value, 'tm', [(1, 0), (2, 3)])  11.5 us
    pallas_call x7, Pallas kernels, lag_sums(): pl.pallas_call(kernel, in_specs=[far_memory] * (len(operands) + 1 + len(p...  7.41 us
    ppermute x3, waiting for transfers between devices, outer(): return lax.ppermute(value, 'tm', [(0, 1), (3, 2)])  7.38 us
    pallas_call x1, Pallas kernels, whiten_own(): pl.pallas_call(kernel, in_specs=[far_memory] * 4, out_specs=[far_memory]...  5.65 us
    ppermute x3, starting transfers between devices, middle(): return lax.ppermute(value, 'tm', [(1, 2), (2, 1)])  4.6 us
    pallas_call x1, Pallas kernels, place(): pl.pallas_call(kernel, in_specs=[far_memory] * len(operands), out_specs=f...  2.87 us
    ppermute x2, starting transfers between devices, inner(): return lax.ppermute(value, 'tm', [(1, 0), (2, 3)])  2.57 us
  transfers between devices with their start and end apart: 10, of which 3 were waited for; matrix products, arithmetic and copies ran while one was open for 3% of the time, Pallas kernels for 17%

profile of v6, /device:TPU:0, one launch (start us, length us, event | category | flops | bytes accessed | tf_op | source)
XLA Modules:
  0.0 76.6 jit_solution(11458963894850011892)
XLA Ops:
  0.0 1.8 %take_far.1._ = f32[32,8,512]{2,1,0:T(8,128)} custom-call(f32[4,32,8,512]{3,2,1,0:T(8,128)} %bitcast.1), custom_call_target="tpu_custom_call" | custom-call | flops 10000000000 | bytes 1000 | tf_op jit(solution)/shard_map/take_far/pallas_call | solution.py:160
  1.8 4.0 %collective-permute-start.1 = (f32[32,8,512]{2,1,0:T(8,128)}, f32[32,8,512]{2,1,0:T(8,128)}, u32[]{:S(2)}, u32[]{:S(2)}) collective-permute-start(f32[32,8,512]{2,1,0:T(8,128)} %take_far.1._), channel_id=1, source_target_pairs={{0,1},{3,2},{4,5},{7,6},{8,9},{11,10},{12,13},{15,14},{16,17},{19,... | collective-permute-start | bytes 1572872 | tf_op jit(solution)/shard_map/ppermute | solution.py:506
  5.8 5.6 %whiten_own.1 = (f32[2,2,8,32,128]{4,3,2,1,0:T(8,128)}, f32[2,2,8,32,128]{4,3,2,1,0:T(8,128)}, f32[2,2,8,32,128]{4,3,2,1,0:T(8,128)}, f32[2,2,8,32,128]{4,3,2,1,...) custom-call(f32[4,32,8,512]{3,2,1,0:T(8,128)} %bitcast.2, ...), custom_call_target="tpu_custom_call" | custom-call | flops 10000000000 | bytes 1000 | tf_op jit(solution)/shard_map/whiten_own/pallas_call | solution.py:212
  11.5 1.5 %collective-permute-start.3 = (f32[2,2,8,32,128]{4,3,2,1,0:T(8,128)}, f32[2,2,8,32,128]{4,3,2,1,0:T(8,128)}, u32[]{:S(2)}, u32[]{:S(2)}) collective-permute-start(f32[2,2,8,32,128]{4,3,2,1,0:T(8,128)} %get-tuple-element.22), channel_id=1, source_target_pairs={{4,1},{8,5},{12,9},{16,13},{20,17},{24,21},{28,25},{3,2},{7,6},{11... | collective-permute-start | bytes 1572872 | tf_op jit(solution)/shard_map/ppermute | solution.py:511
  13.0 2.1 %collective-permute-start.5 = (f32[2,2,8,32,128]{4,3,2,1,0:T(8,128)}, f32[2,2,8,32,128]{4,3,2,1,0:T(8,128)}, u32[]{:S(2)}, u32[]{:S(2)}) collective-permute-start(f32[2,2,8,32,128]{4,3,2,1,0:T(8,128)} %get-tuple-element.17.refs_0_.refs_2_), channel_id=1, source_target_pairs={{0,1},{3,2},{4,5},{7,6},{8,9},{11,10},{12,13},{15,14},{16,17},{19,... | collective-permute-start | bytes 1572872 | tf_op jit(solution)/shard_map/ppermute | solution.py:506
  15.0 1.3 %collective-permute-start = (f32[2,2,8,32,128]{4,3,2,1,0:T(8,128)}, f32[2,2,8,32,128]{4,3,2,1,0:T(8,128)}, u32[]{:S(2)}, u32[]{:S(2)}) collective-permute-start(f32[2,2,8,32,128]{4,3,2,1,0:T(8,128)} %get-tuple-element.15.refs_0_.refs_1_), channel_id=1, source_target_pairs={{4,0},{8,4},{12,8},{16,12},{20,16},{24,20},{28,24},{5,1},{9,5},{13... | collective-permute-start | bytes 1572872 | tf_op jit(solution)/shard_map/ppermute | solution.py:496
  16.3 0.1 lag_inside.2.refs_3_
  16.4 1.2 %collective-permute-done.1.refs_4_ = f32[32,8,512]{2,1,0:T(8,128)} collective-permute-done((f32[32,8,512]{2,1,0:T(8,128)}, f32[32,8,512]{2,1,0:T(8,128)}, u32[]{:S(2)}, u32[]{:S(2)}) %collective-permute-start.1) | collective-permute-done | bytes 524320 | tf_op jit(solution)/shard_map/ppermute | solution.py:506
  17.6 0.1 lag_inside.3
  17.8 1.4 %collective-permute-start.2 = (f32[48,8,256]{2,1,0:T(8,128)}, f32[48,8,256]{2,1,0:T(8,128)}, u32[]{:S(2)}, u32[]{:S(2)}) collective-permute-start(f32[48,8,256]{2,1,0:T(8,128)} %get-tuple-element.20.refs_5_), channel_id=1, source_target_pairs={{1,2},{2,1},{5,6},{6,5},{9,10},{10,9},{13,14},{14,13},{17,18},{18,... | collective-permute-start | bytes 1179656 | tf_op jit(solution)/shard_map/ppermute | solution.py:514
  19.2 0.1 lag_across.3.refs_3_
  19.3 0.1 lag_across.4
  19.4 1.5 %collective-permute-start.6 = (f32[80,8,256]{2,1,0:T(8,128)}, f32[80,8,256]{2,1,0:T(8,128)}, u32[]{:S(2)}, u32[]{:S(2)}) collective-permute-start(f32[80,8,256]{2,1,0:T(8,128)} %lag_across.4), channel_id=1, source_target_pairs={{1,2},{2,1},{5,6},{6,5},{9,10},{10,9},{13,14},{14,13},{17,18},{18,... | collective-permute-start | bytes 1966088 | tf_op jit(solution)/shard_map/ppermute | solution.py:514
  21.0 2.0 %add.3.refs_7_ = f32[48,8,256]{2,1,0:T(8,128)} add(f32[48,8,256]{2,1,0:T(8,128)} %collective-permute-done.2, f32[48,8,256]{2,1,0:T(8,128)} %lag_inside.2.refs_3_) | non-fusion elementwise | flops 98304 | bytes 1179648 | tf_op jit(solution)/shard_map/add | solution.py:535
  22.9 1.3 %collective-permute-start.7 = (f32[48,8,256]{2,1,0:T(8,128)}, f32[48,8,256]{2,1,0:T(8,128)}, u32[]{:S(2)}, u32[]{:S(2)}) collective-permute-start(f32[48,8,256]{2,1,0:T(8,128)} %add.3.refs_7_), channel_id=1, source_target_pairs={{1,0},{2,3},{5,4},{6,7},{9,8},{10,11},{13,12},{14,15},{17,16},{18,... | collective-permute-start | bytes 1179656 | tf_op jit(solution)/shard_map/ppermute | solution.py:517
  24.2 21.7 %collective-permute-start.4 = (f32[2,2,8,32,128]{4,3,2,1,0:T(8,128)}, f32[2,2,8,32,128]{4,3,2,1,0:T(8,128)}, u32[]{:S(2)}, u32[]{:S(2)}) collective-permute-start(f32[2,2,8,32,128]{4,3,2,1,0:T(8,128)} %get-tuple-element.24), channel_id=1, source_target_pairs={{0,1},{3,2},{4,5},{7,6},{8,9},{11,10},{12,13},{15,14},{16,17},{19,... | collective-permute-start | bytes 1572872 | tf_op jit(solution)/shard_map/ppermute | solution.py:506
  45.9 0.2 lag_all.2.refs_6_
  46.1 1.6 %collective-permute-start.8 = (f32[128,8,256]{2,1,0:T(8,128)}, f32[128,8,256]{2,1,0:T(8,128)}, u32[]{:S(2)}, u32[]{:S(2)}) collective-permute-start(f32[128,8,256]{2,1,0:T(8,128)} %lag_all.2.refs_6_), channel_id=1, source_target_pairs={{1,2},{2,1},{5,6},{6,5},{9,10},{10,9},{13,14},{14,13},{17,18},{18,... | collective-permute-start | bytes 3145736 | tf_op jit(solution)/shard_map/ppermute | solution.py:514
  47.7 0.1 lag_across.5.refs_8_
  47.8 1.3 %collective-permute-start.9 = (f32[80,8,256]{2,1,0:T(8,128)}, f32[80,8,256]{2,1,0:T(8,128)}, u32[]{:S(2)}, u32[]{:S(2)}) collective-permute-start(f32[80,8,256]{2,1,0:T(8,128)} %lag_across.5.refs_8_), channel_id=1, source_target_pairs={{1,0},{2,3},{5,4},{6,7},{9,8},{10,11},{13,12},{14,15},{17,16},{18,... | collective-permute-start | bytes 1966088 | tf_op jit(solution)/shard_map/ppermute | solution.py:517
  49.1 6.2 %collective-permute-done.4.refs_5_ = f32[2,2,8,32,128]{4,3,2,1,0:T(8,128)} collective-permute-done((f32[2,2,8,32,128]{4,3,2,1,0:T(8,128)}, f32[2,2,8,32,128]{4,3,2,1,0:T(8,128)}, u32[]{:S(2)}, u32[]{:S(2)}) %collective-permute-start.4) | collective-permute-done | bytes 524320 | tf_op jit(solution)/shard_map/ppermute | solution.py:506
  55.3 6.7 %lag_all.3.refs_0_.refs_3_ = f32[128,8,256]{2,1,0:T(8,128)} custom-call(f32[2,2,8,32,128]{4,3,2,1,0:T(8,128)} %get-tuple-element.15.refs_0_.refs_1_, f32[2,2,8,32,128]{4,3,2,1,0:T(8,128)} %get-tuple-element.16.refs_3_.refs_1_.refs_2_, f32[2,2,8,32,128]{4,3,2,1,0:T(8,128)} %get-tuple-element.17.refs_0_.refs_2_, ...), custom_call_target="tpu_custom_call" | custom-call | flops 10000000000 | bytes 1000 | tf_op jit(solution)/shard_map/lag_all/pallas_call | solution.py:389
  62.0 11.5 %collective-permute-done.9.refs_4_ = f32[80,8,256]{2,1,0:T(8,128)} collective-permute-done((f32[80,8,256]{2,1,0:T(8,128)}, f32[80,8,256]{2,1,0:T(8,128)}, u32[]{:S(2)}, u32[]{:S(2)}) %collective-permute-start.9) | collective-permute-done | bytes 655392 | tf_op jit(solution)/shard_map/ppermute | solution.py:517
  73.6 2.9 %place.1 = f32[32,32,256]{2,1,0:T(8,128)} custom-call(f32[128,8,256]{2,1,0:T(8,128)} %lag_all.3.refs_0_.refs_3_, f32[48,8,256]{2,1,0:T(8,128)} %collective-permute-done.7.refs_1_, f32[128,8,256]{2,1,0:T(8,128)} %collective-permute-done.8.refs_2_.refs_5_, f32[128,8,256]{2,1,0:T(8,128)} %lag_all.3.refs_0_.refs_3_, ...), custom_call_target="tpu_custom_call" | custom-call | flops 10000000000 | bytes 1000 | tf_op jit(solution)/shard_map/place/pallas_call | solution.py:477
  (7 shorter events, 0.0 us)
Async XLA Ops:
  1.8 15.8 %collective-permute-start.1 = (f32[32,8,512]{2,1,0:T(8,128)}, f32[32,8,512]{2,1,0:T(8,128)}, u32[]{:S(2)}, u32[]{:S(2)}) collective-permute-start(f32[32,8,512]{2,1,0:T(8,128)} %take_far.1._), channel_id=1, source_target_pairs={{0,1},{3,2},{4,5},{7,6},{8,9},{11,10},{12,13},{15,14},{16,17},{19,... | collective-permute-start | bytes 1572872 | tf_op jit(solution)/shard_map/ppermute | solution.py:506
  11.5 7.8 %collective-permute-start.3 = (f32[2,2,8,32,128]{4,3,2,1,0:T(8,128)}, f32[2,2,8,32,128]{4,3,2,1,0:T(8,128)}, u32[]{:S(2)}, u32[]{:S(2)}) collective-permute-start(f32[2,2,8,32,128]{4,3,2,1,0:T(8,128)} %get-tuple-element.22), channel_id=1, source_target_pairs={{4,1},{8,5},{12,9},{16,13},{20,17},{24,21},{28,25},{3,2},{7,6},{11... | collective-permute-start | bytes 1572872 | tf_op jit(solution)/shard_map/ppermute | solution.py:511
  13.0 32.9 %collective-permute-start.5 = (f32[2,2,8,32,128]{4,3,2,1,0:T(8,128)}, f32[2,2,8,32,128]{4,3,2,1,0:T(8,128)}, u32[]{:S(2)}, u32[]{:S(2)}) collective-permute-start(f32[2,2,8,32,128]{4,3,2,1,0:T(8,128)} %get-tuple-element.17.refs_0_.refs_2_), channel_id=1, source_target_pairs={{0,1},{3,2},{4,5},{7,6},{8,9},{11,10},{12,13},{15,14},{16,17},{19,... | collective-permute-start | bytes 1572872 | tf_op jit(solution)/shard_map/ppermute | solution.py:506
  15.0 4.1 %collective-permute-start = (f32[2,2,8,32,128]{4,3,2,1,0:T(8,128)}, f32[2,2,8,32,128]{4,3,2,1,0:T(8,128)}, u32[]{:S(2)}, u32[]{:S(2)}) collective-permute-start(f32[2,2,8,32,128]{4,3,2,1,0:T(8,128)} %get-tuple-element.15.refs_0_.refs_1_), channel_id=1, source_target_pairs={{4,0},{8,4},{12,8},{16,12},{20,16},{24,20},{28,24},{5,1},{9,5},{13... | collective-permute-start | bytes 1572872 | tf_op jit(solution)/shard_map/ppermute | solution.py:496
  17.8 3.2 %collective-permute-start.2 = (f32[48,8,256]{2,1,0:T(8,128)}, f32[48,8,256]{2,1,0:T(8,128)}, u32[]{:S(2)}, u32[]{:S(2)}) collective-permute-start(f32[48,8,256]{2,1,0:T(8,128)} %get-tuple-element.20.refs_5_), channel_id=1, source_target_pairs={{1,2},{2,1},{5,6},{6,5},{9,10},{10,9},{13,14},{14,13},{17,18},{18,... | collective-permute-start | bytes 1179656 | tf_op jit(solution)/shard_map/ppermute | solution.py:514
  19.4 28.3 %collective-permute-start.6 = (f32[80,8,256]{2,1,0:T(8,128)}, f32[80,8,256]{2,1,0:T(8,128)}, u32[]{:S(2)}, u32[]{:S(2)}) collective-permute-start(f32[80,8,256]{2,1,0:T(8,128)} %lag_across.4), channel_id=1, source_target_pairs={{1,2},{2,1},{5,6},{6,5},{9,10},{10,9},{13,14},{14,13},{17,18},{18,... | collective-permute-start | bytes 1966088 | tf_op jit(solution)/shard_map/ppermute | solution.py:514
  22.9 39.1 %collective-permute-start.7 = (f32[48,8,256]{2,1,0:T(8,128)}, f32[48,8,256]{2,1,0:T(8,128)}, u32[]{:S(2)}, u32[]{:S(2)}) collective-permute-start(f32[48,8,256]{2,1,0:T(8,128)} %add.3.refs_7_), channel_id=1, source_target_pairs={{1,0},{2,3},{5,4},{6,7},{9,8},{10,11},{13,12},{14,15},{17,16},{18,... | collective-permute-start | bytes 1179656 | tf_op jit(solution)/shard_map/ppermute | solution.py:517
  24.2 31.1 %collective-permute-start.4 = (f32[2,2,8,32,128]{4,3,2,1,0:T(8,128)}, f32[2,2,8,32,128]{4,3,2,1,0:T(8,128)}, u32[]{:S(2)}, u32[]{:S(2)}) collective-permute-start(f32[2,2,8,32,128]{4,3,2,1,0:T(8,128)} %get-tuple-element.24), channel_id=1, source_target_pairs={{0,1},{3,2},{4,5},{7,6},{8,9},{11,10},{12,13},{15,14},{16,17},{19,... | collective-permute-start | bytes 1572872 | tf_op jit(solution)/shard_map/ppermute | solution.py:506
  46.1 27.5 %collective-permute-start.8 = (f32[128,8,256]{2,1,0:T(8,128)}, f32[128,8,256]{2,1,0:T(8,128)}, u32[]{:S(2)}, u32[]{:S(2)}) collective-permute-start(f32[128,8,256]{2,1,0:T(8,128)} %lag_all.2.refs_6_), channel_id=1, source_target_pairs={{1,2},{2,1},{5,6},{6,5},{9,10},{10,9},{13,14},{14,13},{17,18},{18,... | collective-permute-start | bytes 3145736 | tf_op jit(solution)/shard_map/ppermute | solution.py:514
  47.8 25.7 %collective-permute-start.9 = (f32[80,8,256]{2,1,0:T(8,128)}, f32[80,8,256]{2,1,0:T(8,128)}, u32[]{:S(2)}, u32[]{:S(2)}) collective-permute-start(f32[80,8,256]{2,1,0:T(8,128)} %lag_across.5.refs_8_), channel_id=1, source_target_pairs={{1,0},{2,3},{5,4},{6,7},{9,8},{10,11},{13,12},{14,15},{17,16},{18,... | collective-permute-start | bytes 1966088 | tf_op jit(solution)/shard_map/ppermute | solution.py:517

commit v7 on v6

--- a/solution.py
+++ b/solution.py
@@ -20,7 +20,7 @@
 def split_table(table):
     high = table.astype(ml_dtypes.bfloat16)
     low = (table - high.astype(np.float64)).astype(ml_dtypes.bfloat16)
-    return np.concatenate([high, low, high], axis=0)
+    return np.concatenate([high, low], axis=0)
 
 
 def make_tables(win, lags, segs):
@@ -49,7 +49,8 @@
 def dot_split(value, table):
     high = value.astype(jnp.bfloat16)
     low = (value - high.astype(jnp.float32)).astype(jnp.bfloat16)
-    return jnp.dot(jnp.concatenate([high, high, low], axis=1), table, preferred_element_type=jnp.float32)
+    dot = functools.partial(jnp.dot, preferred_element_type=jnp.float32)
+    return dot(jnp.concatenate([high, high], axis=1), table[...]) + dot(low, table[: value.shape[1]])
 
 
 def whiten_block(x_ref, hann, forward, w_ref, stage):
@@ -67,11 +68,11 @@
     quarter = [jnp.concatenate([piece[part] for piece in pieces], axis=0) for part in range(parts)]
     both = jnp.concatenate([quarter[0] + quarter[2], quarter[1] + quarter[3]], axis=1)
     between = jnp.concatenate([quarter[0] - quarter[2], quarter[1] - quarter[3]], axis=1)
-    spectra = (dot_split(both, forward[0]), dot_split(between, forward[1]))
+    spectra = (dot_split(both, forward.at[0]), dot_split(between, forward.at[1]))
     energy = jnp.concatenate(
         [sp[:, :LANES] * sp[:, :LANES] + sp[:, LANES:] * sp[:, LANES:] for sp in spectra], axis=1
     )
-    scale = lax.rsqrt(dot_split(energy, forward[2]) + 1e-06)
+    scale = lax.rsqrt(dot_split(energy, forward.at[2]) + 1e-06)
     for half, sp in enumerate(spectra):
         own = scale[:, LANES * half : LANES * half + LANES]
         real, imag = sp[:, :LANES] * own, sp[:, LANES:] * own
@@ -115,7 +116,7 @@
         out_specs=[far_memory] * count,
         out_shape=[jax.ShapeDtypeStruct(shape, jnp.float32)] * count,
         scratch_shapes=[
-            pltpu.VMEM((win // LANES, near * segs, LANES), jnp.float32),
+            pltpu.VMEM((win // LANES, near * segs + segs, LANES), jnp.float32),
             pltpu.VMEM(consts[0].shape, consts[0].dtype),
             pltpu.VMEM(consts[1].shape, consts[1].dtype),
             pltpu.VMEM((count, near, segs, win), jnp.float32),
@@ -215,7 +216,7 @@
         out_specs=[far_memory] * 6,
         out_shape=[jax.ShapeDtypeStruct(shape, jnp.float32)] * 6,
         scratch_shapes=[
-            pltpu.VMEM((win // LANES, near * segs, LANES), jnp.float32),
+            pltpu.VMEM((win // LANES, near * segs + segs, LANES), jnp.float32),
             pltpu.VMEM(consts[0].shape, consts[0].dtype),
             pltpu.VMEM(consts[1].shape, consts[1].dtype),
             pltpu.VMEM((4, near, segs, win), jnp.float32),
@@ -314,8 +315,6 @@
                 pltpu.make_async_copy(source, place, raw_sems.at[index])
                 for index, (source, place) in enumerate(zip(samples, held))
             ]
-            for raw_copy in raw_copies:
-                raw_copy.start()
         pick = role(lax.axis_index("tm")) if role is not None else None
 
         def copy(number, side, half, place):
@@ -337,29 +336,34 @@
                         def _():
                             copy(number, side, half, place).start()
 
+        if raw is not None:
+            for raw_copy in raw_copies:
+                raw_copy.start()
         table_copy = pltpu.make_async_copy(table_any, table_ref, table_sem)
         table_copy.start()
         if prior:
             prior_copy = pltpu.make_async_copy(priors[0], result, prior_sem)
             prior_copy.start()
 
+        def each_half(half, _):
+            for number, source in enumerate(layout):
+                for side, places in enumerate(source):
+                    copy(number, side, half, places[0]).wait()
+                products(pair.at[number], half, lhs, groups, number == 0)
+            return 0
+
+        def each_raw_half(half, _):
+            products(pair.at[total - 1], half, lhs, groups, False)
+            return 0
+
+        lax.fori_loop(0, halves, each_half, 0)
         if raw is not None:
             for raw_copy in raw_copies:
                 raw_copy.wait()
             whiten_block(held[0], held[1], held[2], pair.at[total - 1], stage)
             white_copy = pltpu.make_async_copy(pair.at[total - 1], white, raw_sems.at[len(extras)])
             white_copy.start()
-
-        def each_half(half, _):
-            for number, source in enumerate(layout):
-                for side, places in enumerate(source):
-                    copy(number, side, half, places[0]).wait()
-                products(pair.at[number], half, lhs, groups, number == 0)
-            if raw is not None:
-                products(pair.at[total - 1], half, lhs, groups, False)
-            return 0
-
-        lax.fori_loop(0, halves, each_half, 0)
+            lax.fori_loop(0, halves, each_raw_half, 0)
         table_copy.wait()
         if prior:
             prior_copy.wait()
@@ -368,7 +372,7 @@
             size = min(chunk, shape[0] - begin)
             span = pl.ds(8 * begin, 8 * size)
             value = jnp.concatenate([lhs[half, span, :] for half in range(halves)], axis=1)
-            lagged = dot_split(value, table_ref[...]).reshape(size, 8, LAGS)
+            lagged = dot_split(value, table_ref).reshape(size, 8, LAGS)
             place = pl.ds(begin, size)
             result[place] = result[place] + lagged if prior else lagged
             copies.append(pltpu.make_async_copy(result.at[place], out.at[place], out_sems.at[len(copies)]))
@@ -383,7 +387,7 @@
     results, spare = [jax.ShapeDtypeStruct(shape, jnp.float32)], []
     if raw is not None:
         results.append(jax.ShapeDtypeStruct(sample.shape, jnp.float32))
-        spare = [pltpu.VMEM((raw.shape[2] // LANES, near * segs, LANES), jnp.float32)]
+        spare = [pltpu.VMEM((raw.shape[2] // LANES, near * segs + segs, LANES), jnp.float32)]
         spare += [pltpu.VMEM(value.shape, value.dtype) for value in extras]
         spare.append(pltpu.SemaphoreType.DMA((len(extras) + 1,)))
     outputs = pl.pallas_call(
@@ -464,7 +468,7 @@
             for part in range(parts):
                 stores.append(
                     pltpu.make_async_copy(
-                        stage.at[part].reshape(near, near, LANES).at[pl.ds(8 * tile, 8)],
+                        stage.at[part].reshape(near + 1, near, LANES).at[pl.ds(8 * tile, 8)],
                         out.at[pl.ds(8 * tile, 8), :, pl.ds(LANES * part, LANES)],
                         out_sems.at[tile, part],
                     )
@@ -481,7 +485,7 @@
         out_shape=jax.ShapeDtypeStruct((near, near, LAGS), jnp.float32),
         scratch_shapes=[pltpu.VMEM((count, len(groups_of(near, kind)), 8, LAGS), jnp.float32) for kind in kinds]
         + [
-            pltpu.VMEM((parts, near * near, LANES), jnp.float32),
+            pltpu.VMEM((parts, near * near + near, LANES), jnp.float32),
             pltpu.SemaphoreType.DMA((tiles, 2, count)),
             pltpu.SemaphoreType.DMA((tiles, parts)),
         ],

time: 77.7 us -> 77.7 us (level)
  no operation moved by 1% of the time
where the time goes in v7:
time: 77.7 us; the launch traced here: 76.6 us
  starting transfers between devices  37.7 us (49%)
  waiting for transfers between devices  19.1 us (25%)
  Pallas kernels  17.6 us (23%)
  other arithmetic  1.97 us (3%)
    ppermute x3, starting transfers between devices, outer(): return lax.ppermute(value, 'tm', [(0, 1), (3, 2)])  27.8 us
    ppermute x2, waiting for transfers between devices, inner(): return lax.ppermute(value, 'tm', [(1, 0), (2, 3)])  11.5 us
    ppermute x3, waiting for transfers between devices, outer(): return lax.ppermute(value, 'tm', [(0, 1), (3, 2)])  7.56 us
    pallas_call x7, Pallas kernels, lag_sums(): pl.pallas_call(kernel, in_specs=[far_memory] * (len(operands) + 1 + len(p...  7.41 us
    pallas_call x1, Pallas kernels, whiten_own(): pl.pallas_call(kernel, in_specs=[far_memory] * 4, out_specs=[far_memory]...  5.47 us
    ppermute x3, starting transfers between devices, middle(): return lax.ppermute(value, 'tm', [(1, 2), (2, 1)])  4.6 us
    pallas_call x1, Pallas kernels, place(): pl.pallas_call(kernel, in_specs=[far_memory] * len(operands), out_specs=f...  2.87 us
    ppermute x2, starting transfers between devices, inner(): return lax.ppermute(value, 'tm', [(1, 0), (2, 3)])  2.57 us
  transfers between devices with their start and end apart: 10, of which 3 were waited for; matrix products, arithmetic and copies ran while one was open for 3% of the time, Pallas kernels for 17%

profile of v7, /device:TPU:0, one launch (start us, length us, event | category | flops | bytes accessed | tf_op | source)
XLA Modules:
  0.0 76.6 jit_solution(16515430229394582193)
XLA Ops:
  0.0 1.8 %take_far.1._ = f32[32,8,512]{2,1,0:T(8,128)} custom-call(f32[4,32,8,512]{3,2,1,0:T(8,128)} %bitcast.1), custom_call_target="tpu_custom_call" | custom-call | flops 10000000000 | bytes 1000 | tf_op jit(solution)/shard_map/take_far/pallas_call | solution.py:161
  1.8 4.0 %collective-permute-start.1 = (f32[32,8,512]{2,1,0:T(8,128)}, f32[32,8,512]{2,1,0:T(8,128)}, u32[]{:S(2)}, u32[]{:S(2)}) collective-permute-start(f32[32,8,512]{2,1,0:T(8,128)} %take_far.1._), channel_id=1, source_target_pairs={{0,1},{3,2},{4,5},{7,6},{8,9},{11,10},{12,13},{15,14},{16,17},{19,... | collective-permute-start | bytes 1572872 | tf_op jit(solution)/shard_map/ppermute | solution.py:510
  5.8 5.5 %whiten_own.1 = (f32[2,2,8,32,128]{4,3,2,1,0:T(8,128)}, f32[2,2,8,32,128]{4,3,2,1,0:T(8,128)}, f32[2,2,8,32,128]{4,3,2,1,0:T(8,128)}, f32[2,2,8,32,128]{4,3,2,1,...) custom-call(f32[4,32,8,512]{3,2,1,0:T(8,128)} %bitcast.2, ...), custom_call_target="tpu_custom_call" | custom-call | flops 10000000000 | bytes 1000 | tf_op jit(solution)/shard_map/whiten_own/pallas_call | solution.py:213
  11.3 1.5 %collective-permute-start.3 = (f32[2,2,8,32,128]{4,3,2,1,0:T(8,128)}, f32[2,2,8,32,128]{4,3,2,1,0:T(8,128)}, u32[]{:S(2)}, u32[]{:S(2)}) collective-permute-start(f32[2,2,8,32,128]{4,3,2,1,0:T(8,128)} %get-tuple-element.22), channel_id=1, source_target_pairs={{4,1},{8,5},{12,9},{16,13},{20,17},{24,21},{28,25},{3,2},{7,6},{11... | collective-permute-start | bytes 1572872 | tf_op jit(solution)/shard_map/ppermute | solution.py:515
  12.8 2.1 %collective-permute-start.5 = (f32[2,2,8,32,128]{4,3,2,1,0:T(8,128)}, f32[2,2,8,32,128]{4,3,2,1,0:T(8,128)}, u32[]{:S(2)}, u32[]{:S(2)}) collective-permute-start(f32[2,2,8,32,128]{4,3,2,1,0:T(8,128)} %get-tuple-element.17.refs_0_.refs_2_), channel_id=1, source_target_pairs={{0,1},{3,2},{4,5},{7,6},{8,9},{11,10},{12,13},{15,14},{16,17},{19,... | collective-permute-start | bytes 1572872 | tf_op jit(solution)/shard_map/ppermute | solution.py:510
  14.9 1.3 %collective-permute-start = (f32[2,2,8,32,128]{4,3,2,1,0:T(8,128)}, f32[2,2,8,32,128]{4,3,2,1,0:T(8,128)}, u32[]{:S(2)}, u32[]{:S(2)}) collective-permute-start(f32[2,2,8,32,128]{4,3,2,1,0:T(8,128)} %get-tuple-element.15.refs_0_.refs_1_), channel_id=1, source_target_pairs={{4,0},{8,4},{12,8},{16,12},{20,16},{24,20},{28,24},{5,1},{9,5},{13... | collective-permute-start | bytes 1572872 | tf_op jit(solution)/shard_map/ppermute | solution.py:500
  16.2 0.1 lag_inside.2.refs_3_
  16.3 1.4 %collective-permute-done.1.refs_4_ = f32[32,8,512]{2,1,0:T(8,128)} collective-permute-done((f32[32,8,512]{2,1,0:T(8,128)}, f32[32,8,512]{2,1,0:T(8,128)}, u32[]{:S(2)}, u32[]{:S(2)}) %collective-permute-start.1) | collective-permute-done | bytes 524320 | tf_op jit(solution)/shard_map/ppermute | solution.py:510
  17.6 0.1 lag_inside.3
  17.8 1.4 %collective-permute-start.2 = (f32[48,8,256]{2,1,0:T(8,128)}, f32[48,8,256]{2,1,0:T(8,128)}, u32[]{:S(2)}, u32[]{:S(2)}) collective-permute-start(f32[48,8,256]{2,1,0:T(8,128)} %get-tuple-element.20.refs_5_), channel_id=1, source_target_pairs={{1,2},{2,1},{5,6},{6,5},{9,10},{10,9},{13,14},{14,13},{17,18},{18,... | collective-permute-start | bytes 1179656 | tf_op jit(solution)/shard_map/ppermute | solution.py:518
  19.2 0.1 lag_across.3.refs_3_
  19.3 0.1 lag_across.4
  19.4 1.5 %collective-permute-start.6 = (f32[80,8,256]{2,1,0:T(8,128)}, f32[80,8,256]{2,1,0:T(8,128)}, u32[]{:S(2)}, u32[]{:S(2)}) collective-permute-start(f32[80,8,256]{2,1,0:T(8,128)} %lag_across.4), channel_id=1, source_target_pairs={{1,2},{2,1},{5,6},{6,5},{9,10},{10,9},{13,14},{14,13},{17,18},{18,... | collective-permute-start | bytes 1966088 | tf_op jit(solution)/shard_map/ppermute | solution.py:518
  21.0 2.0 %add.3.refs_7_ = f32[48,8,256]{2,1,0:T(8,128)} add(f32[48,8,256]{2,1,0:T(8,128)} %collective-permute-done.2, f32[48,8,256]{2,1,0:T(8,128)} %lag_inside.2.refs_3_) | non-fusion elementwise | flops 98304 | bytes 1179648 | tf_op jit(solution)/shard_map/add | solution.py:539
  22.9 1.3 %collective-permute-start.7 = (f32[48,8,256]{2,1,0:T(8,128)}, f32[48,8,256]{2,1,0:T(8,128)}, u32[]{:S(2)}, u32[]{:S(2)}) collective-permute-start(f32[48,8,256]{2,1,0:T(8,128)} %add.3.refs_7_), channel_id=1, source_target_pairs={{1,0},{2,3},{5,4},{6,7},{9,8},{10,11},{13,12},{14,15},{17,16},{18,... | collective-permute-start | bytes 1179656 | tf_op jit(solution)/shard_map/ppermute | solution.py:521
  24.2 21.7 %collective-permute-start.4 = (f32[2,2,8,32,128]{4,3,2,1,0:T(8,128)}, f32[2,2,8,32,128]{4,3,2,1,0:T(8,128)}, u32[]{:S(2)}, u32[]{:S(2)}) collective-permute-start(f32[2,2,8,32,128]{4,3,2,1,0:T(8,128)} %get-tuple-element.24), channel_id=1, source_target_pairs={{0,1},{3,2},{4,5},{7,6},{8,9},{11,10},{12,13},{15,14},{16,17},{19,... | collective-permute-start | bytes 1572872 | tf_op jit(solution)/shard_map/ppermute | solution.py:510
  45.9 0.2 lag_all.2.refs_6_
  46.1 1.6 %collective-permute-start.8 = (f32[128,8,256]{2,1,0:T(8,128)}, f32[128,8,256]{2,1,0:T(8,128)}, u32[]{:S(2)}, u32[]{:S(2)}) collective-permute-start(f32[128,8,256]{2,1,0:T(8,128)} %lag_all.2.refs_6_), channel_id=1, source_target_pairs={{1,2},{2,1},{5,6},{6,5},{9,10},{10,9},{13,14},{14,13},{17,18},{18,... | collective-permute-start | bytes 3145736 | tf_op jit(solution)/shard_map/ppermute | solution.py:518
  47.7 0.1 lag_across.5.refs_8_
  47.8 1.3 %collective-permute-start.9 = (f32[80,8,256]{2,1,0:T(8,128)}, f32[80,8,256]{2,1,0:T(8,128)}, u32[]{:S(2)}, u32[]{:S(2)}) collective-permute-start(f32[80,8,256]{2,1,0:T(8,128)} %lag_across.5.refs_8_), channel_id=1, source_target_pairs={{1,0},{2,3},{5,4},{6,7},{9,8},{10,11},{13,12},{14,15},{17,16},{18,... | collective-permute-start | bytes 1966088 | tf_op jit(solution)/shard_map/ppermute | solution.py:521
  49.1 6.2 %collective-permute-done.4.refs_5_ = f32[2,2,8,32,128]{4,3,2,1,0:T(8,128)} collective-permute-done((f32[2,2,8,32,128]{4,3,2,1,0:T(8,128)}, f32[2,2,8,32,128]{4,3,2,1,0:T(8,128)}, u32[]{:S(2)}, u32[]{:S(2)}) %collective-permute-start.4) | collective-permute-done | bytes 524320 | tf_op jit(solution)/shard_map/ppermute | solution.py:510
  55.3 6.7 %lag_all.3.refs_0_.refs_3_ = f32[128,8,256]{2,1,0:T(8,128)} custom-call(f32[2,2,8,32,128]{4,3,2,1,0:T(8,128)} %get-tuple-element.15.refs_0_.refs_1_, f32[2,2,8,32,128]{4,3,2,1,0:T(8,128)} %get-tuple-element.16.refs_3_.refs_1_.refs_2_, f32[2,2,8,32,128]{4,3,2,1,0:T(8,128)} %get-tuple-element.17.refs_0_.refs_2_, ...), custom_call_target="tpu_custom_call" | custom-call | flops 10000000000 | bytes 1000 | tf_op jit(solution)/shard_map/lag_all/pallas_call | solution.py:393
  62.0 11.5 %collective-permute-done.9.refs_4_ = f32[80,8,256]{2,1,0:T(8,128)} collective-permute-done((f32[80,8,256]{2,1,0:T(8,128)}, f32[80,8,256]{2,1,0:T(8,128)}, u32[]{:S(2)}, u32[]{:S(2)}) %collective-permute-start.9) | collective-permute-done | bytes 655392 | tf_op jit(solution)/shard_map/ppermute | solution.py:521
  73.6 2.9 %place.1 = f32[32,32,256]{2,1,0:T(8,128)} custom-call(f32[128,8,256]{2,1,0:T(8,128)} %lag_all.3.refs_0_.refs_3_, f32[48,8,256]{2,1,0:T(8,128)} %collective-permute-done.7.refs_1_, f32[128,8,256]{2,1,0:T(8,128)} %collective-permute-done.8.refs_2_.refs_5_, f32[128,8,256]{2,1,0:T(8,128)} %lag_all.3.refs_0_.refs_3_, ...), custom_call_target="tpu_custom_call" | custom-call | flops 10000000000 | bytes 1000 | tf_op jit(solution)/shard_map/place/pallas_call | solution.py:481
  (7 shorter events, 0.0 us)
Async XLA Ops:
  1.8 15.8 %collective-permute-start.1 = (f32[32,8,512]{2,1,0:T(8,128)}, f32[32,8,512]{2,1,0:T(8,128)}, u32[]{:S(2)}, u32[]{:S(2)}) collective-permute-start(f32[32,8,512]{2,1,0:T(8,128)} %take_far.1._), channel_id=1, source_target_pairs={{0,1},{3,2},{4,5},{7,6},{8,9},{11,10},{12,13},{15,14},{16,17},{19,... | collective-permute-start | bytes 1572872 | tf_op jit(solution)/shard_map/ppermute | solution.py:510
  11.3 8.0 %collective-permute-start.3 = (f32[2,2,8,32,128]{4,3,2,1,0:T(8,128)}, f32[2,2,8,32,128]{4,3,2,1,0:T(8,128)}, u32[]{:S(2)}, u32[]{:S(2)}) collective-permute-start(f32[2,2,8,32,128]{4,3,2,1,0:T(8,128)} %get-tuple-element.22), channel_id=1, source_target_pairs={{4,1},{8,5},{12,9},{16,13},{20,17},{24,21},{28,25},{3,2},{7,6},{11... | collective-permute-start | bytes 1572872 | tf_op jit(solution)/shard_map/ppermute | solution.py:515
  12.8 33.1 %collective-permute-start.5 = (f32[2,2,8,32,128]{4,3,2,1,0:T(8,128)}, f32[2,2,8,32,128]{4,3,2,1,0:T(8,128)}, u32[]{:S(2)}, u32[]{:S(2)}) collective-permute-start(f32[2,2,8,32,128]{4,3,2,1,0:T(8,128)} %get-tuple-element.17.refs_0_.refs_2_), channel_id=1, source_target_pairs={{0,1},{3,2},{4,5},{7,6},{8,9},{11,10},{12,13},{15,14},{16,17},{19,... | collective-permute-start | bytes 1572872 | tf_op jit(solution)/shard_map/ppermute | solution.py:510
  14.9 4.3 %collective-permute-start = (f32[2,2,8,32,128]{4,3,2,1,0:T(8,128)}, f32[2,2,8,32,128]{4,3,2,1,0:T(8,128)}, u32[]{:S(2)}, u32[]{:S(2)}) collective-permute-start(f32[2,2,8,32,128]{4,3,2,1,0:T(8,128)} %get-tuple-element.15.refs_0_.refs_1_), channel_id=1, source_target_pairs={{4,0},{8,4},{12,8},{16,12},{20,16},{24,20},{28,24},{5,1},{9,5},{13... | collective-permute-start | bytes 1572872 | tf_op jit(solution)/shard_map/ppermute | solution.py:500
  17.8 3.2 %collective-permute-start.2 = (f32[48,8,256]{2,1,0:T(8,128)}, f32[48,8,256]{2,1,0:T(8,128)}, u32[]{:S(2)}, u32[]{:S(2)}) collective-permute-start(f32[48,8,256]{2,1,0:T(8,128)} %get-tuple-element.20.refs_5_), channel_id=1, source_target_pairs={{1,2},{2,1},{5,6},{6,5},{9,10},{10,9},{13,14},{14,13},{17,18},{18,... | collective-permute-start | bytes 1179656 | tf_op jit(solution)/shard_map/ppermute | solution.py:518
  19.4 28.3 %collective-permute-start.6 = (f32[80,8,256]{2,1,0:T(8,128)}, f32[80,8,256]{2,1,0:T(8,128)}, u32[]{:S(2)}, u32[]{:S(2)}) collective-permute-start(f32[80,8,256]{2,1,0:T(8,128)} %lag_across.4), channel_id=1, source_target_pairs={{1,2},{2,1},{5,6},{6,5},{9,10},{10,9},{13,14},{14,13},{17,18},{18,... | collective-permute-start | bytes 1966088 | tf_op jit(solution)/shard_map/ppermute | solution.py:518
  22.9 39.1 %collective-permute-start.7 = (f32[48,8,256]{2,1,0:T(8,128)}, f32[48,8,256]{2,1,0:T(8,128)}, u32[]{:S(2)}, u32[]{:S(2)}) collective-permute-start(f32[48,8,256]{2,1,0:T(8,128)} %add.3.refs_7_), channel_id=1, source_target_pairs={{1,0},{2,3},{5,4},{6,7},{9,8},{10,11},{13,12},{14,15},{17,16},{18,... | collective-permute-start | bytes 1179656 | tf_op jit(solution)/shard_map/ppermute | solution.py:521
  24.2 31.1 %collective-permute-start.4 = (f32[2,2,8,32,128]{4,3,2,1,0:T(8,128)}, f32[2,2,8,32,128]{4,3,2,1,0:T(8,128)}, u32[]{:S(2)}, u32[]{:S(2)}) collective-permute-start(f32[2,2,8,32,128]{4,3,2,1,0:T(8,128)} %get-tuple-element.24), channel_id=1, source_target_pairs={{0,1},{3,2},{4,5},{7,6},{8,9},{11,10},{12,13},{15,14},{16,17},{19,... | collective-permute-start | bytes 1572872 | tf_op jit(solution)/shard_map/ppermute | solution.py:510
  46.1 27.5 %collective-permute-start.8 = (f32[128,8,256]{2,1,0:T(8,128)}, f32[128,8,256]{2,1,0:T(8,128)}, u32[]{:S(2)}, u32[]{:S(2)}) collective-permute-start(f32[128,8,256]{2,1,0:T(8,128)} %lag_all.2.refs_6_), channel_id=1, source_target_pairs={{1,2},{2,1},{5,6},{6,5},{9,10},{10,9},{13,14},{14,13},{17,18},{18,... | collective-permute-start | bytes 3145736 | tf_op jit(solution)/shard_map/ppermute | solution.py:518
  47.8 25.8 %collective-permute-start.9 = (f32[80,8,256]{2,1,0:T(8,128)}, f32[80,8,256]{2,1,0:T(8,128)}, u32[]{:S(2)}, u32[]{:S(2)}) collective-permute-start(f32[80,8,256]{2,1,0:T(8,128)} %lag_across.5.refs_8_), channel_id=1, source_target_pairs={{1,0},{2,3},{5,4},{6,7},{9,8},{10,11},{13,12},{14,15},{17,16},{18,... | collective-permute-start | bytes 1966088 | tf_op jit(solution)/shard_map/ppermute | solution.py:521

commit v8 on v7

--- a/solution.py
+++ b/solution.py
@@ -324,6 +324,9 @@
                 in_sems.at[number, half, side],
             )
 
+        if raw is not None:
+            for raw_copy in raw_copies:
+                raw_copy.start()
         for half in range(halves):
             for number, source in enumerate(layout):
                 for side, places in enumerate(source):
@@ -336,9 +339,6 @@
                         def _():
                             copy(number, side, half, place).start()
 
-        if raw is not None:
-            for raw_copy in raw_copies:
-                raw_copy.start()
         table_copy = pltpu.make_async_copy(table_any, table_ref, table_sem)
         table_copy.start()
         if prior:

time: 77.7 us -> 77.7 us (level)
  no operation moved by 1% of the time
where the time goes in v8:
time: 77.7 us; the launch traced here: 76.6 us
  starting transfers between devices  37.7 us (49%)
  waiting for transfers between devices  19.1 us (25%)
  Pallas kernels  17.6 us (23%)
  other arithmetic  1.97 us (3%)
    ppermute x3, starting transfers between devices, outer(): return lax.ppermute(value, 'tm', [(0, 1), (3, 2)])  27.8 us
    ppermute x2, waiting for transfers between devices, inner(): return lax.ppermute(value, 'tm', [(1, 0), (2, 3)])  11.5 us
    ppermute x3, waiting for transfers between devices, outer(): return lax.ppermute(value, 'tm', [(0, 1), (3, 2)])  7.56 us
    pallas_call x7, Pallas kernels, lag_sums(): pl.pallas_call(kernel, in_specs=[far_memory] * (len(operands) + 1 + len(p...  7.41 us
    pallas_call x1, Pallas kernels, whiten_own(): pl.pallas_call(kernel, in_specs=[far_memory] * 4, out_specs=[far_memory]...  5.47 us
    ppermute x3, starting transfers between devices, middle(): return lax.ppermute(value, 'tm', [(1, 2), (2, 1)])  4.6 us
    pallas_call x1, Pallas kernels, place(): pl.pallas_call(kernel, in_specs=[far_memory] * len(operands), out_specs=f...  2.87 us
    ppermute x2, starting transfers between devices, inner(): return lax.ppermute(value, 'tm', [(1, 0), (2, 3)])  2.57 us
  transfers between devices with their start and end apart: 10, of which 3 were waited for; matrix products, arithmetic and copies ran while one was open for 3% of the time, Pallas kernels for 17%

profile of v8, /device:TPU:0, one launch (start us, length us, event | category | flops | bytes accessed | tf_op | source)
XLA Modules:
  0.0 76.6 jit_solution(12719446126230287730)
XLA Ops:
  0.0 1.8 %take_far.1._ = f32[32,8,512]{2,1,0:T(8,128)} custom-call(f32[4,32,8,512]{3,2,1,0:T(8,128)} %bitcast.1), custom_call_target="tpu_custom_call" | custom-call | flops 10000000000 | bytes 1000 | tf_op jit(solution)/shard_map/take_far/pallas_call | solution.py:161
  1.8 4.0 %collective-permute-start.1 = (f32[32,8,512]{2,1,0:T(8,128)}, f32[32,8,512]{2,1,0:T(8,128)}, u32[]{:S(2)}, u32[]{:S(2)}) collective-permute-start(f32[32,8,512]{2,1,0:T(8,128)} %take_far.1._), channel_id=1, source_target_pairs={{0,1},{3,2},{4,5},{7,6},{8,9},{11,10},{12,13},{15,14},{16,17},{19,... | collective-permute-start | bytes 1572872 | tf_op jit(solution)/shard_map/ppermute | solution.py:510
  5.8 5.5 %whiten_own.1 = (f32[2,2,8,32,128]{4,3,2,1,0:T(8,128)}, f32[2,2,8,32,128]{4,3,2,1,0:T(8,128)}, f32[2,2,8,32,128]{4,3,2,1,0:T(8,128)}, f32[2,2,8,32,128]{4,3,2,1,...) custom-call(f32[4,32,8,512]{3,2,1,0:T(8,128)} %bitcast.2, ...), custom_call_target="tpu_custom_call" | custom-call | flops 10000000000 | bytes 1000 | tf_op jit(solution)/shard_map/whiten_own/pallas_call | solution.py:213
  11.3 1.5 %collective-permute-start.3 = (f32[2,2,8,32,128]{4,3,2,1,0:T(8,128)}, f32[2,2,8,32,128]{4,3,2,1,0:T(8,128)}, u32[]{:S(2)}, u32[]{:S(2)}) collective-permute-start(f32[2,2,8,32,128]{4,3,2,1,0:T(8,128)} %get-tuple-element.22), channel_id=1, source_target_pairs={{4,1},{8,5},{12,9},{16,13},{20,17},{24,21},{28,25},{3,2},{7,6},{11... | collective-permute-start | bytes 1572872 | tf_op jit(solution)/shard_map/ppermute | solution.py:515
  12.8 2.1 %collective-permute-start.5 = (f32[2,2,8,32,128]{4,3,2,1,0:T(8,128)}, f32[2,2,8,32,128]{4,3,2,1,0:T(8,128)}, u32[]{:S(2)}, u32[]{:S(2)}) collective-permute-start(f32[2,2,8,32,128]{4,3,2,1,0:T(8,128)} %get-tuple-element.17.refs_0_.refs_2_), channel_id=1, source_target_pairs={{0,1},{3,2},{4,5},{7,6},{8,9},{11,10},{12,13},{15,14},{16,17},{19,... | collective-permute-start | bytes 1572872 | tf_op jit(solution)/shard_map/ppermute | solution.py:510
  14.9 1.3 %collective-permute-start = (f32[2,2,8,32,128]{4,3,2,1,0:T(8,128)}, f32[2,2,8,32,128]{4,3,2,1,0:T(8,128)}, u32[]{:S(2)}, u32[]{:S(2)}) collective-permute-start(f32[2,2,8,32,128]{4,3,2,1,0:T(8,128)} %get-tuple-element.15.refs_0_.refs_1_), channel_id=1, source_target_pairs={{4,0},{8,4},{12,8},{16,12},{20,16},{24,20},{28,24},{5,1},{9,5},{13... | collective-permute-start | bytes 1572872 | tf_op jit(solution)/shard_map/ppermute | solution.py:500
  16.2 0.1 lag_inside.2.refs_3_
  16.3 1.4 %collective-permute-done.1.refs_4_ = f32[32,8,512]{2,1,0:T(8,128)} collective-permute-done((f32[32,8,512]{2,1,0:T(8,128)}, f32[32,8,512]{2,1,0:T(8,128)}, u32[]{:S(2)}, u32[]{:S(2)}) %collective-permute-start.1) | collective-permute-done | bytes 524320 | tf_op jit(solution)/shard_map/ppermute | solution.py:510
  17.6 0.1 lag_inside.3
  17.8 1.4 %collective-permute-start.2 = (f32[48,8,256]{2,1,0:T(8,128)}, f32[48,8,256]{2,1,0:T(8,128)}, u32[]{:S(2)}, u32[]{:S(2)}) collective-permute-start(f32[48,8,256]{2,1,0:T(8,128)} %get-tuple-element.20.refs_5_), channel_id=1, source_target_pairs={{1,2},{2,1},{5,6},{6,5},{9,10},{10,9},{13,14},{14,13},{17,18},{18,... | collective-permute-start | bytes 1179656 | tf_op jit(solution)/shard_map/ppermute | solution.py:518
  19.2 0.1 lag_across.3.refs_3_
  19.3 0.1 lag_across.4
  19.4 1.5 %collective-permute-start.6 = (f32[80,8,256]{2,1,0:T(8,128)}, f32[80,8,256]{2,1,0:T(8,128)}, u32[]{:S(2)}, u32[]{:S(2)}) collective-permute-start(f32[80,8,256]{2,1,0:T(8,128)} %lag_across.4), channel_id=1, source_target_pairs={{1,2},{2,1},{5,6},{6,5},{9,10},{10,9},{13,14},{14,13},{17,18},{18,... | collective-permute-start | bytes 1966088 | tf_op jit(solution)/shard_map/ppermute | solution.py:518
  21.0 2.0 %add.3.refs_7_ = f32[48,8,256]{2,1,0:T(8,128)} add(f32[48,8,256]{2,1,0:T(8,128)} %collective-permute-done.2, f32[48,8,256]{2,1,0:T(8,128)} %lag_inside.2.refs_3_) | non-fusion elementwise | flops 98304 | bytes 1179648 | tf_op jit(solution)/shard_map/add | solution.py:539
  22.9 1.3 %collective-permute-start.7 = (f32[48,8,256]{2,1,0:T(8,128)}, f32[48,8,256]{2,1,0:T(8,128)}, u32[]{:S(2)}, u32[]{:S(2)}) collective-permute-start(f32[48,8,256]{2,1,0:T(8,128)} %add.3.refs_7_), channel_id=1, source_target_pairs={{1,0},{2,3},{5,4},{6,7},{9,8},{10,11},{13,12},{14,15},{17,16},{18,... | collective-permute-start | bytes 1179656 | tf_op jit(solution)/shard_map/ppermute | solution.py:521
  24.2 21.7 %collective-permute-start.4 = (f32[2,2,8,32,128]{4,3,2,1,0:T(8,128)}, f32[2,2,8,32,128]{4,3,2,1,0:T(8,128)}, u32[]{:S(2)}, u32[]{:S(2)}) collective-permute-start(f32[2,2,8,32,128]{4,3,2,1,0:T(8,128)} %get-tuple-element.24), channel_id=1, source_target_pairs={{0,1},{3,2},{4,5},{7,6},{8,9},{11,10},{12,13},{15,14},{16,17},{19,... | collective-permute-start | bytes 1572872 | tf_op jit(solution)/shard_map/ppermute | solution.py:510
  45.9 0.2 lag_all.2.refs_6_
  46.1 1.6 %collective-permute-start.8 = (f32[128,8,256]{2,1,0:T(8,128)}, f32[128,8,256]{2,1,0:T(8,128)}, u32[]{:S(2)}, u32[]{:S(2)}) collective-permute-start(f32[128,8,256]{2,1,0:T(8,128)} %lag_all.2.refs_6_), channel_id=1, source_target_pairs={{1,2},{2,1},{5,6},{6,5},{9,10},{10,9},{13,14},{14,13},{17,18},{18,... | collective-permute-start | bytes 3145736 | tf_op jit(solution)/shard_map/ppermute | solution.py:518
  47.7 0.1 lag_across.5.refs_8_
  47.8 1.3 %collective-permute-start.9 = (f32[80,8,256]{2,1,0:T(8,128)}, f32[80,8,256]{2,1,0:T(8,128)}, u32[]{:S(2)}, u32[]{:S(2)}) collective-permute-start(f32[80,8,256]{2,1,0:T(8,128)} %lag_across.5.refs_8_), channel_id=1, source_target_pairs={{1,0},{2,3},{5,4},{6,7},{9,8},{10,11},{13,12},{14,15},{17,16},{18,... | collective-permute-start | bytes 1966088 | tf_op jit(solution)/shard_map/ppermute | solution.py:521
  49.1 6.2 %collective-permute-done.4.refs_5_ = f32[2,2,8,32,128]{4,3,2,1,0:T(8,128)} collective-permute-done((f32[2,2,8,32,128]{4,3,2,1,0:T(8,128)}, f32[2,2,8,32,128]{4,3,2,1,0:T(8,128)}, u32[]{:S(2)}, u32[]{:S(2)}) %collective-permute-start.4) | collective-permute-done | bytes 524320 | tf_op jit(solution)/shard_map/ppermute | solution.py:510
  55.3 6.7 %lag_all.3.refs_0_.refs_3_ = f32[128,8,256]{2,1,0:T(8,128)} custom-call(f32[2,2,8,32,128]{4,3,2,1,0:T(8,128)} %get-tuple-element.15.refs_0_.refs_1_, f32[2,2,8,32,128]{4,3,2,1,0:T(8,128)} %get-tuple-element.16.refs_3_.refs_1_.refs_2_, f32[2,2,8,32,128]{4,3,2,1,0:T(8,128)} %get-tuple-element.17.refs_0_.refs_2_, ...), custom_call_target="tpu_custom_call" | custom-call | flops 10000000000 | bytes 1000 | tf_op jit(solution)/shard_map/lag_all/pallas_call | solution.py:393
  62.0 11.5 %collective-permute-done.9.refs_4_ = f32[80,8,256]{2,1,0:T(8,128)} collective-permute-done((f32[80,8,256]{2,1,0:T(8,128)}, f32[80,8,256]{2,1,0:T(8,128)}, u32[]{:S(2)}, u32[]{:S(2)}) %collective-permute-start.9) | collective-permute-done | bytes 655392 | tf_op jit(solution)/shard_map/ppermute | solution.py:521
  73.6 2.9 %place.1 = f32[32,32,256]{2,1,0:T(8,128)} custom-call(f32[128,8,256]{2,1,0:T(8,128)} %lag_all.3.refs_0_.refs_3_, f32[48,8,256]{2,1,0:T(8,128)} %collective-permute-done.7.refs_1_, f32[128,8,256]{2,1,0:T(8,128)} %collective-permute-done.8.refs_2_.refs_5_, f32[128,8,256]{2,1,0:T(8,128)} %lag_all.3.refs_0_.refs_3_, ...), custom_call_target="tpu_custom_call" | custom-call | flops 10000000000 | bytes 1000 | tf_op jit(solution)/shard_map/place/pallas_call | solution.py:481
  (7 shorter events, 0.0 us)
Async XLA Ops:
  1.8 15.8 %collective-permute-start.1 = (f32[32,8,512]{2,1,0:T(8,128)}, f32[32,8,512]{2,1,0:T(8,128)}, u32[]{:S(2)}, u32[]{:S(2)}) collective-permute-start(f32[32,8,512]{2,1,0:T(8,128)} %take_far.1._), channel_id=1, source_target_pairs={{0,1},{3,2},{4,5},{7,6},{8,9},{11,10},{12,13},{15,14},{16,17},{19,... | collective-permute-start | bytes 1572872 | tf_op jit(solution)/shard_map/ppermute | solution.py:510
  11.3 8.0 %collective-permute-start.3 = (f32[2,2,8,32,128]{4,3,2,1,0:T(8,128)}, f32[2,2,8,32,128]{4,3,2,1,0:T(8,128)}, u32[]{:S(2)}, u32[]{:S(2)}) collective-permute-start(f32[2,2,8,32,128]{4,3,2,1,0:T(8,128)} %get-tuple-element.22), channel_id=1, source_target_pairs={{4,1},{8,5},{12,9},{16,13},{20,17},{24,21},{28,25},{3,2},{7,6},{11... | collective-permute-start | bytes 1572872 | tf_op jit(solution)/shard_map/ppermute | solution.py:515
  12.8 33.1 %collective-permute-start.5 = (f32[2,2,8,32,128]{4,3,2,1,0:T(8,128)}, f32[2,2,8,32,128]{4,3,2,1,0:T(8,128)}, u32[]{:S(2)}, u32[]{:S(2)}) collective-permute-start(f32[2,2,8,32,128]{4,3,2,1,0:T(8,128)} %get-tuple-element.17.refs_0_.refs_2_), channel_id=1, source_target_pairs={{0,1},{3,2},{4,5},{7,6},{8,9},{11,10},{12,13},{15,14},{16,17},{19,... | collective-permute-start | bytes 1572872 | tf_op jit(solution)/shard_map/ppermute | solution.py:510
  14.9 4.3 %collective-permute-start = (f32[2,2,8,32,128]{4,3,2,1,0:T(8,128)}, f32[2,2,8,32,128]{4,3,2,1,0:T(8,128)}, u32[]{:S(2)}, u32[]{:S(2)}) collective-permute-start(f32[2,2,8,32,128]{4,3,2,1,0:T(8,128)} %get-tuple-element.15.refs_0_.refs_1_), channel_id=1, source_target_pairs={{4,0},{8,4},{12,8},{16,12},{20,16},{24,20},{28,24},{5,1},{9,5},{13... | collective-permute-start | bytes 1572872 | tf_op jit(solution)/shard_map/ppermute | solution.py:500
  17.8 3.2 %collective-permute-start.2 = (f32[48,8,256]{2,1,0:T(8,128)}, f32[48,8,256]{2,1,0:T(8,128)}, u32[]{:S(2)}, u32[]{:S(2)}) collective-permute-start(f32[48,8,256]{2,1,0:T(8,128)} %get-tuple-element.20.refs_5_), channel_id=1, source_target_pairs={{1,2},{2,1},{5,6},{6,5},{9,10},{10,9},{13,14},{14,13},{17,18},{18,... | collective-permute-start | bytes 1179656 | tf_op jit(solution)/shard_map/ppermute | solution.py:518
  19.4 28.3 %collective-permute-start.6 = (f32[80,8,256]{2,1,0:T(8,128)}, f32[80,8,256]{2,1,0:T(8,128)}, u32[]{:S(2)}, u32[]{:S(2)}) collective-permute-start(f32[80,8,256]{2,1,0:T(8,128)} %lag_across.4), channel_id=1, source_target_pairs={{1,2},{2,1},{5,6},{6,5},{9,10},{10,9},{13,14},{14,13},{17,18},{18,... | collective-permute-start | bytes 1966088 | tf_op jit(solution)/shard_map/ppermute | solution.py:518
  22.9 39.1 %collective-permute-start.7 = (f32[48,8,256]{2,1,0:T(8,128)}, f32[48,8,256]{2,1,0:T(8,128)}, u32[]{:S(2)}, u32[]{:S(2)}) collective-permute-start(f32[48,8,256]{2,1,0:T(8,128)} %add.3.refs_7_), channel_id=1, source_target_pairs={{1,0},{2,3},{5,4},{6,7},{9,8},{10,11},{13,12},{14,15},{17,16},{18,... | collective-permute-start | bytes 1179656 | tf_op jit(solution)/shard_map/ppermute | solution.py:521
  24.2 31.1 %collective-permute-start.4 = (f32[2,2,8,32,128]{4,3,2,1,0:T(8,128)}, f32[2,2,8,32,128]{4,3,2,1,0:T(8,128)}, u32[]{:S(2)}, u32[]{:S(2)}) collective-permute-start(f32[2,2,8,32,128]{4,3,2,1,0:T(8,128)} %get-tuple-element.24), channel_id=1, source_target_pairs={{0,1},{3,2},{4,5},{7,6},{8,9},{11,10},{12,13},{15,14},{16,17},{19,... | collective-permute-start | bytes 1572872 | tf_op jit(solution)/shard_map/ppermute | solution.py:510
  46.1 27.5 %collective-permute-start.8 = (f32[128,8,256]{2,1,0:T(8,128)}, f32[128,8,256]{2,1,0:T(8,128)}, u32[]{:S(2)}, u32[]{:S(2)}) collective-permute-start(f32[128,8,256]{2,1,0:T(8,128)} %lag_all.2.refs_6_), channel_id=1, source_target_pairs={{1,2},{2,1},{5,6},{6,5},{9,10},{10,9},{13,14},{14,13},{17,18},{18,... | collective-permute-start | bytes 3145736 | tf_op jit(solution)/shard_map/ppermute | solution.py:518
  47.8 25.7 %collective-permute-start.9 = (f32[80,8,256]{2,1,0:T(8,128)}, f32[80,8,256]{2,1,0:T(8,128)}, u32[]{:S(2)}, u32[]{:S(2)}) collective-permute-start(f32[80,8,256]{2,1,0:T(8,128)} %lag_across.5.refs_8_), channel_id=1, source_target_pairs={{1,0},{2,3},{5,4},{6,7},{9,8},{10,11},{13,12},{14,15},{17,16},{18,... | collective-permute-start | bytes 1966088 | tf_op jit(solution)/shard_map/ppermute | solution.py:521
